TPU v7x, 1024 devices: a whole 4x8x16 slice. The times are simulated.
1024 devices in a mesh: dp: 16 (over y, core), expert: 64 (over x, z).
Axes of the slice: x: 4, y: 8, z: 16, core: 2. Of those that a mesh axis runs over, the one named last changes fastest.
Arguments:
- out_grad: bfloat16 [16384, 4096], P(('dp', 'expert')), may hold values from -6 to 6
- hidden_acts: bfloat16 [16384, 8, 768], P(('dp', 'expert')), may hold values from -0.23925781 to 0.23925781
- gate_weights: float32 [16384, 8], P(('dp', 'expert')), may hold values from 0 to 1, as said below
- expert_idx: int32 [16384, 8], P(('dp', 'expert')), may hold values from 0 to 63, all different within a row; in each aligned block of 16 rows (0 to 15, 16 to 31, ...) at most 3 rows name the same one
- down_weight: bfloat16 [64, 768, 4096], P('expert'), may hold values from -0.09375 to 0.09375
Outputs:
- act_grad: bfloat16 [16384, 8, 768], P(('dp', 'expert'))
- logit_grad: float32 [16384, 8], P(('dp', 'expert'))
- down_grad: bfloat16 [64, 768, 4096], P('expert', 'dp')
Inputs may be any that keep to these rules, and one draw needn't show every extreme that they name: `expert_idx`: each row names 8 different experts; among the 16 rows of one device no expert is named more than 3 times, a bound that some block reaches. `gate_weights`: each row is positive and sums to one.
All inputs are finite; a program needn't handle non-finite values.
Results may differ from a plain program's by a relative error of at most 0.022.
Values may be sent and summed in bfloat16 or wider, within the bound.
No kernel may reach another device: no remote copies, remote signals or barrier semaphores. Data moves between devices by JAX's collectives and lax.ppermute only.
A program may use at most 64 MiB of HBM per device.

v0:
```python
import jax
import jax.numpy as jnp
from jax import lax
from jax.sharding import PartitionSpec as P


def shards(out_grad, hidden_acts, gate_weights, expert_idx, down_weight):
    tok_rows, top_count = expert_idx.shape
    routed = tok_rows * top_count
    hidden_width = hidden_acts.shape[2]
    owners = lax.axis_size("expert")
    experts = owners * down_weight.shape[0]
    capacity = min(tok_rows, max(2, (3 * tok_rows * top_count + 2 * experts - 1) // (2 * experts)))
    slot_count = experts * capacity
    flat_expert = expert_idx.reshape(routed)
    member = (flat_expert[:, None] == jnp.arange(experts, dtype=jnp.int32)[None, :]).astype(
        jnp.bfloat16
    )
    row_line = jnp.arange(routed, dtype=jnp.int32)
    earlier_mask = (row_line[:, None] > row_line[None, :]).astype(jnp.bfloat16)
    earlier = jnp.dot(earlier_mask, member, preferred_element_type=jnp.float32)
    position = jnp.sum(earlier * member.astype(jnp.float32), axis=1).astype(jnp.int32)
    slot_index = flat_expert * capacity + position
    placement = (jnp.arange(slot_count, dtype=jnp.int32)[:, None] == slot_index[None, :]).astype(
        jnp.bfloat16
    )
    token_place = jnp.sum(placement.reshape(slot_count, tok_rows, top_count), axis=2)
    gate_half = lax.optimization_barrier(gate_weights.astype(jnp.bfloat16))
    send_grads = jnp.dot(token_place, out_grad, preferred_element_type=jnp.float32).astype(
        jnp.bfloat16
    )
    send_acts = jnp.dot(
        placement, hidden_acts.reshape(routed, hidden_width), preferred_element_type=jnp.float32
    ).astype(jnp.bfloat16)
    send_gate = jnp.dot(
        placement, gate_half.reshape(routed, 1), preferred_element_type=jnp.float32
    ).astype(jnp.bfloat16)
    grads_in, acts_in, gate_in = (
        lax.all_to_all(
            send_grads.reshape(owners, capacity, out_grad.shape[1]),
            "expert",
            split_axis=0,
            concat_axis=0,
            tiled=True,
        ),
        lax.all_to_all(
            send_acts.reshape(owners, capacity, hidden_width),
            "expert",
            split_axis=0,
            concat_axis=0,
            tiled=True,
        ),
        lax.all_to_all(
            send_gate.reshape(owners, capacity), "expert", split_axis=0, concat_axis=0, tiled=True
        ),
    )
    grads_in = grads_in.reshape(slot_count, out_grad.shape[1])
    acts_in = acts_in.reshape(slot_count, hidden_width)
    gate_rows = gate_in.reshape(slot_count, 1).astype(jnp.float32)
    expert_weight = down_weight[0]
    grad_hidden = lax.dot_general(
        grads_in, expert_weight, (((1,), (1,)), ((), ())), preferred_element_type=jnp.float32
    )
    act_back = (gate_rows * grad_hidden).astype(jnp.bfloat16)
    score_back = jnp.sum(grad_hidden * acts_in.astype(jnp.float32), axis=1).astype(jnp.bfloat16)
    scaled_grad = (gate_rows * grads_in.astype(jnp.float32)).astype(jnp.bfloat16)
    back_rows, back_scores = (
        lax.all_to_all(
            act_back.reshape(owners, capacity, hidden_width),
            "expert",
            split_axis=0,
            concat_axis=0,
            tiled=True,
        ),
        lax.all_to_all(
            score_back.reshape(owners, capacity), "expert", split_axis=0, concat_axis=0, tiled=True
        ),
    )
    weight_term = lax.dot_general(
        acts_in, scaled_grad, (((0,), (0,)), ((), ())), preferred_element_type=jnp.float32
    )
    summed = lax.psum_scatter(
        weight_term.astype(jnp.bfloat16), "dp", scatter_dimension=0, tiled=True
    )
    down_grad = summed[None]
    act_grad = lax.dot_general(
        placement,
        back_rows.reshape(slot_count, hidden_width),
        (((0,), (0,)), ((), ())),
        preferred_element_type=jnp.float32,
    ).astype(jnp.bfloat16)
    score_tok = lax.dot_general(
        placement,
        back_scores.reshape(slot_count, 1),
        (((0,), (0,)), ((), ())),
        preferred_element_type=jnp.float32,
    ).reshape(tok_rows, top_count)
    logit_grad = gate_weights * (
        score_tok - jnp.sum(gate_weights * score_tok, axis=1, keepdims=True)
    )
    return (act_grad.reshape(tok_rows, top_count, hidden_width), logit_grad, down_grad)


def solution(mesh):
    return jax.shard_map(
        shards,
        mesh=mesh,
        in_specs=(
            P(("dp", "expert"), None),
            P(("dp", "expert"), None, None),
            P(("dp", "expert"), None),
            P(("dp", "expert"), None),
            P("expert", None, None),
        ),
        out_specs=(
            P(("dp", "expert"), None, None),
            P(("dp", "expert"), None),
            P("expert", "dp", None),
        ),
        check_vma=False,
    )
```

profile of v0, /device:TPU:6, one launch (start us, length us, event | category | flops | bytes accessed | tf_op | source)
XLA Modules:
  0.0 260.6 jit_solution(2154957029147665159)
XLA Ops:
  7.2 0.0 copy-start
  7.2 0.0 copy-start.1
  7.2 0.7 convert_element_type.94
  7.9 0.1 copy.44
  8.0 0.1 reshape.149
  8.1 0.8 copy.43
  8.9 0.1 reshape.136
  9.0 0.2 fusion.5
  9.2 0.1 fusion.12
  9.3 0.8 all_to_all.25
  10.1 22.5 %all-to-all-start = ((bf16[64,1,3]{2,1,0:T(2,128)(2,1)}), bf16[64,1,3]{2,1,0:T(2,128)(2,1)S(1)}, u32[]{:S(2)}, u32[]{:S(2)}) async-start(bf16[64,1,3]{2,1,0:T(2,128)(2,1)} %all_to_all.25), calls=%async_computation | async-start | bytes 65536 | tf_op jit(solution)/shard_map/all_to_all | solution.py:53
  32.6 0.0 copy-done
  32.6 0.2 convolution_convert_fusion.1
  32.8 0.9 reshape.144
  33.7 11.3 %all-to-all-done = bf16[64,1,3]{2,1,0:T(2,128)(2,1)S(1)} async-done(((bf16[64,1,3]{2,1,0:T(2,128)(2,1)}), bf16[64,1,3]{2,1,0:T(2,128)(2,1)S(1)}, u32[]{:S(2)}, u32[]{:S(2)}) %all-to-all-start) | async-done | bytes 416 | tf_op jit(solution)/shard_map/all_to_all | solution.py:53
  45.1 6.5 %all-to-all-start.3 = ((bf16[64,3,768]{2,1,0:T(4,128)(2,1)}), bf16[64,3,768]{2,1,0:T(4,128)(2,1)S(1)}, u32[]{:S(2)}, u32[]{:S(2)}) async-start(bf16[64,3,768]{2,1,0:T(4,128)(2,1)} %reshape.144), calls=%async_computation.3 | async-start | bytes 786432 | tf_op jit(solution)/shard_map/all_to_all | solution.py:46
  51.6 0.1 convert_element_type.98
  51.7 0.1 fusion.13
  51.8 0.0 copy-done.1
  51.8 0.6 convolution_convert_fusion
  52.4 2.4 reshape.138
  54.8 22.0 %all-to-all-done.3 = bf16[64,3,768]{2,1,0:T(4,128)(2,1)S(1)} async-done(((bf16[64,3,768]{2,1,0:T(4,128)(2,1)}), bf16[64,3,768]{2,1,0:T(4,128)(2,1)S(1)}, u32[]{:S(2)}, u32[]{:S(2)}) %all-to-all-start.3) | async-done | bytes 294944 | tf_op jit(solution)/shard_map/all_to_all | solution.py:46
  76.7 6.7 %all-to-all-start.1 = ((bf16[64,3,4096]{2,1,0:T(4,128)(2,1)}), bf16[64,3,4096]{2,1,0:T(4,128)(2,1)S(1)}, u32[]{:S(2)}, u32[]{:S(2)}) async-start(bf16[64,3,4096]{2,1,0:T(4,128)(2,1)} %reshape.138), calls=%async_computation.1 | async-start | bytes 4194304 | tf_op jit(solution)/shard_map/all_to_all | solution.py:39
  83.4 0.0 reduce-scatter.2.cloned.1.call-start
  83.5 0.1 copy.48
  83.6 96.7 %all-to-all-done.1 = bf16[64,3,4096]{2,1,0:T(4,128)(2,1)S(1)} async-done(((bf16[64,3,4096]{2,1,0:T(4,128)(2,1)}), bf16[64,3,4096]{2,1,0:T(4,128)(2,1)S(1)}, u32[]{:S(2)}, u32[]{:S(2)}) %all-to-all-start.1) | async-done | bytes 1572896 | tf_op jit(solution)/shard_map/all_to_all | solution.py:39
  180.3 5.5 %bitcast_convert_fusion = bf16[768,4096]{1,0:T(8,128)(2,1)} fusion(bf16[64,3,4096]{2,1,0:T(4,128)(2,1)S(1)} %all-to-all-done.1, f32[64,3]{0,1:T(4,128)S(1)} %copy.48, bf16[64,3,768]{2,1,0:T(4,128)(2,1)S(1)} %all-to-all-done.3), kind=kOutput, calls=%fused_computation | convolution fusion | flops 1213464576 | bytes 8160000 | tf_op jit(solution)/shard_map/dot_general | solution.py:79
  185.8 0.0 reduce-scatter.2.cloned.1.call-update
  185.8 0.1 convert_reduce_fusion
  185.9 0.1 reshape.146
  186.0 0.2 reshape.147
  186.3 2.5 reshape.139
  188.8 5.6 %multiply_reduce_fusion = (bf16[192]{0:T(256)(128)(2,1)S(1)}, bf16[192,768]{1,0:T(8,128)(2,1)S(1)}) fusion(f32[192,768]{1,0:T(8,128)S(1)} %reshape.147, f32[192]{0:T(256)S(1)} %reshape.146, bf16[192,4096]{1,0:T(8,128)(2,1)} %reshape.139, bf16[1,768,4096]{2,1,0:T(8,128)(2,1)} %param.9), kind=kOutput, calls=%fused_computation.12 | convolution fusion | flops 1208549120 | bytes 8750208 | tf_op jit(solution)/shard_map/dot_general | solution.py:61
  194.4 0.8 convert_element_type.116
  195.2 7.3 %all-to-all-start.4 = ((bf16[64,1,3]{2,1,0:T(2,128)(2,1)}), bf16[64,1,3]{2,1,0:T(2,128)(2,1)S(1)}, u32[]{:S(2)}, u32[]{:S(2)}) async-start(bf16[64,1,3]{2,1,0:T(2,128)(2,1)} %convert_element_type.116), calls=%async_computation.4 | async-start | bytes 65536 | tf_op jit(solution)/shard_map/all_to_all | solution.py:75
  202.5 0.9 reshape.140
  203.5 11.6 %all-to-all-done.4 = bf16[64,1,3]{2,1,0:T(2,128)(2,1)S(1)} async-done(((bf16[64,1,3]{2,1,0:T(2,128)(2,1)}), bf16[64,1,3]{2,1,0:T(2,128)(2,1)S(1)}, u32[]{:S(2)}, u32[]{:S(2)}) %all-to-all-start.4) | async-done | bytes 416 | tf_op jit(solution)/shard_map/all_to_all | solution.py:75
  215.0 6.5 %all-to-all-start.2 = ((bf16[64,3,768]{2,1,0:T(4,128)(2,1)}), bf16[64,3,768]{2,1,0:T(4,128)(2,1)S(1)}, u32[]{:S(2)}, u32[]{:S(2)}) async-start(bf16[64,3,768]{2,1,0:T(4,128)(2,1)} %reshape.140), calls=%async_computation.2 | async-start | bytes 786432 | tf_op jit(solution)/shard_map/all_to_all | solution.py:68
  221.5 0.1 reduce.2
  221.6 0.1 reshape.151
  221.8 0.3 fusion.10
  222.1 0.1 copy.51
  222.2 0.0 copy-done.2
  222.2 0.6 fusion.21
  222.8 23.7 %all-to-all-done.2 = bf16[64,3,768]{2,1,0:T(4,128)(2,1)S(1)} async-done(((bf16[64,3,768]{2,1,0:T(4,128)(2,1)}), bf16[64,3,768]{2,1,0:T(4,128)(2,1)S(1)}, u32[]{:S(2)}, u32[]{:S(2)}) %all-to-all-start.2) | async-done | bytes 294944 | tf_op jit(solution)/shard_map/all_to_all | solution.py:68
  246.5 0.2 reshape.141
  246.8 0.9 fusion.4
  247.7 6.0 %reduce-scatter.2.cloned.1.call-done = bf16[48,4096]{1,0:T(8,128)(2,1)} async-done(((bf16[768,4096]{1,0:T(8,128)(2,1)}), bf16[48,4096]{1,0:T(8,128)(2,1)}) %reduce-scatter.2.cloned.1.call-update) | async-done | bytes 393232 | tf_op jit(solution)/shard_map/reduce_scatter | solution.py:82
  (7 shorter events, 0.1 us)
Async XLA Ops:
  7.2 25.4 %copy-start = (bf16[16,8,768]{2,1,0:T(8,128)(2,1)S(1)}, bf16[16,8,768]{2,1,0:T(8,128)(2,1)}, u32[]{:S(2)}) copy-start(bf16[16,8,768]{2,1,0:T(8,128)(2,1)} %param.6) | copy-start | bytes 589828
  7.2 44.6 %copy-start.1 = (bf16[16,4096]{1,0:T(8,128)(2,1)S(1)}, bf16[16,4096]{1,0:T(8,128)(2,1)}, u32[]{:S(2)}) copy-start(bf16[16,4096]{1,0:T(8,128)(2,1)} %param.5) | copy-start | bytes 393220
  10.1 34.9 %all-to-all-start = ((bf16[64,1,3]{2,1,0:T(2,128)(2,1)}), bf16[64,1,3]{2,1,0:T(2,128)(2,1)S(1)}, u32[]{:S(2)}, u32[]{:S(2)}) async-start(bf16[64,1,3]{2,1,0:T(2,128)(2,1)} %all_to_all.25), calls=%async_computation | async-start | bytes 65536 | tf_op jit(solution)/shard_map/all_to_all | solution.py:53
  45.1 31.7 %all-to-all-start.3 = ((bf16[64,3,768]{2,1,0:T(4,128)(2,1)}), bf16[64,3,768]{2,1,0:T(4,128)(2,1)S(1)}, u32[]{:S(2)}, u32[]{:S(2)}) async-start(bf16[64,3,768]{2,1,0:T(4,128)(2,1)} %reshape.144), calls=%async_computation.3 | async-start | bytes 786432 | tf_op jit(solution)/shard_map/all_to_all | solution.py:46
  76.7 103.6 %all-to-all-start.1 = ((bf16[64,3,4096]{2,1,0:T(4,128)(2,1)}), bf16[64,3,4096]{2,1,0:T(4,128)(2,1)S(1)}, u32[]{:S(2)}, u32[]{:S(2)}) async-start(bf16[64,3,4096]{2,1,0:T(4,128)(2,1)} %reshape.138), calls=%async_computation.1 | async-start | bytes 4194304 | tf_op jit(solution)/shard_map/all_to_all | solution.py:39
  83.4 170.3 %reduce-scatter.2.cloned.1.call-start = ((), (), s32[]{:S(2)}) async-start(), calls=%async_computation.6 | async-start | bytes 6684672 | tf_op jit(solution)/shard_map/reduce_scatter | solution.py:82
  188.8 33.4 %copy-start.2 = (f32[16,8]{0,1:T(8,128)S(1)}, f32[16,8]{0,1:T(8,128)}, u32[]{:S(2)}) copy-start(f32[16,8]{0,1:T(8,128)} %param.7) | copy-start | bytes 1540
  195.2 19.8 %all-to-all-start.4 = ((bf16[64,1,3]{2,1,0:T(2,128)(2,1)}), bf16[64,1,3]{2,1,0:T(2,128)(2,1)S(1)}, u32[]{:S(2)}, u32[]{:S(2)}) async-start(bf16[64,1,3]{2,1,0:T(2,128)(2,1)} %convert_element_type.116), calls=%async_computation.4 | async-start | bytes 65536 | tf_op jit(solution)/shard_map/all_to_all | solution.py:75
  215.0 31.5 %all-to-all-start.2 = ((bf16[64,3,768]{2,1,0:T(4,128)(2,1)}), bf16[64,3,768]{2,1,0:T(4,128)(2,1)S(1)}, u32[]{:S(2)}, u32[]{:S(2)}) async-start(bf16[64,3,768]{2,1,0:T(4,128)(2,1)} %reshape.140), calls=%async_computation.2 | async-start | bytes 786432 | tf_op jit(solution)/shard_map/all_to_all | solution.py:68
Sparse Core Ops, SparseCore 0:
  185.9 67.7 reduce-scatter.1
where the time goes:
time: 261 us
  waiting for transfers between devices  171 us (66%)
  starting transfers between devices  49.6 us (19%)
  between operations  14.2 us (5%)
  matrix products  13.5 us (5%)
  local copies, waits for them, and re-layouts  10.3 us (4%)
    all_to_all x1, waiting for transfers between devices, shards(): lax.all_to_all(send_grads.reshape(owners, capacity, out_grad.shape[1]), '...  96.7 us
    all_to_all x1, waiting for transfers between devices, shards(): lax.all_to_all(act_back.reshape(owners, capacity, hidden_width), 'expert'...  23.7 us
    all_to_all x1, starting transfers between devices, shards(): lax.all_to_all(send_gate.reshape(owners, capacity), 'expert', split_axis=...  22.5 us
    all_to_all x1, waiting for transfers between devices, shards(): lax.all_to_all(send_acts.reshape(owners, capacity, hidden_width), 'expert...  22 us
    all_to_all x1, waiting for transfers between devices, shards(): lax.all_to_all(score_back.reshape(owners, capacity), 'expert', split_axis...  11.6 us
    all_to_all x1, waiting for transfers between devices, shards(): lax.all_to_all(send_gate.reshape(owners, capacity), 'expert', split_axis=...  11.3 us
    all_to_all x1, starting transfers between devices, shards(): lax.all_to_all(score_back.reshape(owners, capacity), 'expert', split_axis...  7.35 us
    all_to_all x1, starting transfers between devices, shards(): lax.all_to_all(send_grads.reshape(owners, capacity, out_grad.shape[1]), '...  6.71 us
  transfers between devices with their start and end apart: 6, of which 6 were waited for; matrix products, arithmetic and copies ran while one was open for 7% of the time, Pallas kernels for 0%

commit v1 on v0

v1 whole, which is shorter than its diff:
```python
import jax
import jax.numpy as jnp
from jax import lax
from jax.experimental import pallas as pl
from jax.experimental.pallas import tpu as pltpu
from jax.sharding import Mesh
from jax.sharding import PartitionSpec as P

MOST = 3
CORES = 2
X, Y, Z = 4, 8, 16
BF16 = jnp.bfloat16
F32 = jnp.float32


def weight_kernel(left_own, left_pair, rows_own, rows_pair, out):
    total = jnp.dot(left_own[...], rows_own[...], preferred_element_type=F32)
    total = total + jnp.dot(left_pair[...], rows_pair[...], preferred_element_type=F32)
    out[...] = total.astype(out.dtype)


def weight_term(left_own, left_pair, rows_own, rows_pair):
    half, slots = left_own.shape
    width = rows_own.shape[1]
    block = 1024
    return pl.pallas_call(
        weight_kernel,
        grid=(width // block,),
        out_shape=jax.ShapeDtypeStruct((half, width), BF16),
        in_specs=[
            pl.BlockSpec((half, slots), lambda i: (0, 0)),
            pl.BlockSpec((half, slots), lambda i: (0, 0)),
            pl.BlockSpec((slots, block), lambda i: (0, i)),
            pl.BlockSpec((slots, block), lambda i: (0, i)),
        ],
        out_specs=pl.BlockSpec((half, block), lambda i: (0, i)),
        compiler_params=pltpu.CompilerParams(vmem_limit_bytes=32 * 1024 * 1024),
        cost_estimate=pl.CostEstimate(
            flops=4 * half * slots * width,
            bytes_accessed=2 * (2 * slots * width + half * width + 2 * half * slots),
            transcendentals=0,
        ),
        name="weight_term",
    )(left_own, left_pair, rows_own, rows_pair)


def shards(out_grad, hidden_acts, gate_weights, expert_idx, down_weight):
    tok_rows, top_count = expert_idx.shape
    routed = tok_rows * top_count
    hidden = hidden_acts.shape[2]
    half = hidden // CORES
    experts = X * Z
    slot_count = experts * MOST
    core = lax.axis_index("core")
    z_at = lax.axis_index("z")

    column = lax.all_gather(out_grad, "z", axis=0, tiled=True)

    flat_expert = expert_idx.reshape(routed)
    member = (flat_expert[:, None] == jnp.arange(experts, dtype=jnp.int32)[None, :]).astype(BF16)
    row_line = jnp.arange(routed, dtype=jnp.int32)
    earlier_mask = (row_line[:, None] > row_line[None, :]).astype(BF16)
    earlier = jnp.dot(earlier_mask, member, preferred_element_type=F32)
    position = jnp.sum(earlier * member.astype(F32), axis=1).astype(jnp.int32)
    slot_index = flat_expert * MOST + position
    taken = jnp.arange(slot_count, dtype=jnp.int32)[:, None] == slot_index[None, :]
    placement = taken.astype(BF16)

    token_of = (z_at * tok_rows + row_line // top_count).astype(F32)
    slot_token = jnp.sum(jnp.where(taken, token_of[None, :] + 1.0, 0.0), axis=1) - 1.0
    slot_token = lax.all_to_all(
        slot_token.reshape(X, Z, MOST), "z", split_axis=1, concat_axis=1, tiled=True
    )

    gate_half = lax.optimization_barrier(gate_weights.astype(BF16)).astype(F32)
    flat_acts = hidden_acts.reshape(routed, hidden).astype(F32)
    gated = (gate_half.reshape(routed, 1) * flat_acts).astype(BF16)
    send_acts = jnp.dot(placement, gated, preferred_element_type=F32).astype(BF16)
    acts_in = lax.all_to_all(
        send_acts.reshape(experts, MOST, hidden),
        ("x", "z"),
        split_axis=0,
        concat_axis=0,
        tiled=True,
    ).reshape(slot_count, hidden)

    line = jnp.arange(hidden, dtype=jnp.int32)
    piece = hidden // (Y * CORES)
    unit = ((line % half) // piece * CORES + line // half) * piece + line % piece
    reorder = (unit[:, None] == line[None, :]).astype(BF16)
    left = lax.dot_general(
        reorder, acts_in, (((1,), (1,)), ((), ())), preferred_element_type=F32
    ).astype(BF16)
    left_own = lax.dynamic_slice_in_dim(left, core * half, half, 0)
    left_away = lax.dynamic_slice_in_dim(left, (1 - core) * half, half, 0)
    swap = [(0, 1), (1, 0)]
    left_pair = lax.ppermute(left_away, "core", swap)

    pick = (
        slot_token.reshape(slot_count, 1)
        == jnp.arange(Z * tok_rows, dtype=jnp.int32)[None, :].astype(F32)
    ).astype(BF16)
    picked = jnp.dot(pick, column, preferred_element_type=F32).astype(BF16)
    rows = lax.all_to_all(
        picked.reshape(X, Z * MOST, picked.shape[1]),
        "x",
        split_axis=0,
        concat_axis=0,
        tiled=True,
    ).reshape(slot_count, picked.shape[1])
    rows_pair = lax.ppermute(rows, "core", swap)

    weight_part = weight_term(left_own, left_pair, rows, rows_pair)
    summed = lax.psum_scatter(weight_part, "y", scatter_dimension=0, tiled=True)

    grad_hidden = lax.dot_general(
        rows, down_weight[0], (((1,), (1,)), ((), ())), preferred_element_type=F32
    ).astype(BF16)
    back = lax.all_to_all(
        grad_hidden.reshape(experts, MOST, hidden),
        ("x", "z"),
        split_axis=0,
        concat_axis=0,
        tiled=True,
    ).reshape(slot_count, hidden)
    grad_tok = lax.dot_general(
        placement, back, (((0,), (0,)), ((), ())), preferred_element_type=F32
    )
    act_grad = (gate_half.reshape(routed, 1) * grad_tok).astype(BF16)
    score = jnp.sum(grad_tok * flat_acts, axis=1).astype(BF16).astype(F32)
    score = score.reshape(tok_rows, top_count)
    logit_grad = gate_weights * (score - jnp.sum(gate_weights * score, axis=1, keepdims=True))
    return act_grad.reshape(tok_rows, top_count, hidden), logit_grad, summed[None]


def solution(mesh):
    dims = Mesh(mesh.devices.reshape(Y, CORES, X, Z), ("y", "core", "x", "z"))
    tokens = ("y", "core", "x", "z")
    return jax.shard_map(
        shards,
        mesh=dims,
        in_specs=(
            P(tokens, None),
            P(tokens, None, None),
            P(tokens, None),
            P(tokens, None),
            P(("x", "z"), None, None),
        ),
        out_specs=(
            P(tokens, None, None),
            P(tokens, None),
            P(("x", "z"), ("y", "core"), None),
        ),
        check_vma=False,
    )
```

time: 261 us -> 209 us (0.80)
  waiting for transfers between devices: 171 us -> 127 us
  local copies, waits for them, and re-layouts: 10.3 us -> 5.78 us
  starting transfers between devices: 49.6 us -> 45.5 us
  Pallas kernels: 0 us -> 3.72 us
    all_to_all x5 -> x4, waiting for transfers between devices: 165 us -> 66.2 us  [the longest x1 26.4 us: shards(): lax.all_to_all(grad_hidden.reshape(experts, MOST, hidden), ('x', 'z'), sp...]
    all_gather x0 -> x1, waiting for transfers between devices: none -> 54.2 us  [shards(): column = lax.all_gather(out_grad, 'z', axis=0, tiled=True)]
    all_to_all x5 -> x4, starting transfers between devices: 49.5 us -> 41.6 us  [the longest x1 18.9 us: shards(): lax.all_to_all(slot_token.reshape(X, Z, MOST), 'z', split_axis=1, concat_...]
    reshape x6 -> x4, local copies, waits for them, and re-layouts: 7.03 us -> 2.98 us  [the longest x1 0.96 us: shards(): acts_in = lax.all_to_all(send_acts.reshape(experts, MOST, hidden), ('x',...]
    ppermute x0 -> x2, starting transfers between devices: none -> 3.84 us  [the longest x1 1.92 us: shards(): rows_pair = lax.ppermute(rows, 'core', swap)]
    pallas_call x0 -> x1, Pallas kernels: none -> 3.72 us  [weight_term(): pl.pallas_call(weight_kernel, grid=(width // block,), out_shape=jax.Shape...]
    dot_general x8 -> x6, matrix products: 13.5 us -> 11.5 us  [the longest x1 5.09 us: shards(): lax.dot_general(rows, down_weight[0], (((1,), (1,)), ((), ())), preferred...]
  transfers between devices with their start and end apart: 6 -> 8, of which waited for: 6 -> 7; matrix products, arithmetic and copies ran while one was open for 7% -> 7% of each run, Pallas kernels for 0% -> 0%
where the time goes in v1:
time: 209 us; the launch traced here: 208 us
  waiting for transfers between devices  127 us (61%)
  starting transfers between devices  45.5 us (22%)
  between operations  14.2 us (7%)
  matrix products  11.5 us (6%)
  local copies, waits for them, and re-layouts  5.78 us (3%)
  Pallas kernels  3.72 us (2%)
    all_gather x1, waiting for transfers between devices, shards(): column = lax.all_gather(out_grad, 'z', axis=0, tiled=True)  54.2 us
    all_to_all x1, waiting for transfers between devices, shards(): lax.all_to_all(grad_hidden.reshape(experts, MOST, hidden), ('x', 'z'), sp...  26.4 us
    all_to_all x1, starting transfers between devices, shards(): lax.all_to_all(slot_token.reshape(X, Z, MOST), 'z', split_axis=1, concat_...  18.9 us
    all_to_all x1, waiting for transfers between devices, shards(): lax.all_to_all(send_acts.reshape(experts, MOST, hidden), ('x', 'z'), spli...  17 us
    all_to_all x1, waiting for transfers between devices, shards(): lax.all_to_all(slot_token.reshape(X, Z, MOST), 'z', split_axis=1, concat_...  12.6 us
    all_to_all x1, starting transfers between devices, shards(): lax.all_to_all(send_acts.reshape(experts, MOST, hidden), ('x', 'z'), spli...  10.8 us
    all_to_all x1, waiting for transfers between devices, shards(): lax.all_to_all(picked.reshape(X, Z * MOST, picked.shape[1]), 'x', split_a...  10.3 us
    all_to_all x1, starting transfers between devices, shards(): lax.all_to_all(grad_hidden.reshape(experts, MOST, hidden), ('x', 'z'), sp...  6.99 us
  transfers between devices with their start and end apart: 8, of which 7 were waited for; matrix products, arithmetic and copies ran while one was open for 7% of the time, Pallas kernels for 0%

profile of v1, /device:TPU:6, one launch (start us, length us, event | category | flops | bytes accessed | tf_op | source)
XLA Modules:
  0.0 208.4 jit_solution(5721527212034021373)
XLA Ops:
  7.2 0.0 all-gather.2.cloned.1.call-start
  7.2 0.7 all-gather.2.cloned.1.call-update
  7.9 0.8 copy.29
  8.7 0.1 reshape.116
  8.8 0.2 fusion.8
  8.9 0.1 select_reduce_fusion
  9.1 0.1 sub.35
  9.2 0.6 copy.30
  9.9 18.9 %all-to-all-start = ((f32[4,16,3]{2,0,1:T(4,128)}), f32[4,16,3]{2,0,1:T(4,128)S(1)}, u32[]{:S(2)}, u32[]{:S(2)}) async-start(f32[4,16,3]{2,0,1:T(4,128)} %copy.30), calls=%async_computation | async-start | bytes 65536 | tf_op jit(solution)/shard_map/all_to_all | solution.py:71
  28.7 12.6 %all-to-all-done = f32[4,16,3]{2,0,1:T(4,128)S(1)} async-done(((f32[4,16,3]{2,0,1:T(4,128)}), f32[4,16,3]{2,0,1:T(4,128)S(1)}, u32[]{:S(2)}, u32[]{:S(2)}) %all-to-all-start) | async-done | bytes 800 | tf_op jit(solution)/shard_map/all_to_all | solution.py:71
  41.3 0.1 eq.63
  41.4 54.2 %all-gather.2.cloned.1.call-done = bf16[256,4096]{1,0:T(8,128)(2,1)} async-done(((bf16[16,4096]{1,0:T(8,128)(2,1)}), bf16[256,4096]{1,0:T(8,128)(2,1)}) %all-gather.2.cloned.1.call-update) | async-done | bytes 2097168 | tf_op jit(solution)/shard_map/all_gather | solution.py:57
  95.7 3.4 %convolution_convert_fusion = bf16[192,4096]{1,0:T(8,128)(2,1)} fusion(bf16[256,4096]{1,0:T(8,128)(2,1)} %all-gather.2.cloned.1.call-done, f32[256]{0:T(256)S(1)} %iota_convert_fusion, f32[192]{0:T(256)S(1)} %eq.63), kind=kOutput, calls=%fused_computation.2 | convolution fusion | flops 403488768 | bytes 3671808 | tf_op jit(solution)/shard_map/dot_general | solution.py:103
  99.0 0.0 copy-start.2
  99.0 0.0 copy-start
  99.0 4.9 %all-to-all-start.1 = ((bf16[4,48,4096]{2,1,0:T(8,128)(2,1)}), bf16[4,48,4096]{2,1,0:T(8,128)(2,1)S(1)}, u32[]{:S(2)}, u32[]{:S(2)}) async-start(bf16[4,48,4096]{2,1,0:T(8,128)(2,1)} %bitcast), calls=%async_computation.1 | async-start | bytes 3145728 | tf_op jit(solution)/shard_map/all_to_all | solution.py:104
  104.0 0.0 copy-done.2
  104.0 0.1 copy.28
  104.0 0.1 reshape.124
  104.1 0.0 copy-done
  104.1 0.3 convolution_convert_fusion.1
  104.4 0.9 reshape.122
  105.3 10.3 %all-to-all-done.1 = bf16[4,48,4096]{2,1,0:T(8,128)(2,1)S(1)} async-done(((bf16[4,48,4096]{2,1,0:T(8,128)(2,1)}), bf16[4,48,4096]{2,1,0:T(8,128)(2,1)S(1)}, u32[]{:S(2)}, u32[]{:S(2)}) %all-to-all-start.1) | async-done | bytes 1572896 | tf_op jit(solution)/shard_map/all_to_all | solution.py:104
  115.6 10.8 %all-to-all-start.3 = ((bf16[64,3,768]{2,1,0:T(4,128)(2,1)}), bf16[64,3,768]{2,1,0:T(4,128)(2,1)S(1)}, u32[]{:S(2)}, u32[]{:S(2)}) async-start(bf16[64,3,768]{2,1,0:T(4,128)(2,1)} %reshape.122), calls=%async_computation.3 | async-start | bytes 786432 | tf_op jit(solution)/shard_map/all_to_all | solution.py:79
  126.4 0.0 reduce-scatter.2.cloned.1.call-start
  126.5 1.9 collective-permute-start.1
  128.4 17.0 %all-to-all-done.3 = bf16[64,3,768]{2,1,0:T(4,128)(2,1)S(1)} async-done(((bf16[64,3,768]{2,1,0:T(4,128)(2,1)}), bf16[64,3,768]{2,1,0:T(4,128)(2,1)S(1)}, u32[]{:S(2)}, u32[]{:S(2)}) %all-to-all-start.3) | async-done | bytes 294944 | tf_op jit(solution)/shard_map/all_to_all | solution.py:79
  145.4 1.0 reshape.123
  146.4 1.5 fusion.3
  147.9 1.9 collective-permute-start
  149.9 1.4 collective-permute-done.left_pair
  151.3 0.0 collective-permute-done.1.rows_pair
  151.3 3.7 %weight_term.1 = bf16[384,4096]{1,0:T(8,128)(2,1)} custom-call(bf16[384,192]{1,0:T(8,128)(2,1)S(1)} %get-tuple-element.16.left_own, bf16[384,192]{1,0:T(8,128)(2,1)S(1)} %collective-permute-done.left_pair, bf16[192,4096]{1,0:T(8,128)(2,1)S(1)} %bitcast.22, bf16[192,4096]{1,0:T(8,128)(2,1)S(1)} %collective-permute-done.1.rows_pair), custom_call_target="tpu_custom_call" | custom-call | flops 1207959552 | bytes 6586368 | tf_op jit(solution)/shard_map/weight_term/pallas_call | solution.py:26
  155.0 0.0 reduce-scatter.2.cloned.1.call-update
  155.0 5.1 %fusion.4 = bf16[192,768]{1,0:T(8,128)(2,1)S(1)} fusion(bf16[192,4096]{1,0:T(8,128)(2,1)S(1)} %bitcast.23, bf16[1,768,4096]{2,1,0:T(8,128)(2,1)} %param.9), kind=kOutput, calls=%fused_computation.6 | convolution fusion | flops 1208107008 | bytes 8159232 | tf_op jit(solution)/shard_map/dot_general | solution.py:116
  160.1 0.0 copy-start.1
  160.1 0.9 reshape.119
  161.0 7.0 %all-to-all-start.2 = ((bf16[64,3,768]{2,1,0:T(4,128)(2,1)}), bf16[64,3,768]{2,1,0:T(4,128)(2,1)S(1)}, u32[]{:S(2)}, u32[]{:S(2)}) async-start(bf16[64,3,768]{2,1,0:T(4,128)(2,1)} %reshape.119), calls=%async_computation.2 | async-start | bytes 786432 | tf_op jit(solution)/shard_map/all_to_all | solution.py:119
  168.0 0.1 copy.33
  168.1 26.4 %all-to-all-done.2 = bf16[64,3,768]{2,1,0:T(4,128)(2,1)S(1)} async-done(((bf16[64,3,768]{2,1,0:T(4,128)(2,1)}), bf16[64,3,768]{2,1,0:T(4,128)(2,1)S(1)}, u32[]{:S(2)}, u32[]{:S(2)}) %all-to-all-start.2) | async-done | bytes 294944 | tf_op jit(solution)/shard_map/all_to_all | solution.py:119
  194.5 0.2 reshape.120
  194.8 0.0 copy-done.1
  194.8 1.0 fusion.9
  195.8 0.1 reshape.126
  195.9 0.1 multiply_reduce_fusion
  196.0 0.1 subtract_multiply_fusion
  196.1 0.7 copy.35
  196.8 4.8 %reduce-scatter.2.cloned.1.call-done = bf16[48,4096]{1,0:T(8,128)(2,1)} async-done(((bf16[384,4096]{1,0:T(8,128)(2,1)}), bf16[48,4096]{1,0:T(8,128)(2,1)}) %reduce-scatter.2.cloned.1.call-update) | async-done | bytes 393232 | tf_op jit(solution)/shard_map/reduce_scatter | solution.py:114
  (8 shorter events, 0.1 us)
Async XLA Ops:
  7.2 88.5 %all-gather.2.cloned.1.call-start = ((), (), s32[]{:S(2)}) async-start(), calls=%async_computation.5 | async-start | bytes 2228224 | tf_op jit(solution)/shard_map/all_gather | solution.py:57
  9.9 31.4 %all-to-all-start = ((f32[4,16,3]{2,0,1:T(4,128)}), f32[4,16,3]{2,0,1:T(4,128)S(1)}, u32[]{:S(2)}, u32[]{:S(2)}) async-start(f32[4,16,3]{2,0,1:T(4,128)} %copy.30), calls=%async_computation | async-start | bytes 65536 | tf_op jit(solution)/shard_map/all_to_all | solution.py:71
  99.0 4.9 %copy-start.2 = (f32[16,8]{0,1:T(8,128)S(1)}, f32[16,8]{0,1:T(8,128)}, u32[]{:S(2)}) copy-start(f32[16,8]{0,1:T(8,128)} %param.7) | copy-start | bytes 1540
  99.0 5.1 %copy-start = (bf16[16,8,768]{2,1,0:T(8,128)(2,1)S(1)}, bf16[16,8,768]{2,1,0:T(8,128)(2,1)}, u32[]{:S(2)}) copy-start(bf16[16,8,768]{2,1,0:T(8,128)(2,1)} %param.6) | copy-start | bytes 589828
  99.0 16.6 %all-to-all-start.1 = ((bf16[4,48,4096]{2,1,0:T(8,128)(2,1)}), bf16[4,48,4096]{2,1,0:T(8,128)(2,1)S(1)}, u32[]{:S(2)}, u32[]{:S(2)}) async-start(bf16[4,48,4096]{2,1,0:T(8,128)(2,1)} %bitcast), calls=%async_computation.1 | async-start | bytes 3145728 | tf_op jit(solution)/shard_map/all_to_all | solution.py:104
  115.6 29.8 %all-to-all-start.3 = ((bf16[64,3,768]{2,1,0:T(4,128)(2,1)}), bf16[64,3,768]{2,1,0:T(4,128)(2,1)S(1)}, u32[]{:S(2)}, u32[]{:S(2)}) async-start(bf16[64,3,768]{2,1,0:T(4,128)(2,1)} %reshape.122), calls=%async_computation.3 | async-start | bytes 786432 | tf_op jit(solution)/shard_map/all_to_all | solution.py:79
  126.4 75.1 %reduce-scatter.2.cloned.1.call-start = ((), (), s32[]{:S(2)}) async-start(), calls=%async_computation.6 | async-start | bytes 3538944 | tf_op jit(solution)/shard_map/reduce_scatter | solution.py:114
  126.5 24.8 %collective-permute-start.1 = (bf16[192,4096]{1,0:T(8,128)(2,1)S(1)}, bf16[192,4096]{1,0:T(8,128)(2,1)S(1)}, u32[]{:S(2)}, u32[]{:S(2)}) collective-permute-start(bf16[192,4096]{1,0:T(8,128)(2,1)S(1)} %bitcast.21), channel_id=1, source_target_pairs={{0,64},{64,0},{1,65},{65,1},{2,66},{66,2},{3,67},{67,3},{4,68},{68... | collective-permute-start | bytes 4718600 | tf_op jit(solution)/shard_map/ppermute | solution.py:111
  147.9 3.3 %collective-permute-start = (bf16[384,192]{1,0:T(8,128)(2,1)S(1)}, bf16[384,192]{1,0:T(8,128)(2,1)S(1)}, u32[]{:S(2)}, u32[]{:S(2)}) collective-permute-start(bf16[384,192]{1,0:T(8,128)(2,1)S(1)} %get-tuple-element.15), channel_id=1, source_target_pairs={{0,64},{64,0},{1,65},{65,1},{2,66},{66,2},{3,67},{67,3},{4,68},{68... | collective-permute-start | bytes 442376 | tf_op jit(solution)/shard_map/ppermute | solution.py:97
  160.1 34.6 %copy-start.1 = (bf16[16,8,768]{2,1,0:T(8,128)(2,1)S(1)}, bf16[16,8,768]{2,1,0:T(8,128)(2,1)}, u32[]{:S(2)}) copy-start(bf16[16,8,768]{2,1,0:T(8,128)(2,1)} %param.6) | copy-start | bytes 589828
  161.0 33.5 %all-to-all-start.2 = ((bf16[64,3,768]{2,1,0:T(4,128)(2,1)}), bf16[64,3,768]{2,1,0:T(4,128)(2,1)S(1)}, u32[]{:S(2)}, u32[]{:S(2)}) async-start(bf16[64,3,768]{2,1,0:T(4,128)(2,1)} %reshape.119), calls=%async_computation.2 | async-start | bytes 786432 | tf_op jit(solution)/shard_map/all_to_all | solution.py:119
Sparse Core Ops, SparseCore 0:
  10.7 84.9 all-gather.1
  155.1 46.3 reduce-scatter.1

commit v2 on v1

v2 whole, which is shorter than its diff:
```python
import functools

import jax
import jax.numpy as jnp
from jax import lax
from jax.experimental import pallas as pl
from jax.experimental.pallas import tpu as pltpu
from jax.sharding import Mesh
from jax.sharding import PartitionSpec as P

MOST = 3
CORES = 2
X, Y, Z = 4, 8, 16
LANES = 128
EARLY = 1536
BLOCK = 512
BF16 = jnp.bfloat16
F32 = jnp.float32
ROOM = 32 * 1024 * 1024


def pick_kernel(pick, column, after, out):
    del after
    out[...] = jnp.dot(pick[...], column[...], preferred_element_type=F32).astype(out.dtype)


def pick_rows(pick, column, width, after):
    slots, tokens = pick.shape
    return pl.pallas_call(
        pick_kernel,
        grid=(width // BLOCK,),
        out_shape=jax.ShapeDtypeStruct((slots, width), BF16),
        in_specs=[
            pl.BlockSpec((slots, tokens), lambda i: (0, 0)),
            pl.BlockSpec((tokens, BLOCK), lambda i: (0, i)),
            pl.BlockSpec(memory_space=pl.ANY),
        ],
        out_specs=pl.BlockSpec((slots, BLOCK), lambda i: (0, i)),
        compiler_params=pltpu.CompilerParams(vmem_limit_bytes=ROOM),
        cost_estimate=pl.CostEstimate(
            flops=2 * slots * tokens * width,
            bytes_accessed=2 * width * (slots + tokens),
            transcendentals=0,
        ),
        name="pick_rows",
    )(pick, column, after)


def weight_kernel(left_own, left_pair, rows_own, rows_pair, *rest):
    out = rest[-1]
    total = jnp.dot(left_own[...], rows_own[...], preferred_element_type=F32)
    total = total + jnp.dot(left_pair[...], rows_pair[...], preferred_element_type=F32)
    out[...] = total.astype(out.dtype)


def weight_term(left_own, left_pair, rows_own, rows_pair, full, start, into):
    half, slots = left_own.shape
    width = rows_own.shape[1]
    first = start // BLOCK
    operands = [left_own, left_pair, rows_own, rows_pair]
    in_specs = [
        pl.BlockSpec((half, slots), lambda i: (0, 0)),
        pl.BlockSpec((half, slots), lambda i: (0, 0)),
        pl.BlockSpec((slots, BLOCK), lambda i: (0, i)),
        pl.BlockSpec((slots, BLOCK), lambda i: (0, i)),
    ]
    aliases = {}
    if into is not None:
        operands.append(into)
        in_specs.append(pl.BlockSpec(memory_space=pl.ANY))
        aliases = {4: 0}
    return pl.pallas_call(
        weight_kernel,
        grid=(width // BLOCK,),
        out_shape=jax.ShapeDtypeStruct((half, full), BF16),
        in_specs=in_specs,
        out_specs=pl.BlockSpec((half, BLOCK), lambda i: (0, i + first)),
        input_output_aliases=aliases,
        compiler_params=pltpu.CompilerParams(vmem_limit_bytes=ROOM),
        cost_estimate=pl.CostEstimate(
            flops=4 * half * slots * width,
            bytes_accessed=2 * (2 * slots * width + half * width + 2 * half * slots),
            transcendentals=0,
        ),
        name="weight_term",
    )(*operands)


def hidden_kernel(early_steps, rows_early, rows_late, weight, out, total):
    step = pl.program_id(0)

    @pl.when(step == 0)
    def _():
        total[...] = jnp.zeros_like(total)

    def add(rows):
        total[...] += lax.dot_general(
            rows[...], weight[...], (((1,), (1,)), ((), ())), preferred_element_type=F32
        )

    @pl.when(step < early_steps)
    def _():
        add(rows_early)

    @pl.when(step >= early_steps)
    def _():
        add(rows_late)

    @pl.when(step == pl.num_programs(0) - 1)
    def _():
        out[...] = total[...].astype(out.dtype)


def hidden_term(rows_early, rows_late, weight):
    slots = rows_early.shape[0]
    hidden, width = weight.shape[1:]
    early = rows_early.shape[1] // BLOCK
    return pl.pallas_call(
        functools.partial(hidden_kernel, early),
        grid=(width // BLOCK,),
        out_shape=jax.ShapeDtypeStruct((slots, hidden), BF16),
        in_specs=[
            pl.BlockSpec((slots, BLOCK), lambda i: (0, jnp.minimum(i, early - 1))),
            pl.BlockSpec((slots, BLOCK), lambda i: (0, jnp.maximum(i - early, 0))),
            pl.BlockSpec((None, hidden, BLOCK), lambda i: (0, 0, i)),
        ],
        out_specs=pl.BlockSpec((slots, hidden), lambda i: (0, 0)),
        scratch_shapes=[pltpu.VMEM((slots, hidden), F32)],
        compiler_params=pltpu.CompilerParams(vmem_limit_bytes=ROOM),
        cost_estimate=pl.CostEstimate(
            flops=2 * slots * hidden * width,
            bytes_accessed=2 * (slots * width + hidden * width + slots * hidden),
            transcendentals=0,
        ),
        name="hidden_term",
    )(rows_early, rows_late, weight)


def shards(out_grad, hidden_acts, gate_weights, expert_idx, down_weight):
    tok_rows, top_count = expert_idx.shape
    routed = tok_rows * top_count
    width = out_grad.shape[1]
    hidden = hidden_acts.shape[2]
    half = hidden // CORES
    experts = X * Z
    slot_count = experts * MOST
    core = lax.axis_index("core")
    z_at = lax.axis_index("z")
    swap = [(0, 1), (1, 0)]

    column_late = lax.all_gather(out_grad[:, EARLY:], "z", axis=0, tiled=True)

    flat_expert = expert_idx.reshape(routed)
    member = (flat_expert[:, None] == jnp.arange(experts, dtype=jnp.int32)[None, :]).astype(BF16)
    row_line = jnp.arange(routed, dtype=jnp.int32)
    earlier_mask = (row_line[:, None] > row_line[None, :]).astype(BF16)
    earlier = jnp.dot(earlier_mask, member, preferred_element_type=F32)
    position = jnp.sum(earlier * member.astype(F32), axis=1).astype(jnp.int32)
    slot_index = flat_expert * MOST + position
    placement = (jnp.arange(slot_count, dtype=jnp.int32)[:, None] == slot_index[None, :]).astype(BF16)

    plane_of = (jnp.arange(Z, dtype=jnp.int32)[:, None] == (flat_expert % Z)[None, :]).astype(BF16)
    slot_of = (flat_expert // Z) * MOST + position
    token_of = (row_line // top_count + 1).astype(F32)
    token_at = jnp.where(
        slot_of[:, None] == jnp.arange(LANES, dtype=jnp.int32)[None, :], token_of[:, None], 0.0
    ).astype(BF16)
    table = jnp.dot(plane_of, token_at, preferred_element_type=F32).astype(BF16)

    gate_half = lax.optimization_barrier(gate_weights.astype(BF16)).astype(F32)
    flat_acts = hidden_acts.reshape(routed, hidden).astype(F32)
    gated = (gate_half.reshape(routed, 1) * flat_acts).astype(BF16)
    send_acts = jnp.dot(placement, gated, preferred_element_type=F32).astype(BF16)
    acts_in = lax.all_to_all(
        send_acts.reshape(experts, MOST, hidden),
        ("x", "z"),
        split_axis=0,
        concat_axis=0,
        tiled=True,
    ).reshape(slot_count, hidden)

    line = jnp.arange(hidden, dtype=jnp.int32)
    piece = hidden // (Y * CORES)
    unit = ((line % half) // piece * CORES + line // half) * piece + line % piece
    reorder = (unit[:, None] == line[None, :]).astype(BF16)
    left = lax.dot_general(
        reorder, acts_in, (((1,), (1,)), ((), ())), preferred_element_type=F32
    ).astype(BF16)
    left_own = lax.dynamic_slice_in_dim(left, core * half, half, 0)
    left_away = lax.dynamic_slice_in_dim(left, (1 - core) * half, half, 0)
    left_pair = lax.ppermute(left_away, "core", swap)

    column_early = lax.all_gather(
        jnp.concatenate([out_grad[:, :EARLY], table], axis=1), "z", axis=0, tiled=True
    )
    tables = column_early[:, EARLY : EARLY + X * MOST].reshape(Z, Z, X, MOST)
    mine = lax.dynamic_slice_in_dim(tables, z_at, 1, 1).reshape(Z, X, MOST).astype(F32)
    base = (jnp.arange(Z, dtype=jnp.int32) * tok_rows).astype(F32)
    token = jnp.where(mine > 0.0, mine - 1.0 + base[:, None, None], -1.0)
    token = jnp.transpose(token, (1, 0, 2)).reshape(slot_count, 1)
    pick = (token == jnp.arange(Z * tok_rows, dtype=jnp.int32)[None, :].astype(F32)).astype(BF16)

    def rows_of(column, columns, after):
        picked = pick_rows(pick, column, columns, after)
        return lax.all_to_all(
            picked.reshape(X, Z * MOST, columns), "x", split_axis=0, concat_axis=0, tiled=True
        ).reshape(slot_count, columns)

    rows_early = rows_of(column_early, EARLY, left_own)
    pair_early = lax.ppermute(rows_early, "core", swap)
    part = weight_term(left_own, left_pair, rows_early, pair_early, width, 0, None)
    rows_late = rows_of(column_late, width - EARLY, part)
    pair_late = lax.ppermute(rows_late, "core", swap)
    part = weight_term(left_own, left_pair, rows_late, pair_late, width, EARLY, part)
    summed = lax.psum_scatter(part, "y", scatter_dimension=0, tiled=True)

    grad_hidden = hidden_term(rows_early, rows_late, down_weight)
    back = lax.all_to_all(
        grad_hidden.reshape(experts, MOST, hidden),
        ("x", "z"),
        split_axis=0,
        concat_axis=0,
        tiled=True,
    ).reshape(slot_count, hidden)
    grad_tok = lax.dot_general(
        placement, back, (((0,), (0,)), ((), ())), preferred_element_type=F32
    )
    act_grad = (gate_half.reshape(routed, 1) * grad_tok).astype(BF16)
    score = jnp.sum(grad_tok * flat_acts, axis=1).astype(BF16).astype(F32)
    score = score.reshape(tok_rows, top_count)
    logit_grad = gate_weights * (score - jnp.sum(gate_weights * score, axis=1, keepdims=True))
    return act_grad.reshape(tok_rows, top_count, hidden), logit_grad, summed[None]


def solution(mesh):
    dims = Mesh(mesh.devices.reshape(Y, CORES, X, Z), ("y", "core", "x", "z"))
    tokens = ("y", "core", "x", "z")
    return jax.shard_map(
        shards,
        mesh=dims,
        in_specs=(
            P(tokens, None),
            P(tokens, None, None),
            P(tokens, None),
            P(tokens, None),
            P(("x", "z"), None, None),
        ),
        out_specs=(
            P(tokens, None, None),
            P(tokens, None),
            P(("x", "z"), ("y", "core"), None),
        ),
        check_vma=False,
    )
```

time: 209 us -> 200 us (0.957)
  waiting for transfers between devices: 127 us -> 34.2 us
  blocking collectives: 0 us -> 80.3 us
  Pallas kernels: 3.72 us -> 12.3 us
  matrix products: 11.5 us -> 3.22 us
  local copies, waits for them, and re-layouts: 5.78 us -> 11.3 us
  starting transfers between devices: 45.5 us -> 42.3 us
    all_gather x1, waiting for transfers between devices: 54.2 us -> 0.01 us  [shards(): column_late = lax.all_gather(out_grad[:, EARLY:], 'z', axis=0, tiled=True)]
    all_gather x0 -> x1, blocking collectives: none -> 52.1 us  [shards(): lax.all_gather(jnp.concatenate([out_grad[:, :EARLY], table], axis=1), 'z'...]
    all_to_all x0 -> x2, blocking collectives: none -> 28.3 us  [rows_of(): lax.all_to_all(picked.reshape(X, Z * MOST, columns), 'x', split_axis=0, c...]
    all_to_all x2 -> x0, starting transfers between devices: 23.8 us -> none  [the longest x1 18.9 us: shards(): lax.all_to_all(slot_token.reshape(X, Z, MOST), 'z', split_axis=1, concat_...]
    all_to_all x2 -> x0, waiting for transfers between devices: 22.8 us -> none  [the longest x1 12.6 us: shards(): lax.all_to_all(slot_token.reshape(X, Z, MOST), 'z', split_axis=1, concat_...]
    all_to_all x1, waiting for transfers between devices: 17 us -> 0.01 us  [shards(): lax.all_to_all(send_acts.reshape(experts, MOST, hidden), ('x', 'z'), spli...]
    all_to_all x1, starting transfers between devices: 10.8 us -> 22.5 us  [shards(): lax.all_to_all(send_acts.reshape(experts, MOST, hidden), ('x', 'z'), spli...]
    pallas_call x1 -> x5, Pallas kernels: 3.72 us -> 12.3 us  [the longest x2 5.98 us: weight_term(): pl.pallas_call(weight_kernel, grid=(width // BLOCK,), out_shape=jax.Shape...]
  transfers between devices with their start and end apart: 8 -> 7, of which waited for: 7 -> 4; matrix products, arithmetic and copies ran while one was open for 7% -> 5% of each run, Pallas kernels for 0% -> 4%
where the time goes in v2:
time: 200 us; the launch traced here: 199 us
  blocking collectives  80.3 us (40%)
  starting transfers between devices  42.3 us (21%)
  waiting for transfers between devices  34.2 us (17%)
  between operations  14.2 us (7%)
  Pallas kernels  12.3 us (6%)
  local copies, waits for them, and re-layouts  11.3 us (6%)
  matrix products  3.22 us (2%)
    all_gather x1, blocking collectives, shards(): lax.all_gather(jnp.concatenate([out_grad[:, :EARLY], table], axis=1), 'z'...  52.1 us
    all_to_all x2, blocking collectives, rows_of(): lax.all_to_all(picked.reshape(X, Z * MOST, columns), 'x', split_axis=0, c...  28.3 us
    all_to_all x1, waiting for transfers between devices, shards(): lax.all_to_all(grad_hidden.reshape(experts, MOST, hidden), ('x', 'z'), sp...  26.4 us
    all_to_all x1, starting transfers between devices, shards(): lax.all_to_all(send_acts.reshape(experts, MOST, hidden), ('x', 'z'), spli...  22.5 us
    all_to_all x1, starting transfers between devices, shards(): lax.all_to_all(grad_hidden.reshape(experts, MOST, hidden), ('x', 'z'), sp...  13.5 us
    pallas_call x2, Pallas kernels, weight_term(): pl.pallas_call(weight_kernel, grid=(width // BLOCK,), out_shape=jax.Shape...  5.98 us
    unnamed x12, local copies, waits for them, and re-layouts  5.76 us
    pallas_call x1, Pallas kernels, hidden_term(): pl.pallas_call(functools.partial(hidden_kernel, early), grid=(width // BL...  4.28 us
  transfers between devices with their start and end apart: 7, of which 4 were waited for; matrix products, arithmetic and copies ran while one was open for 5% of the time, Pallas kernels for 4%

profile of v2, /device:TPU:6, one launch (start us, length us, event | category | flops | bytes accessed | tf_op | source)
XLA Modules:
  0.0 198.9 jit_solution(5428162876981254475)
XLA Ops:
  7.2 1.5 slice.11
  8.8 0.7 convert_element_type.90
  9.5 0.1 copy.45
  9.5 0.1 reshape.195
  9.6 0.8 copy.46
  10.4 0.1 reshape.184
  10.5 0.2 fusion.3
  10.7 1.2 convolution_convert_fusion
  11.9 0.9 reshape.186
  12.8 22.5 %all-to-all-start = ((bf16[64,3,768]{2,1,0:T(4,128)(2,1)}), bf16[64,3,768]{2,1,0:T(4,128)(2,1)S(1)}, u32[]{:S(2)}, u32[]{:S(2)}) async-start(bf16[64,3,768]{2,1,0:T(4,128)(2,1)} %reshape.186), calls=%async_computation | async-start | bytes 786432 | tf_op jit(solution)/shard_map/all_to_all | solution.py:174
  35.3 0.0 reduce-scatter.2.cloned.1.call-start
  35.3 0.8 slice.9
  36.1 0.2 convolution_convert_fusion.1
  36.3 52.1 %all_gather.6.column = bf16[256,1664]{1,0:T(8,128)(2,1)S(1)} all-gather(bf16[16,1664]{1,0:T(8,128)(2,1)S(1)} %pad_maximum_fusion), channel_id=1, replica_groups=mesh['y'=8,'core'=2,'x'=4,'z'=16] {'z'}, dimensions={0}, use_global_device_ids=true | all-gather | bytes 905216 | tf_op jit(solution)/shard_map/all_gather | solution.py:193
  88.4 0.1 copy.47
  88.5 0.1 reshape.185
  88.6 0.1 constant_dynamic-slice_fusion.2
  88.7 0.1 copy.55
  88.9 0.1 copy.49
  89.0 0.1 eq.94
  89.2 0.1 compare_convert_fusion.pick
  89.3 0.2 reshape.187
  89.5 0.6 fusion.1
  90.2 0.8 pick_rows.2
  91.0 10.7 %all_to_all.20 = bf16[4,48,1536]{2,1,0:T(8,128)(2,1)S(1)} all-to-all(bf16[4,48,1536]{2,1,0:T(8,128)(2,1)S(1)} %bitcast.39), channel_id=1, replica_groups=mesh['y'=8,'core'=2,'x'=4,'z'=16] {'x'}, dimensions={0} | all-to-all | bytes 1179648 | tf_op jit(solution)/shard_map/all_to_all | solution.py:205
  101.7 1.9 collective-permute-start.1
  103.6 2.4 %collective-permute-start = (bf16[384,192]{1,0:T(8,128)(2,1)S(1)}, bf16[384,192]{1,0:T(8,128)(2,1)S(1)}, u32[]{:S(2)}, u32[]{:S(2)}) collective-permute-start(bf16[384,192]{1,0:T(8,128)(2,1)S(1)} %get-tuple-element.20), channel_id=1, source_target_pairs={{0,64},{64,0},{1,65},{65,1},{2,66},{66,2},{3,67},{67,3},{4,68},{68... | collective-permute-start | bytes 442376 | tf_op jit(solution)/shard_map/ppermute | solution.py:191
  106.0 1.0 collective-permute-done.left_pair
  107.1 2.4 %weight_term.2.after.rest_0_ = bf16[384,4096]{1,0:T(8,128)(2,1)} custom-call(bf16[384,192]{1,0:T(8,128)(2,1)S(1)} %get-tuple-element.21.after.left_own, bf16[384,192]{1,0:T(8,128)(2,1)S(1)} %collective-permute-done.left_pair, bf16[192,1536]{1,0:T(8,128)(2,1)S(1)} %bitcast.36, bf16[192,1536]{1,0:T(8,128)(2,1)S(1)} %collective-permute-done.1.rows_pair), custom_call_target="tpu_custom_call" | custom-call | flops 452984832 | bytes 2654208 | tf_op jit(solution)/shard_map/weight_term/pallas_call | solution.py:72
  109.5 1.3 copy-done.1
  110.8 1.2 pick_rows.3
  112.1 17.6 %all_to_all.21 = bf16[4,48,2560]{2,1,0:T(8,128)(2,1)S(1)} all-to-all(bf16[4,48,2560]{2,1,0:T(8,128)(2,1)S(1)} %bitcast.38), channel_id=1, replica_groups=mesh['y'=8,'core'=2,'x'=4,'z'=16] {'x'}, dimensions={0} | all-to-all | bytes 1966080 | tf_op jit(solution)/shard_map/all_to_all | solution.py:205
  129.7 1.9 collective-permute-start.2
  131.6 2.5 %collective-permute-done.2.rows_pair = bf16[192,2560]{1,0:T(8,128)(2,1)S(1)} collective-permute-done((bf16[192,2560]{1,0:T(8,128)(2,1)S(1)}, bf16[192,2560]{1,0:T(8,128)(2,1)S(1)}, u32[]{:S(2)}, u32[]{:S(2)}) %collective-permute-start.2) | collective-permute-done | bytes 983072 | tf_op jit(solution)/shard_map/ppermute | solution.py:213
  134.1 3.5 %weight_term.3 = bf16[384,4096]{1,0:T(8,128)(2,1)} custom-call(bf16[384,192]{1,0:T(8,128)(2,1)S(1)} %get-tuple-element.21.after.left_own, bf16[384,192]{1,0:T(8,128)(2,1)S(1)} %collective-permute-done.left_pair, bf16[192,2560]{1,0:T(8,128)(2,1)S(1)} %bitcast.33, ...), custom_call_target="tpu_custom_call", output_to_operand_aliasing={{}: (4, {})} | custom-call | flops 754974720 | bytes 4227072 | tf_op jit(solution)/shard_map/weight_term/pallas_call | solution.py:72
  137.7 2.8 %copy-done = bf16[1,768,4096]{2,1,0:T(8,128)(2,1)S(1)} copy-done((bf16[1,768,4096]{2,1,0:T(8,128)(2,1)S(1)}, bf16[1,768,4096]{2,1,0:T(8,128)(2,1)}, u32[]{:S(2)}) %copy-start) | copy-done | bytes 6291480
  140.5 4.3 %hidden_term.1 = bf16[192,768]{1,0:T(8,128)(2,1)S(1)} custom-call(bf16[192,1536]{1,0:T(8,128)(2,1)S(1)} %bitcast.37, bf16[192,2560]{1,0:T(8,128)(2,1)S(1)} %bitcast.34, bf16[1,768,4096]{2,1,0:T(8,128)(2,1)S(1)} %copy-done), custom_call_target="tpu_custom_call" | custom-call | flops 1207959552 | bytes 8159232 | tf_op jit(solution)/shard_map/hidden_term/pallas_call | solution.py:118
  144.8 0.9 reshape.192
  145.7 13.5 %all-to-all-start.3 = ((bf16[64,3,768]{2,1,0:T(4,128)(2,1)}), bf16[64,3,768]{2,1,0:T(4,128)(2,1)S(1)}, u32[]{:S(2)}, u32[]{:S(2)}) async-start(bf16[64,3,768]{2,1,0:T(4,128)(2,1)} %reshape.192), calls=%async_computation.3 | async-start | bytes 786432 | tf_op jit(solution)/shard_map/all_to_all | solution.py:218
  159.2 0.1 copy.52
  159.3 26.4 %all-to-all-done.3 = bf16[64,3,768]{2,1,0:T(4,128)(2,1)S(1)} async-done(((bf16[64,3,768]{2,1,0:T(4,128)(2,1)}), bf16[64,3,768]{2,1,0:T(4,128)(2,1)S(1)}, u32[]{:S(2)}, u32[]{:S(2)}) %all-to-all-start.3) | async-done | bytes 294944 | tf_op jit(solution)/shard_map/all_to_all | solution.py:218
  185.7 0.2 reshape.193
  186.0 1.0 fusion.5
  187.0 0.1 reshape.197
  187.1 0.1 multiply_reduce_fusion
  187.2 0.1 subtract_multiply_fusion
  187.3 0.7 copy.53
  188.0 4.1 %reduce-scatter.2.cloned.1.call-done = bf16[48,4096]{1,0:T(8,128)(2,1)} async-done(((bf16[384,4096]{1,0:T(8,128)(2,1)}), bf16[48,4096]{1,0:T(8,128)(2,1)}) %reduce-scatter.2.cloned.1.call-update) | async-done | bytes 393232 | tf_op jit(solution)/shard_map/reduce_scatter | solution.py:215
  (20 shorter events, 0.2 us)
Async XLA Ops:
  7.2 102.3 %all-gather.2.cloned.1.call-start = ((), (), s32[]{:S(2)}) async-start(), calls=%async_computation.5 | async-start | bytes 1392640 | tf_op jit(solution)/shard_map/all_gather | solution.py:151
  12.8 76.5 %all-to-all-start = ((bf16[64,3,768]{2,1,0:T(4,128)(2,1)}), bf16[64,3,768]{2,1,0:T(4,128)(2,1)S(1)}, u32[]{:S(2)}, u32[]{:S(2)}) async-start(bf16[64,3,768]{2,1,0:T(4,128)(2,1)} %reshape.186), calls=%async_computation | async-start | bytes 786432 | tf_op jit(solution)/shard_map/all_to_all | solution.py:174
  35.3 156.8 %reduce-scatter.2.cloned.1.call-start = ((), (), s32[]{:S(2)}) async-start(), calls=%async_computation.6 | async-start | bytes 3538944 | tf_op jit(solution)/shard_map/reduce_scatter | solution.py:215
  101.7 5.4 %collective-permute-start.1 = (bf16[192,1536]{1,0:T(8,128)(2,1)S(1)}, bf16[192,1536]{1,0:T(8,128)(2,1)S(1)}, u32[]{:S(2)}, u32[]{:S(2)}) collective-permute-start(bf16[192,1536]{1,0:T(8,128)(2,1)S(1)} %bitcast.35), channel_id=1, source_target_pairs={{0,64},{64,0},{1,65},{65,1},{2,66},{66,2},{3,67},{67,3},{4,68},{68... | collective-permute-start | bytes 1769480 | tf_op jit(solution)/shard_map/ppermute | solution.py:210
  103.6 3.5 %collective-permute-start = (bf16[384,192]{1,0:T(8,128)(2,1)S(1)}, bf16[384,192]{1,0:T(8,128)(2,1)S(1)}, u32[]{:S(2)}, u32[]{:S(2)}) collective-permute-start(bf16[384,192]{1,0:T(8,128)(2,1)S(1)} %get-tuple-element.20), channel_id=1, source_target_pairs={{0,64},{64,0},{1,65},{65,1},{2,66},{66,2},{3,67},{67,3},{4,68},{68... | collective-permute-start | bytes 442376 | tf_op jit(solution)/shard_map/ppermute | solution.py:191
  109.5 1.3 copy-start.1
  129.7 4.4 %collective-permute-start.2 = (bf16[192,2560]{1,0:T(8,128)(2,1)S(1)}, bf16[192,2560]{1,0:T(8,128)(2,1)S(1)}, u32[]{:S(2)}, u32[]{:S(2)}) collective-permute-start(bf16[192,2560]{1,0:T(8,128)(2,1)S(1)} %bitcast.32), channel_id=1, source_target_pairs={{0,64},{64,0},{1,65},{65,1},{2,66},{66,2},{3,67},{67,3},{4,68},{68... | collective-permute-start | bytes 2949128 | tf_op jit(solution)/shard_map/ppermute | solution.py:213
  137.7 2.8 %copy-start = (bf16[1,768,4096]{2,1,0:T(8,128)(2,1)S(1)}, bf16[1,768,4096]{2,1,0:T(8,128)(2,1)}, u32[]{:S(2)}) copy-start(bf16[1,768,4096]{2,1,0:T(8,128)(2,1)} %weight.1) | copy-start | bytes 18874372
  140.5 18.7 %copy-start.3 = (f32[16,8]{0,1:T(8,128)S(1)}, f32[16,8]{0,1:T(8,128)}, u32[]{:S(2)}) copy-start(f32[16,8]{0,1:T(8,128)} %param.7) | copy-start | bytes 1540
  140.5 45.5 %copy-start.2 = (bf16[16,8,768]{2,1,0:T(8,128)(2,1)S(1)}, bf16[16,8,768]{2,1,0:T(8,128)(2,1)}, u32[]{:S(2)}) copy-start(bf16[16,8,768]{2,1,0:T(8,128)(2,1)} %param.6) | copy-start | bytes 589828
  145.7 40.0 %all-to-all-start.3 = ((bf16[64,3,768]{2,1,0:T(4,128)(2,1)}), bf16[64,3,768]{2,1,0:T(4,128)(2,1)S(1)}, u32[]{:S(2)}, u32[]{:S(2)}) async-start(bf16[64,3,768]{2,1,0:T(4,128)(2,1)} %reshape.192), calls=%async_computation.3 | async-start | bytes 786432 | tf_op jit(solution)/shard_map/all_to_all | solution.py:218
Sparse Core Ops, SparseCore 0:
  11.2 88.5 all-gather.1
  137.8 54.2 reduce-scatter.1

commit v3 on v1

--- a/solution.py
+++ b/solution.py
@@ -9,8 +9,38 @@
 MOST = 3
 CORES = 2
 X, Y, Z = 4, 8, 16
+BLOCK = 1024
 BF16 = jnp.bfloat16
 F32 = jnp.float32
+MIB = 1024 * 1024
+
+
+def pick_kernel(pick, column, after, out):
+    del after
+    out[...] = jnp.dot(pick[...], column[...], preferred_element_type=F32).astype(out.dtype)
+
+
+def pick_rows(pick, column, after):
+    slots, tokens = pick.shape
+    width = column.shape[1]
+    return pl.pallas_call(
+        pick_kernel,
+        grid=(width // BLOCK,),
+        out_shape=jax.ShapeDtypeStruct((slots, width), BF16),
+        in_specs=[
+            pl.BlockSpec((slots, tokens), lambda i: (0, 0)),
+            pl.BlockSpec((tokens, BLOCK), lambda i: (0, i)),
+            pl.BlockSpec(memory_space=pl.ANY),
+        ],
+        out_specs=pl.BlockSpec((slots, BLOCK), lambda i: (0, i)),
+        compiler_params=pltpu.CompilerParams(vmem_limit_bytes=60 * MIB),
+        cost_estimate=pl.CostEstimate(
+            flops=2 * slots * tokens * width,
+            bytes_accessed=2 * width * (slots + tokens),
+            transcendentals=0,
+        ),
+        name="pick_rows",
+    )(pick, column, after)
 
 
 def weight_kernel(left_own, left_pair, rows_own, rows_pair, out):
@@ -22,19 +52,18 @@
 def weight_term(left_own, left_pair, rows_own, rows_pair):
     half, slots = left_own.shape
     width = rows_own.shape[1]
-    block = 1024
     return pl.pallas_call(
         weight_kernel,
-        grid=(width // block,),
+        grid=(width // BLOCK,),
         out_shape=jax.ShapeDtypeStruct((half, width), BF16),
         in_specs=[
             pl.BlockSpec((half, slots), lambda i: (0, 0)),
             pl.BlockSpec((half, slots), lambda i: (0, 0)),
-            pl.BlockSpec((slots, block), lambda i: (0, i)),
-            pl.BlockSpec((slots, block), lambda i: (0, i)),
+            pl.BlockSpec((slots, BLOCK), lambda i: (0, i)),
+            pl.BlockSpec((slots, BLOCK), lambda i: (0, i)),
         ],
-        out_specs=pl.BlockSpec((half, block), lambda i: (0, i)),
-        compiler_params=pltpu.CompilerParams(vmem_limit_bytes=32 * 1024 * 1024),
+        out_specs=pl.BlockSpec((half, BLOCK), lambda i: (0, i)),
+        compiler_params=pltpu.CompilerParams(vmem_limit_bytes=49 * MIB),
         cost_estimate=pl.CostEstimate(
             flops=4 * half * slots * width,
             bytes_accessed=2 * (2 * slots * width + half * width + 2 * half * slots),
@@ -44,15 +73,56 @@
     )(left_own, left_pair, rows_own, rows_pair)
 
 
+def hidden_kernel(rows, weight, out, total):
+    step = pl.program_id(0)
+
+    @pl.when(step == 0)
+    def _():
+        total[...] = jnp.zeros_like(total)
+
+    total[...] += lax.dot_general(
+        rows[...], weight[...], (((1,), (1,)), ((), ())), preferred_element_type=F32
+    )
+
+    @pl.when(step == pl.num_programs(0) - 1)
+    def _():
+        out[...] = total[...].astype(out.dtype)
+
+
+def hidden_term(rows, weight):
+    slots = rows.shape[0]
+    hidden, width = weight.shape[1:]
+    return pl.pallas_call(
+        hidden_kernel,
+        grid=(width // BLOCK,),
+        out_shape=jax.ShapeDtypeStruct((slots, hidden), BF16),
+        in_specs=[
+            pl.BlockSpec((slots, BLOCK), lambda i: (0, i)),
+            pl.BlockSpec((None, hidden, BLOCK), lambda i: (0, 0, i)),
+        ],
+        out_specs=pl.BlockSpec((slots, hidden), lambda i: (0, 0)),
+        scratch_shapes=[pltpu.VMEM((slots, hidden), F32)],
+        compiler_params=pltpu.CompilerParams(vmem_limit_bytes=49 * MIB),
+        cost_estimate=pl.CostEstimate(
+            flops=2 * slots * hidden * width,
+            bytes_accessed=2 * (slots * width + hidden * width + slots * hidden),
+            transcendentals=0,
+        ),
+        name="hidden_term",
+    )(rows, weight)
+
+
 def shards(out_grad, hidden_acts, gate_weights, expert_idx, down_weight):
     tok_rows, top_count = expert_idx.shape
     routed = tok_rows * top_count
+    width = out_grad.shape[1]
     hidden = hidden_acts.shape[2]
     half = hidden // CORES
     experts = X * Z
     slot_count = experts * MOST
     core = lax.axis_index("core")
     z_at = lax.axis_index("z")
+    swap = [(0, 1), (1, 0)]
 
     column = lax.all_gather(out_grad, "z", axis=0, tiled=True)
 
@@ -63,14 +133,15 @@
     earlier = jnp.dot(earlier_mask, member, preferred_element_type=F32)
     position = jnp.sum(earlier * member.astype(F32), axis=1).astype(jnp.int32)
     slot_index = flat_expert * MOST + position
+    placement = (jnp.arange(slot_count, dtype=jnp.int32)[:, None] == slot_index[None, :]).astype(BF16)
+
     taken = jnp.arange(slot_count, dtype=jnp.int32)[:, None] == slot_index[None, :]
-    placement = taken.astype(BF16)
-
     token_of = (z_at * tok_rows + row_line // top_count).astype(F32)
-    slot_token = jnp.sum(jnp.where(taken, token_of[None, :] + 1.0, 0.0), axis=1) - 1.0
-    slot_token = lax.all_to_all(
-        slot_token.reshape(X, Z, MOST), "z", split_axis=1, concat_axis=1, tiled=True
-    )
+    token = jnp.sum(jnp.where(taken, token_of[None, :] + 1.0, 0.0), axis=1) - 1.0
+    token = lax.all_to_all(
+        token.reshape(X, Z, MOST), "z", split_axis=1, concat_axis=1, tiled=True
+    ).reshape(slot_count, 1)
+    pick = (token == jnp.arange(Z * tok_rows, dtype=jnp.int32)[None, :].astype(F32)).astype(BF16)
 
     gate_half = lax.optimization_barrier(gate_weights.astype(BF16)).astype(F32)
     flat_acts = hidden_acts.reshape(routed, hidden).astype(F32)
@@ -93,29 +164,19 @@
     ).astype(BF16)
     left_own = lax.dynamic_slice_in_dim(left, core * half, half, 0)
     left_away = lax.dynamic_slice_in_dim(left, (1 - core) * half, half, 0)
-    swap = [(0, 1), (1, 0)]
+
+    picked = pick_rows(pick, column, acts_in)
+    rows = lax.all_to_all(
+        picked.reshape(X, Z * MOST, width), "x", split_axis=0, concat_axis=0, tiled=True
+    ).reshape(slot_count, width)
+    rows, left_own, left_away = lax.optimization_barrier((rows, left_own, left_away))
     left_pair = lax.ppermute(left_away, "core", swap)
-
-    pick = (
-        slot_token.reshape(slot_count, 1)
-        == jnp.arange(Z * tok_rows, dtype=jnp.int32)[None, :].astype(F32)
-    ).astype(BF16)
-    picked = jnp.dot(pick, column, preferred_element_type=F32).astype(BF16)
-    rows = lax.all_to_all(
-        picked.reshape(X, Z * MOST, picked.shape[1]),
-        "x",
-        split_axis=0,
-        concat_axis=0,
-        tiled=True,
-    ).reshape(slot_count, picked.shape[1])
     rows_pair = lax.ppermute(rows, "core", swap)
 
-    weight_part = weight_term(left_own, left_pair, rows, rows_pair)
-    summed = lax.psum_scatter(weight_part, "y", scatter_dimension=0, tiled=True)
-
-    grad_hidden = lax.dot_general(
-        rows, down_weight[0], (((1,), (1,)), ((), ())), preferred_element_type=F32
-    ).astype(BF16)
+    part = weight_term(left_own, left_pair, rows, rows_pair)
+    summed = lax.psum_scatter(part, "y", scatter_dimension=0, tiled=True)
+
+    grad_hidden = hidden_term(rows, down_weight)
     back = lax.all_to_all(
         grad_hidden.reshape(experts, MOST, hidden),
         ("x", "z"),

time: 209 us -> 194 us (0.928)
  waiting for transfers between devices: 127 us -> 110 us
  Pallas kernels: 3.72 us -> 13.1 us
  matrix products: 11.5 us -> 3.01 us
    all_gather x1, waiting for transfers between devices: 54.2 us -> 26.6 us  [shards(): column = lax.all_gather(out_grad, 'z', axis=0, tiled=True)]
    all_to_all x1, waiting for transfers between devices: 17 us -> 29.7 us  [shards(): lax.all_to_all(send_acts.reshape(experts, MOST, hidden), ('x', 'z'), spli...]
    pallas_call x1 -> x3, Pallas kernels: 3.72 us -> 13.1 us  [the longest x1 5.18 us: hidden_term(): pl.pallas_call(hidden_kernel, grid=(width // BLOCK,), out_shape=jax.Shape...]
    dot_general x2 -> x0, matrix products: 8.45 us -> none  [the longest x1 5.09 us: shards(): lax.dot_general(rows, down_weight[0], (((1,), (1,)), ((), ())), preferred...]
    all_to_all x1, starting transfers between devices: 10.8 us -> 6.07 us  [shards(): lax.all_to_all(send_acts.reshape(experts, MOST, hidden), ('x', 'z'), spli...]
    all_to_all x1, starting transfers between devices: 6.99 us -> 10.4 us  [shards(): lax.all_to_all(grad_hidden.reshape(experts, MOST, hidden), ('x', 'z'), sp...]
  transfers between devices with their start and end apart: 8 -> 8, of which waited for: 7 -> 7; matrix products, arithmetic and copies ran while one was open for 7% -> 5% of each run, Pallas kernels for 0% -> 3%
where the time goes in v3:
time: 194 us; the launch traced here: 193 us
  waiting for transfers between devices  110 us (57%)
  starting transfers between devices  44.9 us (23%)
  between operations  14.2 us (7%)
  Pallas kernels  13.1 us (7%)
  local copies, waits for them, and re-layouts  5.78 us (3%)
  matrix products  3.01 us (2%)
    all_to_all x1, waiting for transfers between devices, shards(): lax.all_to_all(send_acts.reshape(experts, MOST, hidden), ('x', 'z'), spli...  29.7 us
    all_gather x1, waiting for transfers between devices, shards(): column = lax.all_gather(out_grad, 'z', axis=0, tiled=True)  26.6 us
    all_to_all x1, waiting for transfers between devices, shards(): lax.all_to_all(grad_hidden.reshape(experts, MOST, hidden), ('x', 'z'), sp...  26.5 us
    all_to_all x1, starting transfers between devices, shards(): lax.all_to_all(token.reshape(X, Z, MOST), 'z', split_axis=1, concat_axis=...  18.9 us
    all_to_all x1, waiting for transfers between devices, shards(): lax.all_to_all(picked.reshape(X, Z * MOST, width), 'x', split_axis=0, con...  11.5 us
    all_to_all x1, starting transfers between devices, shards(): lax.all_to_all(grad_hidden.reshape(experts, MOST, hidden), ('x', 'z'), sp...  10.4 us
    all_to_all x1, waiting for transfers between devices, shards(): lax.all_to_all(token.reshape(X, Z, MOST), 'z', split_axis=1, concat_axis=...  9.58 us
    all_to_all x1, starting transfers between devices, shards(): lax.all_to_all(send_acts.reshape(experts, MOST, hidden), ('x', 'z'), spli...  6.07 us
  transfers between devices with their start and end apart: 8, of which 7 were waited for; matrix products, arithmetic and copies ran while one was open for 5% of the time, Pallas kernels for 3%

profile of v3, /device:TPU:6, one launch (start us, length us, event | category | flops | bytes accessed | tf_op | source)
XLA Modules:
  0.0 193.0 jit_solution(9117689765545915811)
XLA Ops:
  7.2 0.0 all-gather.2.cloned.1.call-start
  7.2 0.7 all-gather.2.cloned.1.call-update
  7.9 0.8 copy.29
  8.7 0.1 reshape.116
  8.8 0.2 fusion.3
  8.9 0.1 select_reduce_fusion
  9.1 0.1 sub.35
  9.2 0.6 copy.30
  9.9 18.9 %all-to-all-start = ((f32[4,16,3]{2,0,1:T(4,128)}), f32[4,16,3]{2,0,1:T(4,128)S(1)}, u32[]{:S(2)}, u32[]{:S(2)}) async-start(f32[4,16,3]{2,0,1:T(4,128)} %copy.30), calls=%async_computation | async-start | bytes 65536 | tf_op jit(solution)/shard_map/all_to_all | solution.py:141
  28.7 0.7 convert_element_type.68
  29.4 0.1 copy.28
  29.5 0.1 reshape.124
  29.6 1.2 convolution_convert_fusion
  30.8 0.9 reshape.117
  31.7 9.6 %all-to-all-done = f32[4,16,3]{2,0,1:T(4,128)S(1)} async-done(((f32[4,16,3]{2,0,1:T(4,128)}), f32[4,16,3]{2,0,1:T(4,128)S(1)}, u32[]{:S(2)}, u32[]{:S(2)}) %all-to-all-start) | async-done | bytes 800 | tf_op jit(solution)/shard_map/all_to_all | solution.py:141
  41.3 6.1 %all-to-all-start.1 = ((bf16[64,3,768]{2,1,0:T(4,128)(2,1)}), bf16[64,3,768]{2,1,0:T(4,128)(2,1)S(1)}, u32[]{:S(2)}, u32[]{:S(2)}) async-start(bf16[64,3,768]{2,1,0:T(4,128)(2,1)} %reshape.117), calls=%async_computation.1 | async-start | bytes 786432 | tf_op jit(solution)/shard_map/all_to_all | solution.py:150
  47.4 0.1 eq.35
  47.5 0.7 compare_convert_fusion.pick
  48.3 29.7 %all-to-all-done.1 = bf16[64,3,768]{2,1,0:T(4,128)(2,1)S(1)} async-done(((bf16[64,3,768]{2,1,0:T(4,128)(2,1)}), bf16[64,3,768]{2,1,0:T(4,128)(2,1)S(1)}, u32[]{:S(2)}, u32[]{:S(2)}) %all-to-all-start.1) | async-done | bytes 294944 | tf_op jit(solution)/shard_map/all_to_all | solution.py:150
  78.0 1.0 reshape.118.after
  79.0 26.6 %all-gather.2.cloned.1.call-done.column = bf16[256,4096]{1,0:T(8,128)(2,1)} async-done(((bf16[16,4096]{1,0:T(8,128)(2,1)}), bf16[256,4096]{1,0:T(8,128)(2,1)}) %all-gather.2.cloned.1.call-update) | async-done | bytes 2097168 | tf_op jit(solution)/shard_map/all_gather | solution.py:127
  105.6 4.2 %pick_rows.1 = bf16[192,4096]{1,0:T(8,128)(2,1)} custom-call(bf16[192,256]{1,0:T(8,128)(2,1)} %compare_convert_fusion.pick, bf16[256,4096]{1,0:T(8,128)(2,1)} %all-gather.2.cloned.1.call-done.column, bf16[192,768]{1,0:T(8,128)(2,1)} %reshape.118.after), custom_call_target="tpu_custom_call" | custom-call | flops 402653184 | bytes 3670016 | tf_op jit(solution)/shard_map/pick_rows/pallas_call | solution.py:26
  109.8 5.2 %all-to-all-start.2 = ((bf16[4,48,4096]{2,1,0:T(8,128)(2,1)}), bf16[4,48,4096]{2,1,0:T(8,128)(2,1)S(1)}, u32[]{:S(2)}, u32[]{:S(2)}) async-start(bf16[4,48,4096]{2,1,0:T(8,128)(2,1)} %bitcast.17), calls=%async_computation.2 | async-start | bytes 3145728 | tf_op jit(solution)/shard_map/all_to_all | solution.py:169
  115.0 0.0 reduce-scatter.2.cloned.1.call-start
  115.1 0.0 copy-done
  115.1 0.6 fusion.1
  115.7 11.5 %all-to-all-done.2 = bf16[4,48,4096]{2,1,0:T(8,128)(2,1)S(1)} async-done(((bf16[4,48,4096]{2,1,0:T(8,128)(2,1)}), bf16[4,48,4096]{2,1,0:T(8,128)(2,1)S(1)}, u32[]{:S(2)}, u32[]{:S(2)}) %all-to-all-start.2) | async-done | bytes 1572896 | tf_op jit(solution)/shard_map/all_to_all | solution.py:169
  127.2 1.9 collective-permute-start.1
  129.1 2.4 %collective-permute-start = (bf16[384,192]{1,0:T(8,128)(2,1)S(1)}, bf16[384,192]{1,0:T(8,128)(2,1)S(1)}, u32[]{:S(2)}, u32[]{:S(2)}) collective-permute-start(bf16[384,192]{1,0:T(8,128)(2,1)S(1)} %get-tuple-element.8), channel_id=1, source_target_pairs={{0,64},{64,0},{1,65},{65,1},{2,66},{66,2},{3,67},{67,3},{4,68},{68... | collective-permute-start | bytes 442376 | tf_op jit(solution)/shard_map/ppermute | solution.py:173
  131.5 1.2 collective-permute-done.left_pair
  132.7 0.0 collective-permute-done.1.rows_pair
  132.7 3.7 %weight_term.1 = bf16[384,4096]{1,0:T(8,128)(2,1)} custom-call(bf16[384,192]{1,0:T(8,128)(2,1)S(1)} %get-tuple-element.7.left_own, bf16[384,192]{1,0:T(8,128)(2,1)S(1)} %collective-permute-done.left_pair, bf16[192,4096]{1,0:T(8,128)(2,1)S(1)} %bitcast.15, bf16[192,4096]{1,0:T(8,128)(2,1)S(1)} %collective-permute-done.1.rows_pair), custom_call_target="tpu_custom_call" | custom-call | flops 1207959552 | bytes 6586368 | tf_op jit(solution)/shard_map/weight_term/pallas_call | solution.py:55
  136.5 0.0 reduce-scatter.2.cloned.1.call-update
  136.5 0.0 copy-start.2
  136.5 0.0 copy-start.1
  136.5 5.2 %hidden_term.1 = bf16[192,768]{1,0:T(8,128)(2,1)S(1)} custom-call(bf16[192,4096]{1,0:T(8,128)(2,1)S(1)} %bitcast.16, bf16[1,768,4096]{2,1,0:T(8,128)(2,1)} %weight.1), custom_call_target="tpu_custom_call" | custom-call | flops 1207959552 | bytes 8159232 | tf_op jit(solution)/shard_map/hidden_term/pallas_call | solution.py:95
  141.7 0.9 reshape.121
  142.6 10.4 %all-to-all-start.3 = ((bf16[64,3,768]{2,1,0:T(4,128)(2,1)}), bf16[64,3,768]{2,1,0:T(4,128)(2,1)S(1)}, u32[]{:S(2)}, u32[]{:S(2)}) async-start(bf16[64,3,768]{2,1,0:T(4,128)(2,1)} %reshape.121), calls=%async_computation.3 | async-start | bytes 786432 | tf_op jit(solution)/shard_map/all_to_all | solution.py:180
  153.0 0.0 copy-done.2
  153.0 0.1 copy.34
  153.1 26.5 %all-to-all-done.3 = bf16[64,3,768]{2,1,0:T(4,128)(2,1)S(1)} async-done(((bf16[64,3,768]{2,1,0:T(4,128)(2,1)}), bf16[64,3,768]{2,1,0:T(4,128)(2,1)S(1)}, u32[]{:S(2)}, u32[]{:S(2)}) %all-to-all-start.3) | async-done | bytes 294944 | tf_op jit(solution)/shard_map/all_to_all | solution.py:180
  179.5 0.2 reshape.122
  179.8 1.0 fusion.5
  180.8 0.1 reshape.126
  180.9 0.1 multiply_reduce_fusion
  181.0 0.1 subtract_multiply_fusion
  181.1 0.7 copy.35
  181.8 4.4 %reduce-scatter.2.cloned.1.call-done = bf16[48,4096]{1,0:T(8,128)(2,1)} async-done(((bf16[384,4096]{1,0:T(8,128)(2,1)}), bf16[48,4096]{1,0:T(8,128)(2,1)}) %reduce-scatter.2.cloned.1.call-update) | async-done | bytes 393232 | tf_op jit(solution)/shard_map/reduce_scatter | solution.py:177
  (9 shorter events, 0.1 us)
Async XLA Ops:
  7.2 98.4 %all-gather.2.cloned.1.call-start = ((), (), s32[]{:S(2)}) async-start(), calls=%async_computation.5 | async-start | bytes 2228224 | tf_op jit(solution)/shard_map/all_gather | solution.py:127
  9.9 31.4 %all-to-all-start = ((f32[4,16,3]{2,0,1:T(4,128)}), f32[4,16,3]{2,0,1:T(4,128)S(1)}, u32[]{:S(2)}, u32[]{:S(2)}) async-start(f32[4,16,3]{2,0,1:T(4,128)} %copy.30), calls=%async_computation | async-start | bytes 65536 | tf_op jit(solution)/shard_map/all_to_all | solution.py:141
  41.3 36.7 %all-to-all-start.1 = ((bf16[64,3,768]{2,1,0:T(4,128)(2,1)}), bf16[64,3,768]{2,1,0:T(4,128)(2,1)S(1)}, u32[]{:S(2)}, u32[]{:S(2)}) async-start(bf16[64,3,768]{2,1,0:T(4,128)(2,1)} %reshape.117), calls=%async_computation.1 | async-start | bytes 786432 | tf_op jit(solution)/shard_map/all_to_all | solution.py:150
  109.8 5.2 %copy-start = (bf16[192,768]{1,0:T(8,128)(2,1)S(1)}, bf16[192,768]{1,0:T(8,128)(2,1)}, u32[]{:S(2)}) copy-start(bf16[192,768]{1,0:T(8,128)(2,1)} %reshape.118.after) | copy-start | bytes 884740
  109.8 17.3 %all-to-all-start.2 = ((bf16[4,48,4096]{2,1,0:T(8,128)(2,1)}), bf16[4,48,4096]{2,1,0:T(8,128)(2,1)S(1)}, u32[]{:S(2)}, u32[]{:S(2)}) async-start(bf16[4,48,4096]{2,1,0:T(8,128)(2,1)} %bitcast.17), calls=%async_computation.2 | async-start | bytes 3145728 | tf_op jit(solution)/shard_map/all_to_all | solution.py:169
  115.0 71.2 %reduce-scatter.2.cloned.1.call-start = ((), (), s32[]{:S(2)}) async-start(), calls=%async_computation.6 | async-start | bytes 3538944 | tf_op jit(solution)/shard_map/reduce_scatter | solution.py:177
  127.2 5.6 %collective-permute-start.1 = (bf16[192,4096]{1,0:T(8,128)(2,1)S(1)}, bf16[192,4096]{1,0:T(8,128)(2,1)S(1)}, u32[]{:S(2)}, u32[]{:S(2)}) collective-permute-start(bf16[192,4096]{1,0:T(8,128)(2,1)S(1)} %bitcast.14), channel_id=1, source_target_pairs={{0,64},{64,0},{1,65},{65,1},{2,66},{66,2},{3,67},{67,3},{4,68},{68... | collective-permute-start | bytes 4718600 | tf_op jit(solution)/shard_map/ppermute | solution.py:174
  129.1 3.7 %collective-permute-start = (bf16[384,192]{1,0:T(8,128)(2,1)S(1)}, bf16[384,192]{1,0:T(8,128)(2,1)S(1)}, u32[]{:S(2)}, u32[]{:S(2)}) collective-permute-start(bf16[384,192]{1,0:T(8,128)(2,1)S(1)} %get-tuple-element.8), channel_id=1, source_target_pairs={{0,64},{64,0},{1,65},{65,1},{2,66},{66,2},{3,67},{67,3},{4,68},{68... | collective-permute-start | bytes 442376 | tf_op jit(solution)/shard_map/ppermute | solution.py:173
  136.5 16.5 %copy-start.2 = (f32[16,8]{0,1:T(8,128)S(1)}, f32[16,8]{0,1:T(8,128)}, u32[]{:S(2)}) copy-start(f32[16,8]{0,1:T(8,128)} %param.7) | copy-start | bytes 1540
  136.5 43.3 %copy-start.1 = (bf16[16,8,768]{2,1,0:T(8,128)(2,1)S(1)}, bf16[16,8,768]{2,1,0:T(8,128)(2,1)}, u32[]{:S(2)}) copy-start(bf16[16,8,768]{2,1,0:T(8,128)(2,1)} %param.6) | copy-start | bytes 589828
  142.6 36.9 %all-to-all-start.3 = ((bf16[64,3,768]{2,1,0:T(4,128)(2,1)}), bf16[64,3,768]{2,1,0:T(4,128)(2,1)S(1)}, u32[]{:S(2)}, u32[]{:S(2)}) async-start(bf16[64,3,768]{2,1,0:T(4,128)(2,1)} %reshape.121), calls=%async_computation.3 | async-start | bytes 786432 | tf_op jit(solution)/shard_map/all_to_all | solution.py:180
Sparse Core Ops, SparseCore 0:
  10.7 94.8 all-gather.1
  136.6 49.5 reduce-scatter.1

commit v4 on v3

--- a/solution.py
+++ b/solution.py
@@ -7,40 +7,60 @@
 from jax.sharding import PartitionSpec as P
 
 MOST = 3
+TOK = 16
 CORES = 2
-X, Y, Z = 4, 8, 16
+X, Y, ZH, ZL = 4, 8, 4, 4
+Z = ZH * ZL
+LANES = 128
 BLOCK = 1024
 BF16 = jnp.bfloat16
 F32 = jnp.float32
 MIB = 1024 * 1024
 
 
-def pick_kernel(pick, column, after, out):
+def pick_kernel(home, lane, *refs):
+    blocks, tables, (after, out, pick) = refs[:5], refs[5:10], refs[10:]
     del after
-    out[...] = jnp.dot(pick[...], column[...], preferred_element_type=F32).astype(out.dtype)
-
-
-def pick_rows(pick, column, after):
     slots, tokens = pick.shape
-    width = column.shape[1]
+
+    @pl.when(pl.program_id(0) == 0)
+    def _():
+        at = lax.broadcasted_iota(jnp.int32, (slots, tokens), 1)
+        line = jnp.where(at == home[...], 1.0, 0.0).astype(BF16)
+        table = jnp.concatenate([ref[...] for ref in tables], axis=0)
+        values = jnp.dot(line, table, preferred_element_type=F32)
+        lanes = lax.broadcasted_iota(jnp.int32, values.shape, 1)
+        value = jnp.sum(jnp.where(lanes == lane[...], values, 0.0), axis=1, keepdims=True)
+        first = home[...] // TOK * TOK
+        token = jnp.where(value > 0.0, value.astype(jnp.int32) - 1 + first, -1)
+        pick[...] = jnp.where(at == token, 1.0, 0.0).astype(pick.dtype)
+
+    held = jnp.concatenate([ref[...] for ref in blocks], axis=0)
+    out[...] = jnp.dot(pick[...], held, preferred_element_type=F32).astype(out.dtype)
+
+
+def pick_rows(home, lane, blocks, width, after):
+    slots = home.shape[0]
+    tokens = sum(block.shape[0] for block in blocks)
+    last = width // LANES
     return pl.pallas_call(
         pick_kernel,
         grid=(width // BLOCK,),
         out_shape=jax.ShapeDtypeStruct((slots, width), BF16),
-        in_specs=[
-            pl.BlockSpec((slots, tokens), lambda i: (0, 0)),
-            pl.BlockSpec((tokens, BLOCK), lambda i: (0, i)),
-            pl.BlockSpec(memory_space=pl.ANY),
-        ],
+        in_specs=[pl.BlockSpec((slots, 1), lambda i: (0, 0))] * 2
+        + [pl.BlockSpec((block.shape[0], BLOCK), lambda i: (0, i)) for block in blocks]
+        + [pl.BlockSpec((block.shape[0], LANES), lambda i: (0, last)) for block in blocks]
+        + [pl.BlockSpec(memory_space=pl.ANY)],
         out_specs=pl.BlockSpec((slots, BLOCK), lambda i: (0, i)),
-        compiler_params=pltpu.CompilerParams(vmem_limit_bytes=60 * MIB),
+        scratch_shapes=[pltpu.VMEM((slots, tokens), BF16)],
+        compiler_params=pltpu.CompilerParams(vmem_limit_bytes=49 * MIB),
         cost_estimate=pl.CostEstimate(
             flops=2 * slots * tokens * width,
             bytes_accessed=2 * width * (slots + tokens),
             transcendentals=0,
         ),
         name="pick_rows",
-    )(pick, column, after)
+    )(home, lane, *blocks, *blocks, after)
 
 
 def weight_kernel(left_own, left_pair, rows_own, rows_pair, out):
@@ -73,7 +93,7 @@
     )(left_own, left_pair, rows_own, rows_pair)
 
 
-def hidden_kernel(rows, weight, out, total):
+def hidden_kernel(rows, weight, order, out, total):
     step = pl.program_id(0)
 
     @pl.when(step == 0)
@@ -86,10 +106,11 @@
 
     @pl.when(step == pl.num_programs(0) - 1)
     def _():
-        out[...] = total[...].astype(out.dtype)
-
-
-def hidden_term(rows, weight):
+        rounded = total[...].astype(BF16)
+        out[...] = jnp.dot(order[...], rounded, preferred_element_type=F32).astype(out.dtype)
+
+
+def hidden_term(rows, weight, order):
     slots = rows.shape[0]
     hidden, width = weight.shape[1:]
     return pl.pallas_call(
@@ -99,6 +120,7 @@
         in_specs=[
             pl.BlockSpec((slots, BLOCK), lambda i: (0, i)),
             pl.BlockSpec((None, hidden, BLOCK), lambda i: (0, 0, i)),
+            pl.BlockSpec((slots, slots), lambda i: (0, 0)),
         ],
         out_specs=pl.BlockSpec((slots, hidden), lambda i: (0, 0)),
         scratch_shapes=[pltpu.VMEM((slots, hidden), F32)],
@@ -109,7 +131,7 @@
             transcendentals=0,
         ),
         name="hidden_term",
-    )(rows, weight)
+    )(rows, weight, order)
 
 
 def shards(out_grad, hidden_acts, gate_weights, expert_idx, down_weight):
@@ -121,10 +143,9 @@
     experts = X * Z
     slot_count = experts * MOST
     core = lax.axis_index("core")
-    z_at = lax.axis_index("z")
+    planes = ("zh", "zl")
+    z_at = lax.axis_index(planes)
     swap = [(0, 1), (1, 0)]
-
-    column = lax.all_gather(out_grad, "z", axis=0, tiled=True)
 
     flat_expert = expert_idx.reshape(routed)
     member = (flat_expert[:, None] == jnp.arange(experts, dtype=jnp.int32)[None, :]).astype(BF16)
@@ -135,13 +156,27 @@
     slot_index = flat_expert * MOST + position
     placement = (jnp.arange(slot_count, dtype=jnp.int32)[:, None] == slot_index[None, :]).astype(BF16)
 
-    taken = jnp.arange(slot_count, dtype=jnp.int32)[:, None] == slot_index[None, :]
-    token_of = (z_at * tok_rows + row_line // top_count).astype(F32)
-    token = jnp.sum(jnp.where(taken, token_of[None, :] + 1.0, 0.0), axis=1) - 1.0
-    token = lax.all_to_all(
-        token.reshape(X, Z, MOST), "z", split_axis=1, concat_axis=1, tiled=True
-    ).reshape(slot_count, 1)
-    pick = (token == jnp.arange(Z * tok_rows, dtype=jnp.int32)[None, :].astype(F32)).astype(BF16)
+    plane_of = (jnp.arange(Z, dtype=jnp.int32)[:, None] == (flat_expert % Z)[None, :]).astype(BF16)
+    lane_of = (flat_expert // Z) * MOST + position
+    token_of = (row_line // top_count + 1).astype(F32)
+    token_at = jnp.where(
+        lane_of[:, None] == jnp.arange(LANES, dtype=jnp.int32)[None, :], token_of[:, None], 0.0
+    ).astype(BF16)
+    table = jnp.dot(plane_of, token_at, preferred_element_type=F32).astype(BF16)
+
+    own = lax.all_gather(jnp.concatenate([out_grad, table], axis=1), "zh", axis=0, tiled=True)
+
+    def shifted(part, by):
+        return lax.ppermute(part, planes, [(i, (i + by) % Z) for i in range(Z)])
+
+    middle = own.shape[0] // 2
+    blocks = (
+        own,
+        shifted(own, -1),
+        shifted(own, 1),
+        shifted(own[:middle], 2),
+        shifted(own[middle:], -2),
+    )
 
     gate_half = lax.optimization_barrier(gate_weights.astype(BF16)).astype(F32)
     flat_acts = hidden_acts.reshape(routed, hidden).astype(F32)
@@ -149,23 +184,36 @@
     send_acts = jnp.dot(placement, gated, preferred_element_type=F32).astype(BF16)
     acts_in = lax.all_to_all(
         send_acts.reshape(experts, MOST, hidden),
-        ("x", "z"),
+        ("x",) + planes,
         split_axis=0,
         concat_axis=0,
         tiled=True,
     ).reshape(slot_count, hidden)
 
+    slot = jnp.arange(slot_count, dtype=jnp.int32)
+    per_x = Z * MOST
+    held, high, rank = slot // (ZH * MOST) % ZL, slot // MOST % ZH, slot % MOST
+    turn = jnp.where(held == 1, 1, jnp.where(held == 2, ZL - 1, jnp.where(held == 3, 2, 0)))
+    source = high * ZL + (z_at + turn) % ZL
+    home_slot = slot // per_x * per_x + source * MOST + rank
+    order = (slot[:, None] == home_slot[None, :]).astype(BF16)
+
     line = jnp.arange(hidden, dtype=jnp.int32)
     piece = hidden // (Y * CORES)
     unit = ((line % half) // piece * CORES + line // half) * piece + line % piece
     reorder = (unit[:, None] == line[None, :]).astype(BF16)
+    acts_rows = lax.dot_general(
+        order, acts_in, (((0,), (0,)), ((), ())), preferred_element_type=F32
+    ).astype(BF16)
     left = lax.dot_general(
-        reorder, acts_in, (((1,), (1,)), ((), ())), preferred_element_type=F32
+        reorder, acts_rows, (((1,), (1,)), ((), ())), preferred_element_type=F32
     ).astype(BF16)
     left_own = lax.dynamic_slice_in_dim(left, core * half, half, 0)
     left_away = lax.dynamic_slice_in_dim(left, (1 - core) * half, half, 0)
 
-    picked = pick_rows(pick, column, acts_in)
+    home = (held * ZH + high) * tok_rows + z_at
+    lane = slot // per_x * MOST + rank
+    picked = pick_rows(home[:, None], lane[:, None], blocks, width, acts_in)
     rows = lax.all_to_all(
         picked.reshape(X, Z * MOST, width), "x", split_axis=0, concat_axis=0, tiled=True
     ).reshape(slot_count, width)
@@ -176,10 +224,10 @@
     part = weight_term(left_own, left_pair, rows, rows_pair)
     summed = lax.psum_scatter(part, "y", scatter_dimension=0, tiled=True)
 
-    grad_hidden = hidden_term(rows, down_weight)
+    grad_hidden = hidden_term(rows, down_weight, order)
     back = lax.all_to_all(
         grad_hidden.reshape(experts, MOST, hidden),
-        ("x", "z"),
+        ("x",) + planes,
         split_axis=0,
         concat_axis=0,
         tiled=True,
@@ -195,8 +243,9 @@
 
 
 def solution(mesh):
-    dims = Mesh(mesh.devices.reshape(Y, CORES, X, Z), ("y", "core", "x", "z"))
-    tokens = ("y", "core", "x", "z")
+    dims = Mesh(mesh.devices.reshape(Y, CORES, X, ZH, ZL), ("y", "core", "x", "zh", "zl"))
+    experts = ("x", "zh", "zl")
+    tokens = ("y", "core") + experts
     return jax.shard_map(
         shards,
         mesh=dims,
@@ -205,12 +254,12 @@
             P(tokens, None, None),
             P(tokens, None),
             P(tokens, None),
-            P(("x", "z"), None, None),
+            P(experts, None, None),
         ),
         out_specs=(
             P(tokens, None, None),
             P(tokens, None),
-            P(("x", "z"), ("y", "core"), None),
+            P(experts, ("y", "core"), None),
         ),
         check_vma=False,
     )

time: 194 us -> 198 us (1.021)
  waiting for transfers between devices: 110 us -> 70.3 us
  blocking collectives: 0 us -> 37.1 us
  starting transfers between devices: 44.9 us -> 52.9 us
    all_gather x0 -> x1, blocking collectives: none -> 37.1 us  [shards(): lax.all_gather(jnp.concatenate([out_grad, table], axis=1), 'zh', axis=0,...]
    all_gather x1 -> x0, waiting for transfers between devices: 26.6 us -> none  [shards(): column = lax.all_gather(out_grad, 'z', axis=0, tiled=True)]
    all_to_all x3 -> x2, waiting for transfers between devices: 65.8 us -> 44.2 us  [the longest x1 26.4 us: shards(): lax.all_to_all(grad_hidden.reshape(experts, MOST, hidden), ('x',) + plane...]
    ppermute x0 -> x4, starting transfers between devices: none -> 19.2 us  [shifted(): return lax.ppermute(part, planes, [(i, (i + by) % Z) for i in range(Z)])]
    all_to_all x3 -> x2, starting transfers between devices: 35.3 us -> 24.8 us  [the longest x1 13.7 us: shards(): lax.all_to_all(grad_hidden.reshape(experts, MOST, hidden), ('x',) + plane...]
    all_to_all x1, waiting for transfers between devices: 11.5 us -> 16.9 us  [shards(): lax.all_to_all(picked.reshape(X, Z * MOST, width), 'x', split_axis=0, con...]
    ppermute x0 -> x4, waiting for transfers between devices: none -> 3.28 us  [shifted(): return lax.ppermute(part, planes, [(i, (i + by) % Z) for i in range(Z)])]
  transfers between devices with their start and end apart: 8 -> 10, of which waited for: 7 -> 7; matrix products, arithmetic and copies ran while one was open for 5% -> 4% of each run, Pallas kernels for 3% -> 3%
where the time goes in v4:
time: 198 us
  waiting for transfers between devices  70.3 us (36%)
  starting transfers between devices  52.9 us (27%)
  blocking collectives  37.1 us (19%)
  between operations  14.2 us (7%)
  Pallas kernels  12.7 us (6%)
  local copies, waits for them, and re-layouts  4.92 us (2%)
  matrix products  3.43 us (2%)
  other arithmetic  2.04 us (1%)
    all_gather x1, blocking collectives, shards(): lax.all_gather(jnp.concatenate([out_grad, table], axis=1), 'zh', axis=0,...  37.1 us
    all_to_all x1, waiting for transfers between devices, shards(): lax.all_to_all(grad_hidden.reshape(experts, MOST, hidden), ('x',) + plane...  26.4 us
    ppermute x4, starting transfers between devices, shifted(): return lax.ppermute(part, planes, [(i, (i + by) % Z) for i in range(Z)])  19.2 us
    all_to_all x1, waiting for transfers between devices, shards(): lax.all_to_all(send_acts.reshape(experts, MOST, hidden), ('x',) + planes,...  17.7 us
    all_to_all x1, waiting for transfers between devices, shards(): lax.all_to_all(picked.reshape(X, Z * MOST, width), 'x', split_axis=0, con...  16.9 us
    all_to_all x1, starting transfers between devices, shards(): lax.all_to_all(grad_hidden.reshape(experts, MOST, hidden), ('x',) + plane...  13.7 us
    all_to_all x1, starting transfers between devices, shards(): lax.all_to_all(send_acts.reshape(experts, MOST, hidden), ('x',) + planes,...  11 us
    pallas_call x1, Pallas kernels, hidden_term(): pl.pallas_call(hidden_kernel, grid=(width // BLOCK,), out_shape=jax.Shape...  5.38 us
  transfers between devices with their start and end apart: 10, of which 7 were waited for; matrix products, arithmetic and copies ran while one was open for 4% of the time, Pallas kernels for 3%

profile of v4, /device:TPU:6, one launch (start us, length us, event | category | flops | bytes accessed | tf_op | source)
XLA Modules:
  0.0 197.6 jit_solution(16261558098164480327)
XLA Ops:
  7.2 0.8 copy.15
  7.9 0.1 reshape.415
  8.0 0.2 fusion.3
  8.2 0.2 convolution_convert_fusion.2
  8.4 0.9 pad_maximum_fusion
  9.3 37.1 %all_gather.3.refs_0_.refs_5_ = bf16[64,4224]{1,0:T(8,128)(2,1)S(1)} all-gather(bf16[16,4224]{1,0:T(8,128)(2,1)S(1)} %pad_maximum_fusion), channel_id=1, replica_groups=mesh['y'=8,'core'=2,'x'=4,'zh'=4,'zl'=4] {'zh'}, dimensions={0}, use_global_device_ids=true | all-gather | bytes 675840 | tf_op jit(solution)/shard_map/all_gather | solution.py:167
  46.4 9.3 %collective-permute-start = (bf16[64,4224]{1,0:T(8,128)(2,1)S(1)}, bf16[64,4224]{1,0:T(8,128)(2,1)S(1)}, u32[]{:S(2)}, u32[]{:S(2)}) collective-permute-start(bf16[64,4224]{1,0:T(8,128)(2,1)S(1)} %all_gather.3.refs_0_.refs_5_), channel_id=1, source_target_pairs={{0,15},{1,0},{2,1},{3,2},{4,3},{5,4},{6,5},{7,6},{8,7},{9,8},{10,9... | collective-permute-start | bytes 1622024 | tf_op jit(solution)/shard_map/ppermute | solution.py:170
  55.7 1.9 collective-permute-start.1
  57.7 0.7 convert_element_type.74
  58.3 0.1 copy.14
  58.4 0.1 reshape.423
  58.5 1.2 convolution_convert_fusion.1
  59.7 0.9 reshape.416
  60.6 11.0 %all-to-all-start = ((bf16[64,3,768]{2,1,0:T(4,128)(2,1)}), bf16[64,3,768]{2,1,0:T(4,128)(2,1)S(1)}, u32[]{:S(2)}, u32[]{:S(2)}) async-start(bf16[64,3,768]{2,1,0:T(4,128)(2,1)} %reshape.416), calls=%async_computation | async-start | bytes 786432 | tf_op jit(solution)/shard_map/all_to_all | solution.py:185
  71.7 0.8 fusion.78
  72.4 4.3 %collective-permute-start.2 = (bf16[32,4224]{1,0:T(8,128)(2,1)}, bf16[32,4224]{1,0:T(8,128)(2,1)S(1)}, u32[]{:S(2)}, u32[]{:S(2)}) collective-permute-start(bf16[32,4224]{1,0:T(8,128)(2,1)} %get-tuple-element.16), channel_id=1, source_target_pairs={{0,2},{1,3},{2,4},{3,5},{4,6},{5,7},{6,8},{7,9},{8,10},{9,11},{10,... | collective-permute-start | bytes 811016 | tf_op jit(solution)/shard_map/ppermute | solution.py:170
  76.7 3.7 %collective-permute-start.3 = (bf16[32,4224]{1,0:T(8,128)(2,1)S(1)}, bf16[32,4224]{1,0:T(8,128)(2,1)S(1)}, u32[]{:S(2)}, u32[]{:S(2)}) collective-permute-start(bf16[32,4224]{1,0:T(8,128)(2,1)S(1)} %get-tuple-element.15), channel_id=1, source_target_pairs={{0,14},{1,15},{2,0},{3,1},{4,2},{5,3},{6,4},{7,5},{8,6},{9,7},{10,... | collective-permute-start | bytes 811016 | tf_op jit(solution)/shard_map/ppermute | solution.py:170
  80.4 0.1 fusion.18
  80.5 17.7 %all-to-all-done = bf16[64,3,768]{2,1,0:T(4,128)(2,1)S(1)} async-done(((bf16[64,3,768]{2,1,0:T(4,128)(2,1)}), bf16[64,3,768]{2,1,0:T(4,128)(2,1)S(1)}, u32[]{:S(2)}, u32[]{:S(2)}) %all-to-all-start) | async-done | bytes 294944 | tf_op jit(solution)/shard_map/all_to_all | solution.py:185
  98.3 0.2 reshape.417.refs_10_
  98.5 1.9 collective-permute-done.2.refs_3_.refs_8_
  100.4 1.4 collective-permute-done.3.refs_4_.refs_9_
  101.8 0.0 collective-permute-done.refs_1_.refs_6_
  101.8 0.0 collective-permute-done.1.refs_2_.refs_7_
  101.8 3.6 %pick_rows.1 = bf16[192,4096]{1,0:T(8,128)(2,1)} custom-call(s32[192,1]{1,0:T(8,128)S(1)} %get-tuple-element.26.home, s32[192,1]{1,0:T(8,128)S(1)} %get-tuple-element.25.lane, bf16[64,4224]{1,0:T(8,128)(2,1)S(1)} %all_gather.3.refs_0_.refs_5_, bf16[64,4224]{1,0:T(8,128)(2,1)S(1)} %collective-permute-done.refs_1_.refs_6_, ...), custom_call_target="tpu_custom_call" | custom-call | flops 402653184 | bytes 3670016 | tf_op jit(solution)/shard_map/pick_rows/pallas_call | solution.py:46
  105.4 4.7 %all-to-all-start.1 = ((bf16[4,48,4096]{2,1,0:T(8,128)(2,1)}), bf16[4,48,4096]{2,1,0:T(8,128)(2,1)S(1)}, u32[]{:S(2)}, u32[]{:S(2)}) async-start(bf16[4,48,4096]{2,1,0:T(8,128)(2,1)} %bitcast.1), calls=%async_computation.1 | async-start | bytes 3145728 | tf_op jit(solution)/shard_map/all_to_all | solution.py:217
  110.1 0.8 fusion.1
  111.0 16.9 %all-to-all-done.1 = bf16[4,48,4096]{2,1,0:T(8,128)(2,1)S(1)} async-done(((bf16[4,48,4096]{2,1,0:T(8,128)(2,1)}), bf16[4,48,4096]{2,1,0:T(8,128)(2,1)S(1)}, u32[]{:S(2)}, u32[]{:S(2)}) %all-to-all-start.1) | async-done | bytes 1572896 | tf_op jit(solution)/shard_map/all_to_all | solution.py:217
  127.9 1.9 collective-permute-start.5
  129.8 2.4 %collective-permute-start.4 = (bf16[384,192]{1,0:T(8,128)(2,1)S(1)}, bf16[384,192]{1,0:T(8,128)(2,1)S(1)}, u32[]{:S(2)}, u32[]{:S(2)}) collective-permute-start(bf16[384,192]{1,0:T(8,128)(2,1)S(1)} %get-tuple-element.8), channel_id=1, source_target_pairs={{0,64},{64,0},{1,65},{65,1},{2,66},{66,2},{3,67},{67,3},{4,68},{68... | collective-permute-start | bytes 442376 | tf_op jit(solution)/shard_map/ppermute | solution.py:221
  132.2 1.2 collective-permute-done.4.left_pair
  133.5 0.0 collective-permute-done.5.rows_pair
  133.5 3.7 %weight_term.1 = bf16[384,4096]{1,0:T(8,128)(2,1)} custom-call(bf16[384,192]{1,0:T(8,128)(2,1)S(1)} %get-tuple-element.7.left_own, bf16[384,192]{1,0:T(8,128)(2,1)S(1)} %collective-permute-done.4.left_pair, bf16[192,4096]{1,0:T(8,128)(2,1)S(1)} %bitcast.15, bf16[192,4096]{1,0:T(8,128)(2,1)S(1)} %collective-permute-done.5.rows_pair), custom_call_target="tpu_custom_call" | custom-call | flops 1207959552 | bytes 6586368 | tf_op jit(solution)/shard_map/weight_term/pallas_call | solution.py:75
  137.2 0.0 reduce-scatter.2.cloned.1.call-update
  137.3 0.0 copy-start.1
  137.3 0.0 copy-start
  137.3 5.4 %hidden_term.1 = bf16[192,768]{1,0:T(8,128)(2,1)S(1)} custom-call(bf16[192,4096]{1,0:T(8,128)(2,1)S(1)} %bitcast.16, bf16[1,768,4096]{2,1,0:T(8,128)(2,1)} %weight.1, bf16[192,192]{1,0:T(8,128)(2,1)S(1)} %fusion.13.order), custom_call_target="tpu_custom_call" | custom-call | flops 1207959552 | bytes 8159232 | tf_op jit(solution)/shard_map/hidden_term/pallas_call | solution.py:116
  142.7 0.9 reshape.420
  143.6 13.7 %all-to-all-start.2 = ((bf16[64,3,768]{2,1,0:T(4,128)(2,1)}), bf16[64,3,768]{2,1,0:T(4,128)(2,1)S(1)}, u32[]{:S(2)}, u32[]{:S(2)}) async-start(bf16[64,3,768]{2,1,0:T(4,128)(2,1)} %reshape.420), calls=%async_computation.2 | async-start | bytes 786432 | tf_op jit(solution)/shard_map/all_to_all | solution.py:228
  157.3 0.1 copy.18
  157.4 26.4 %all-to-all-done.2 = bf16[64,3,768]{2,1,0:T(4,128)(2,1)S(1)} async-done(((bf16[64,3,768]{2,1,0:T(4,128)(2,1)}), bf16[64,3,768]{2,1,0:T(4,128)(2,1)S(1)}, u32[]{:S(2)}, u32[]{:S(2)}) %all-to-all-start.2) | async-done | bytes 294944 | tf_op jit(solution)/shard_map/all_to_all | solution.py:228
  183.8 0.2 reshape.421
  184.1 1.0 fusion.5
  185.1 0.1 reshape.425
  185.2 0.1 multiply_reduce_fusion
  185.3 0.1 subtract_multiply_fusion
  185.4 0.7 copy.19
  186.1 4.7 %reduce-scatter.2.cloned.1.call-done = bf16[48,4096]{1,0:T(8,128)(2,1)} async-done(((bf16[384,4096]{1,0:T(8,128)(2,1)}), bf16[48,4096]{1,0:T(8,128)(2,1)}) %reduce-scatter.2.cloned.1.call-update) | async-done | bytes 393232 | tf_op jit(solution)/shard_map/reduce_scatter | solution.py:225
  (8 shorter events, 0.1 us)
Async XLA Ops:
  46.4 55.4 %collective-permute-start = (bf16[64,4224]{1,0:T(8,128)(2,1)S(1)}, bf16[64,4224]{1,0:T(8,128)(2,1)S(1)}, u32[]{:S(2)}, u32[]{:S(2)}) collective-permute-start(bf16[64,4224]{1,0:T(8,128)(2,1)S(1)} %all_gather.3.refs_0_.refs_5_), channel_id=1, source_target_pairs={{0,15},{1,0},{2,1},{3,2},{4,3},{5,4},{6,5},{7,6},{8,7},{9,8},{10,9... | collective-permute-start | bytes 1622024 | tf_op jit(solution)/shard_map/ppermute | solution.py:170
  55.7 46.1 %collective-permute-start.1 = (bf16[64,4224]{1,0:T(8,128)(2,1)S(1)}, bf16[64,4224]{1,0:T(8,128)(2,1)S(1)}, u32[]{:S(2)}, u32[]{:S(2)}) collective-permute-start(bf16[64,4224]{1,0:T(8,128)(2,1)S(1)} %all_gather.3.refs_0_.refs_5_), channel_id=1, source_target_pairs={{0,1},{1,2},{2,3},{3,4},{4,5},{5,6},{6,7},{7,8},{8,9},{9,10},{10,1... | collective-permute-start | bytes 1622024 | tf_op jit(solution)/shard_map/ppermute | solution.py:170
  60.6 37.6 %all-to-all-start = ((bf16[64,3,768]{2,1,0:T(4,128)(2,1)}), bf16[64,3,768]{2,1,0:T(4,128)(2,1)S(1)}, u32[]{:S(2)}, u32[]{:S(2)}) async-start(bf16[64,3,768]{2,1,0:T(4,128)(2,1)} %reshape.416), calls=%async_computation | async-start | bytes 786432 | tf_op jit(solution)/shard_map/all_to_all | solution.py:185
  72.4 28.0 %collective-permute-start.2 = (bf16[32,4224]{1,0:T(8,128)(2,1)}, bf16[32,4224]{1,0:T(8,128)(2,1)S(1)}, u32[]{:S(2)}, u32[]{:S(2)}) collective-permute-start(bf16[32,4224]{1,0:T(8,128)(2,1)} %get-tuple-element.16), channel_id=1, source_target_pairs={{0,2},{1,3},{2,4},{3,5},{4,6},{5,7},{6,8},{7,9},{8,10},{9,11},{10,... | collective-permute-start | bytes 811016 | tf_op jit(solution)/shard_map/ppermute | solution.py:170
  76.7 25.1 %collective-permute-start.3 = (bf16[32,4224]{1,0:T(8,128)(2,1)S(1)}, bf16[32,4224]{1,0:T(8,128)(2,1)S(1)}, u32[]{:S(2)}, u32[]{:S(2)}) collective-permute-start(bf16[32,4224]{1,0:T(8,128)(2,1)S(1)} %get-tuple-element.15), channel_id=1, source_target_pairs={{0,14},{1,15},{2,0},{3,1},{4,2},{5,3},{6,4},{7,5},{8,6},{9,7},{10,... | collective-permute-start | bytes 811016 | tf_op jit(solution)/shard_map/ppermute | solution.py:170
  105.4 22.5 %all-to-all-start.1 = ((bf16[4,48,4096]{2,1,0:T(8,128)(2,1)}), bf16[4,48,4096]{2,1,0:T(8,128)(2,1)S(1)}, u32[]{:S(2)}, u32[]{:S(2)}) async-start(bf16[4,48,4096]{2,1,0:T(8,128)(2,1)} %bitcast.1), calls=%async_computation.1 | async-start | bytes 3145728 | tf_op jit(solution)/shard_map/all_to_all | solution.py:217
  110.1 80.7 %reduce-scatter.2.cloned.1.call-start = ((), (), s32[]{:S(2)}) async-start(), calls=%async_computation.4 | async-start | bytes 3538944 | tf_op jit(solution)/shard_map/reduce_scatter | solution.py:225
  127.9 5.6 %collective-permute-start.5 = (bf16[192,4096]{1,0:T(8,128)(2,1)S(1)}, bf16[192,4096]{1,0:T(8,128)(2,1)S(1)}, u32[]{:S(2)}, u32[]{:S(2)}) collective-permute-start(bf16[192,4096]{1,0:T(8,128)(2,1)S(1)} %bitcast.14), channel_id=1, source_target_pairs={{0,64},{64,0},{1,65},{65,1},{2,66},{66,2},{3,67},{67,3},{4,68},{68... | collective-permute-start | bytes 4718600 | tf_op jit(solution)/shard_map/ppermute | solution.py:222
  129.8 3.7 %collective-permute-start.4 = (bf16[384,192]{1,0:T(8,128)(2,1)S(1)}, bf16[384,192]{1,0:T(8,128)(2,1)S(1)}, u32[]{:S(2)}, u32[]{:S(2)}) collective-permute-start(bf16[384,192]{1,0:T(8,128)(2,1)S(1)} %get-tuple-element.8), channel_id=1, source_target_pairs={{0,64},{64,0},{1,65},{65,1},{2,66},{66,2},{3,67},{67,3},{4,68},{68... | collective-permute-start | bytes 442376 | tf_op jit(solution)/shard_map/ppermute | solution.py:221
  137.3 20.0 %copy-start.1 = (f32[16,8]{0,1:T(8,128)S(1)}, f32[16,8]{0,1:T(8,128)}, u32[]{:S(2)}) copy-start(f32[16,8]{0,1:T(8,128)} %param.7) | copy-start | bytes 1540
  137.3 46.8 %copy-start = (bf16[16,8,768]{2,1,0:T(8,128)(2,1)S(1)}, bf16[16,8,768]{2,1,0:T(8,128)(2,1)}, u32[]{:S(2)}) copy-start(bf16[16,8,768]{2,1,0:T(8,128)(2,1)} %param.6) | copy-start | bytes 589828
  143.6 40.3 %all-to-all-start.2 = ((bf16[64,3,768]{2,1,0:T(4,128)(2,1)}), bf16[64,3,768]{2,1,0:T(4,128)(2,1)S(1)}, u32[]{:S(2)}, u32[]{:S(2)}) async-start(bf16[64,3,768]{2,1,0:T(4,128)(2,1)} %reshape.420), calls=%async_computation.2 | async-start | bytes 786432 | tf_op jit(solution)/shard_map/all_to_all | solution.py:228
Sparse Core Ops, SparseCore 0:
  137.3 53.3 reduce-scatter.1

commit v5 on v4

--- a/solution.py
+++ b/solution.py
@@ -19,8 +19,7 @@
 
 
 def pick_kernel(home, lane, *refs):
-    blocks, tables, (after, out, pick) = refs[:5], refs[5:10], refs[10:]
-    del after
+    blocks, tables, outs, pick = refs[:5], refs[5:10], refs[10:-1], refs[-1]
     slots, tokens = pick.shape
 
     @pl.when(pl.program_id(0) == 0)
@@ -36,22 +35,24 @@
         pick[...] = jnp.where(at == token, 1.0, 0.0).astype(pick.dtype)
 
     held = jnp.concatenate([ref[...] for ref in blocks], axis=0)
-    out[...] = jnp.dot(pick[...], held, preferred_element_type=F32).astype(out.dtype)
-
-
-def pick_rows(home, lane, blocks, width, after):
+    rows = jnp.dot(pick[...], held, preferred_element_type=F32).astype(BF16)
+    share = rows.shape[0] // len(outs)
+    for number, out in enumerate(outs):
+        out[...] = rows[number * share : (number + 1) * share]
+
+
+def pick_rows(home, lane, blocks, width):
     slots = home.shape[0]
     tokens = sum(block.shape[0] for block in blocks)
     last = width // LANES
     return pl.pallas_call(
         pick_kernel,
         grid=(width // BLOCK,),
-        out_shape=jax.ShapeDtypeStruct((slots, width), BF16),
+        out_shape=[jax.ShapeDtypeStruct((slots // X, width), BF16)] * X,
         in_specs=[pl.BlockSpec((slots, 1), lambda i: (0, 0))] * 2
         + [pl.BlockSpec((block.shape[0], BLOCK), lambda i: (0, i)) for block in blocks]
-        + [pl.BlockSpec((block.shape[0], LANES), lambda i: (0, last)) for block in blocks]
-        + [pl.BlockSpec(memory_space=pl.ANY)],
-        out_specs=pl.BlockSpec((slots, BLOCK), lambda i: (0, i)),
+        + [pl.BlockSpec((block.shape[0], LANES), lambda i: (0, last)) for block in blocks],
+        out_specs=[pl.BlockSpec((slots // X, BLOCK), lambda i: (0, i))] * X,
         scratch_shapes=[pltpu.VMEM((slots, tokens), BF16)],
         compiler_params=pltpu.CompilerParams(vmem_limit_bytes=49 * MIB),
         cost_estimate=pl.CostEstimate(
@@ -60,28 +61,29 @@
             transcendentals=0,
         ),
         name="pick_rows",
-    )(home, lane, *blocks, *blocks, after)
-
-
-def weight_kernel(left_own, left_pair, rows_own, rows_pair, out):
-    total = jnp.dot(left_own[...], rows_own[...], preferred_element_type=F32)
-    total = total + jnp.dot(left_pair[...], rows_pair[...], preferred_element_type=F32)
+    )(home, lane, *blocks, *blocks)
+
+
+def joined(refs):
+    return jnp.concatenate([ref[...] for ref in refs], axis=0)
+
+
+def weight_kernel(left_own, left_pair, *refs):
+    own, pair, out = refs[:X], refs[X : 2 * X], refs[2 * X]
+    total = jnp.dot(left_own[...], joined(own), preferred_element_type=F32)
+    total = total + jnp.dot(left_pair[...], joined(pair), preferred_element_type=F32)
     out[...] = total.astype(out.dtype)
 
 
 def weight_term(left_own, left_pair, rows_own, rows_pair):
     half, slots = left_own.shape
-    width = rows_own.shape[1]
+    share, width = rows_own[0].shape
     return pl.pallas_call(
         weight_kernel,
         grid=(width // BLOCK,),
         out_shape=jax.ShapeDtypeStruct((half, width), BF16),
-        in_specs=[
-            pl.BlockSpec((half, slots), lambda i: (0, 0)),
-            pl.BlockSpec((half, slots), lambda i: (0, 0)),
-            pl.BlockSpec((slots, BLOCK), lambda i: (0, i)),
-            pl.BlockSpec((slots, BLOCK), lambda i: (0, i)),
-        ],
+        in_specs=[pl.BlockSpec((half, slots), lambda i: (0, 0))] * 2
+        + [pl.BlockSpec((share, BLOCK), lambda i: (0, i))] * (2 * X),
         out_specs=pl.BlockSpec((half, BLOCK), lambda i: (0, i)),
         compiler_params=pltpu.CompilerParams(vmem_limit_bytes=49 * MIB),
         cost_estimate=pl.CostEstimate(
@@ -90,10 +92,11 @@
             transcendentals=0,
         ),
         name="weight_term",
-    )(left_own, left_pair, rows_own, rows_pair)
-
-
-def hidden_kernel(rows, weight, order, out, total):
+    )(left_own, left_pair, *rows_own, *rows_pair)
+
+
+def hidden_kernel(weight, order, *refs):
+    rows, (out, total) = refs[:X], refs[X:]
     step = pl.program_id(0)
 
     @pl.when(step == 0)
@@ -101,7 +104,7 @@
         total[...] = jnp.zeros_like(total)
 
     total[...] += lax.dot_general(
-        rows[...], weight[...], (((1,), (1,)), ((), ())), preferred_element_type=F32
+        joined(rows), weight[...], (((1,), (1,)), ((), ())), preferred_element_type=F32
     )
 
     @pl.when(step == pl.num_programs(0) - 1)
@@ -111,17 +114,17 @@
 
 
 def hidden_term(rows, weight, order):
-    slots = rows.shape[0]
+    slots = order.shape[0]
     hidden, width = weight.shape[1:]
     return pl.pallas_call(
         hidden_kernel,
         grid=(width // BLOCK,),
         out_shape=jax.ShapeDtypeStruct((slots, hidden), BF16),
         in_specs=[
-            pl.BlockSpec((slots, BLOCK), lambda i: (0, i)),
             pl.BlockSpec((None, hidden, BLOCK), lambda i: (0, 0, i)),
             pl.BlockSpec((slots, slots), lambda i: (0, 0)),
-        ],
+        ]
+        + [pl.BlockSpec((slots // X, BLOCK), lambda i: (0, i))] * X,
         out_specs=pl.BlockSpec((slots, hidden), lambda i: (0, 0)),
         scratch_shapes=[pltpu.VMEM((slots, hidden), F32)],
         compiler_params=pltpu.CompilerParams(vmem_limit_bytes=49 * MIB),
@@ -131,7 +134,7 @@
             transcendentals=0,
         ),
         name="hidden_term",
-    )(rows, weight, order)
+    )(weight, order, *rows)
 
 
 def shards(out_grad, hidden_acts, gate_weights, expert_idx, down_weight):
@@ -144,6 +147,7 @@
     slot_count = experts * MOST
     core = lax.axis_index("core")
     planes = ("zh", "zl")
+    x_at = lax.axis_index("x")
     z_at = lax.axis_index(planes)
     swap = [(0, 1), (1, 0)]
 
@@ -182,6 +186,7 @@
     flat_acts = hidden_acts.reshape(routed, hidden).astype(F32)
     gated = (gate_half.reshape(routed, 1) * flat_acts).astype(BF16)
     send_acts = jnp.dot(placement, gated, preferred_element_type=F32).astype(BF16)
+    send_acts, _ = lax.optimization_barrier((send_acts, blocks[1:]))
     acts_in = lax.all_to_all(
         send_acts.reshape(experts, MOST, hidden),
         ("x",) + planes,
@@ -195,7 +200,8 @@
     held, high, rank = slot // (ZH * MOST) % ZL, slot // MOST % ZH, slot % MOST
     turn = jnp.where(held == 1, 1, jnp.where(held == 2, ZL - 1, jnp.where(held == 3, 2, 0)))
     source = high * ZL + (z_at + turn) % ZL
-    home_slot = slot // per_x * per_x + source * MOST + rank
+    steps = slot // per_x
+    home_slot = (x_at + X - steps) % X * per_x + source * MOST + rank
     order = (slot[:, None] == home_slot[None, :]).astype(BF16)
 
     line = jnp.arange(hidden, dtype=jnp.int32)
@@ -212,14 +218,13 @@
     left_away = lax.dynamic_slice_in_dim(left, (1 - core) * half, half, 0)
 
     home = (held * ZH + high) * tok_rows + z_at
-    lane = slot // per_x * MOST + rank
-    picked = pick_rows(home[:, None], lane[:, None], blocks, width, acts_in)
-    rows = lax.all_to_all(
-        picked.reshape(X, Z * MOST, width), "x", split_axis=0, concat_axis=0, tiled=True
-    ).reshape(slot_count, width)
-    rows, left_own, left_away = lax.optimization_barrier((rows, left_own, left_away))
+    lane = (x_at + steps) % X * MOST + rank
+    picked = pick_rows(home[:, None], lane[:, None], blocks, width)
+    rows = [picked[0]] + [
+        lax.ppermute(picked[by], "x", [(i, (i + by) % X) for i in range(X)]) for by in range(1, X)
+    ]
+    rows_pair = [lax.ppermute(part, "core", swap) for part in rows]
     left_pair = lax.ppermute(left_away, "core", swap)
-    rows_pair = lax.ppermute(rows, "core", swap)
 
     part = weight_term(left_own, left_pair, rows, rows_pair)
     summed = lax.psum_scatter(part, "y", scatter_dimension=0, tiled=True)

time: 198 us -> 199 us (level)
  waiting for transfers between devices: 70.3 us -> 56.7 us
  starting transfers between devices: 52.9 us -> 65.9 us
    all_to_all x1, waiting for transfers between devices: 17.7 us -> 0.01 us  [shards(): lax.all_to_all(send_acts.reshape(experts, MOST, hidden), ('x',) + planes,...]
    all_to_all x1 -> x0, waiting for transfers between devices: 16.9 us -> none  [shards(): lax.all_to_all(picked.reshape(X, Z * MOST, width), 'x', split_axis=0, con...]
    ppermute x1 -> x7, starting transfers between devices: 1.91 us -> 18.4 us  [the longest x3 10.2 us: shards(): lax.ppermute(picked[by], 'x', [(i, (i + by) % X) for i in range(X)])]
    ppermute x4, waiting for transfers between devices: 3.28 us -> 14.8 us  [shifted(): return lax.ppermute(part, planes, [(i, (i + by) % Z) for i in range(Z)])]
    ppermute x1 -> x7, waiting for transfers between devices: 0.01 us -> 9.36 us  [the longest x3 9.35 us: shards(): lax.ppermute(picked[by], 'x', [(i, (i + by) % X) for i in range(X)])]
    all_to_all x1 -> x0, starting transfers between devices: 4.69 us -> none  [shards(): lax.all_to_all(picked.reshape(X, Z * MOST, width), 'x', split_axis=0, con...]
  transfers between devices with their start and end apart: 10 -> 15, of which waited for: 7 -> 6; matrix products, arithmetic and copies ran while one was open for 4% -> 4% of each run, Pallas kernels for 3% -> 4%
where the time goes in v5:
time: 199 us; the launch traced here: 198 us
  starting transfers between devices  65.9 us (33%)
  waiting for transfers between devices  56.7 us (28%)
  blocking collectives  37.1 us (19%)
  between operations  14.3 us (7%)
  Pallas kernels  13.6 us (7%)
  local copies, waits for them, and re-layouts  5.21 us (3%)
  matrix products  3.43 us (2%)
  other arithmetic  2.08 us (1%)
    all_gather x1, blocking collectives, shards(): lax.all_gather(jnp.concatenate([out_grad, table], axis=1), 'zh', axis=0,...  37.1 us
    all_to_all x1, waiting for transfers between devices, shards(): lax.all_to_all(grad_hidden.reshape(experts, MOST, hidden), ('x',) + plane...  26.4 us
    ppermute x4, starting transfers between devices, shifted(): return lax.ppermute(part, planes, [(i, (i + by) % Z) for i in range(Z)])  19.2 us
    ppermute x4, waiting for transfers between devices, shifted(): return lax.ppermute(part, planes, [(i, (i + by) % Z) for i in range(Z)])  14.8 us
    all_to_all x1, starting transfers between devices, shards(): lax.all_to_all(grad_hidden.reshape(experts, MOST, hidden), ('x',) + plane...  14.3 us
    all_to_all x1, starting transfers between devices, shards(): lax.all_to_all(send_acts.reshape(experts, MOST, hidden), ('x',) + planes,...  12.1 us
    ppermute x3, starting transfers between devices, shards(): lax.ppermute(picked[by], 'x', [(i, (i + by) % X) for i in range(X)])  10.2 us
    ppermute x3, waiting for transfers between devices, shards(): lax.ppermute(picked[by], 'x', [(i, (i + by) % X) for i in range(X)])  9.35 us
  transfers between devices with their start and end apart: 15, of which 6 were waited for; matrix products, arithmetic and copies ran while one was open for 4% of the time, Pallas kernels for 4%

profile of v5, /device:TPU:6, one launch (start us, length us, event | category | flops | bytes accessed | tf_op | source)
XLA Modules:
  0.0 198.4 jit_solution(7321179253018192572)
XLA Ops:
  7.2 0.8 copy.15
  7.9 0.1 reshape.457
  8.0 0.2 fusion.3
  8.2 0.2 convolution_convert_fusion.2
  8.4 0.9 pad_maximum_fusion
  9.3 37.1 %all_gather.3.refs_0_.refs_5_ = bf16[64,4224]{1,0:T(8,128)(2,1)S(1)} all-gather(bf16[16,4224]{1,0:T(8,128)(2,1)S(1)} %pad_maximum_fusion), channel_id=1, replica_groups=mesh['y'=8,'core'=2,'x'=4,'zh'=4,'zl'=4] {'zh'}, dimensions={0}, use_global_device_ids=true | all-gather | bytes 675840 | tf_op jit(solution)/shard_map/all_gather | solution.py:171
  46.4 9.3 %collective-permute-start = (bf16[64,4224]{1,0:T(8,128)(2,1)S(1)}, bf16[64,4224]{1,0:T(8,128)(2,1)S(1)}, u32[]{:S(2)}, u32[]{:S(2)}) collective-permute-start(bf16[64,4224]{1,0:T(8,128)(2,1)S(1)} %all_gather.3.refs_0_.refs_5_), channel_id=1, source_target_pairs={{0,15},{1,0},{2,1},{3,2},{4,3},{5,4},{6,5},{7,6},{8,7},{9,8},{10,9... | collective-permute-start | bytes 1622024 | tf_op jit(solution)/shard_map/ppermute | solution.py:174
  55.7 1.9 collective-permute-start.1
  57.7 1.9 collective-permute-start.2
  59.6 6.0 %collective-permute-start.3 = (bf16[32,4224]{1,0:T(8,128)(2,1)S(1)}, bf16[32,4224]{1,0:T(8,128)(2,1)S(1)}, u32[]{:S(2)}, u32[]{:S(2)}) collective-permute-start(bf16[32,4224]{1,0:T(8,128)(2,1)S(1)} %get-tuple-element.19), channel_id=1, source_target_pairs={{0,14},{1,15},{2,0},{3,1},{4,2},{5,3},{6,4},{7,5},{8,6},{9,7},{10,... | collective-permute-start | bytes 811016 | tf_op jit(solution)/shard_map/ppermute | solution.py:174
  65.7 0.7 convert_element_type.74
  66.4 0.1 copy.14
  66.4 0.1 reshape.463
  66.5 1.2 convolution_convert_fusion.1
  67.8 14.8 %collective-permute-done.2.refs_3_.refs_8_ = bf16[32,4224]{1,0:T(8,128)(2,1)S(1)} collective-permute-done((bf16[32,4224]{1,0:T(8,128)(2,1)S(1)}, bf16[32,4224]{1,0:T(8,128)(2,1)S(1)}, u32[]{:S(2)}, u32[]{:S(2)}) %collective-permute-start.2) | collective-permute-done | bytes 270368 | tf_op jit(solution)/shard_map/ppermute | solution.py:174
  82.6 0.9 reshape.461
  83.5 12.1 %all-to-all-start.1 = ((bf16[64,3,768]{2,1,0:T(4,128)(2,1)}), bf16[64,3,768]{2,1,0:T(4,128)(2,1)}, u32[]{:S(2)}, u32[]{:S(2)}) async-start(bf16[64,3,768]{2,1,0:T(4,128)(2,1)} %reshape.461), calls=%async_computation.1 | async-start | bytes 786432 | tf_op jit(solution)/shard_map/all_to_all | solution.py:190
  95.6 0.0 reduce-scatter.2.cloned.1.call-start
  95.7 0.2 fusion.22
  95.9 3.4 %pick_rows.1 = (bf16[48,4096]{1,0:T(8,128)(2,1)S(1)}, bf16[48,4096]{1,0:T(8,128)(2,1)}, bf16[48,4096]{1,0:T(8,128)(2,1)}, bf16[48,4096]{1,0:T(8,128)(2,1)S(1)}) custom-call(s32[192,1]{1,0:T(8,128)S(1)} %get-tuple-element.29.home, s32[192,1]{1,0:T(8,128)S(1)} %get-tuple-element.30.lane, bf16[64,4224]{1,0:T(8,128)(2,1)S(1)} %all_gather.3.refs_0_.refs_5_, ...), custom_call_target="tpu_custom_call" | custom-call | flops 402653184 | bytes 3670016 | tf_op jit(solution)/shard_map/pick_rows/pallas_call | solution.py:48
  99.3 3.2 %collective-permute-start.5 = (bf16[48,4096]{1,0:T(8,128)(2,1)}, bf16[48,4096]{1,0:T(8,128)(2,1)S(1)}, u32[]{:S(2)}, u32[]{:S(2)}) collective-permute-start(bf16[48,4096]{1,0:T(8,128)(2,1)} %get-tuple-element.10), channel_id=1, source_target_pairs={{0,32},{16,48},{32,0},{48,16},{1,33},{17,49},{33,1},{49,17},{2,34}... | collective-permute-start | bytes 1179656 | tf_op jit(solution)/shard_map/ppermute | solution.py:224
  102.4 1.9 collective-permute-start.6
  104.4 5.1 %collective-permute-start.4 = (bf16[48,4096]{1,0:T(8,128)(2,1)}, bf16[48,4096]{1,0:T(8,128)(2,1)S(1)}, u32[]{:S(2)}, u32[]{:S(2)}) collective-permute-start(bf16[48,4096]{1,0:T(8,128)(2,1)} %get-tuple-element.9), channel_id=1, source_target_pairs={{0,16},{16,32},{32,48},{48,0},{1,17},{17,33},{33,49},{49,1},{2,18}... | collective-permute-start | bytes 1179656 | tf_op jit(solution)/shard_map/ppermute | solution.py:224
  109.6 1.9 collective-permute-start.8
  111.5 5.3 %collective-permute-done.5.refs_2_ = bf16[48,4096]{1,0:T(8,128)(2,1)S(1)} collective-permute-done((bf16[48,4096]{1,0:T(8,128)(2,1)}, bf16[48,4096]{1,0:T(8,128)(2,1)S(1)}, u32[]{:S(2)}, u32[]{:S(2)}) %collective-permute-start.5) | collective-permute-done | bytes 393248 | tf_op jit(solution)/shard_map/ppermute | solution.py:224
  116.8 1.9 collective-permute-start.10
  118.7 4.1 %collective-permute-done.6.refs_3_ = bf16[48,4096]{1,0:T(8,128)(2,1)S(1)} collective-permute-done((bf16[48,4096]{1,0:T(8,128)(2,1)S(1)}, bf16[48,4096]{1,0:T(8,128)(2,1)S(1)}, u32[]{:S(2)}, u32[]{:S(2)}) %collective-permute-start.6) | collective-permute-done | bytes 393248 | tf_op jit(solution)/shard_map/ppermute | solution.py:224
  122.8 1.9 collective-permute-start.11
  124.7 2.4 %collective-permute-start.9 = (bf16[48,4096]{1,0:T(8,128)(2,1)S(1)}, bf16[48,4096]{1,0:T(8,128)(2,1)}, u32[]{:S(2)}, u32[]{:S(2)}) collective-permute-start(bf16[48,4096]{1,0:T(8,128)(2,1)S(1)} %collective-permute-done.4.refs_1_), channel_id=1, source_target_pairs={{0,64},{64,0},{1,65},{65,1},{2,66},{66,2},{3,67},{67,3},{4,68},{68... | collective-permute-start | bytes 1179656 | tf_op jit(solution)/shard_map/ppermute | solution.py:226
  127.1 1.2 reshape.462
  128.4 0.8 fusion.1
  129.2 1.9 collective-permute-start.7
  131.2 1.4 collective-permute-done.7.left_pair
  132.5 4.9 %weight_term.1 = bf16[384,4096]{1,0:T(8,128)(2,1)} custom-call(bf16[384,192]{1,0:T(8,128)(2,1)S(1)} %get-tuple-element.22.left_own, bf16[384,192]{1,0:T(8,128)(2,1)S(1)} %collective-permute-done.7.left_pair, bf16[48,4096]{1,0:T(8,128)(2,1)S(1)} %get-tuple-element.8.refs_0_, bf16[48,4096]{1,0:T(8,128)(2,1)S(1)} %collective-permute-done.4.refs_1_, ...), custom_call_target="tpu_custom_call" | custom-call | flops 1207959552 | bytes 6586368 | tf_op jit(solution)/shard_map/weight_term/pallas_call | solution.py:81
  137.4 0.0 reduce-scatter.2.cloned.1.call-update
  137.5 0.0 copy-start.1
  137.5 5.3 %hidden_term.1 = bf16[192,768]{1,0:T(8,128)(2,1)S(1)} custom-call(bf16[1,768,4096]{2,1,0:T(8,128)(2,1)} %weight.1, bf16[192,192]{1,0:T(8,128)(2,1)S(1)} %fusion.13.order, bf16[48,4096]{1,0:T(8,128)(2,1)S(1)} %get-tuple-element.8.refs_0_, bf16[48,4096]{1,0:T(8,128)(2,1)S(1)} %collective-permute-done.4.refs_1_, ...), custom_call_target="tpu_custom_call" | custom-call | flops 1207959552 | bytes 8159232 | tf_op jit(solution)/shard_map/hidden_term/pallas_call | solution.py:119
  142.8 0.9 reshape.458
  143.7 14.3 %all-to-all-start = ((bf16[64,3,768]{2,1,0:T(4,128)(2,1)}), bf16[64,3,768]{2,1,0:T(4,128)(2,1)S(1)}, u32[]{:S(2)}, u32[]{:S(2)}) async-start(bf16[64,3,768]{2,1,0:T(4,128)(2,1)} %reshape.458), calls=%async_computation | async-start | bytes 786432 | tf_op jit(solution)/shard_map/all_to_all | solution.py:233
  158.0 0.1 copy.17
  158.1 26.4 %all-to-all-done = bf16[64,3,768]{2,1,0:T(4,128)(2,1)S(1)} async-done(((bf16[64,3,768]{2,1,0:T(4,128)(2,1)}), bf16[64,3,768]{2,1,0:T(4,128)(2,1)S(1)}, u32[]{:S(2)}, u32[]{:S(2)}) %all-to-all-start) | async-done | bytes 294944 | tf_op jit(solution)/shard_map/all_to_all | solution.py:233
  184.5 0.2 reshape.459
  184.8 1.0 fusion.4
  185.8 0.1 reshape.465
  185.9 0.1 multiply_reduce_fusion
  186.0 0.1 subtract_multiply_fusion
  186.1 0.7 copy.19
  186.8 4.8 %reduce-scatter.2.cloned.1.call-done = bf16[48,4096]{1,0:T(8,128)(2,1)} async-done(((bf16[384,4096]{1,0:T(8,128)(2,1)}), bf16[48,4096]{1,0:T(8,128)(2,1)}) %reduce-scatter.2.cloned.1.call-update) | async-done | bytes 393232 | tf_op jit(solution)/shard_map/reduce_scatter | solution.py:230
  (18 shorter events, 0.2 us)
Async XLA Ops:
  46.4 36.2 %collective-permute-start = (bf16[64,4224]{1,0:T(8,128)(2,1)S(1)}, bf16[64,4224]{1,0:T(8,128)(2,1)S(1)}, u32[]{:S(2)}, u32[]{:S(2)}) collective-permute-start(bf16[64,4224]{1,0:T(8,128)(2,1)S(1)} %all_gather.3.refs_0_.refs_5_), channel_id=1, source_target_pairs={{0,15},{1,0},{2,1},{3,2},{4,3},{5,4},{6,5},{7,6},{8,7},{9,8},{10,9... | collective-permute-start | bytes 1622024 | tf_op jit(solution)/shard_map/ppermute | solution.py:174
  55.7 26.8 %collective-permute-start.1 = (bf16[64,4224]{1,0:T(8,128)(2,1)S(1)}, bf16[64,4224]{1,0:T(8,128)(2,1)S(1)}, u32[]{:S(2)}, u32[]{:S(2)}) collective-permute-start(bf16[64,4224]{1,0:T(8,128)(2,1)S(1)} %all_gather.3.refs_0_.refs_5_), channel_id=1, source_target_pairs={{0,1},{1,2},{2,3},{3,4},{4,5},{5,6},{6,7},{7,8},{8,9},{9,10},{10,1... | collective-permute-start | bytes 1622024 | tf_op jit(solution)/shard_map/ppermute | solution.py:174
  57.7 24.9 %collective-permute-start.2 = (bf16[32,4224]{1,0:T(8,128)(2,1)S(1)}, bf16[32,4224]{1,0:T(8,128)(2,1)S(1)}, u32[]{:S(2)}, u32[]{:S(2)}) collective-permute-start(bf16[32,4224]{1,0:T(8,128)(2,1)S(1)} %get-tuple-element.20), channel_id=1, source_target_pairs={{0,2},{1,3},{2,4},{3,5},{4,6},{5,7},{6,8},{7,9},{8,10},{9,11},{10,... | collective-permute-start | bytes 811016 | tf_op jit(solution)/shard_map/ppermute | solution.py:174
  59.6 22.9 %collective-permute-start.3 = (bf16[32,4224]{1,0:T(8,128)(2,1)S(1)}, bf16[32,4224]{1,0:T(8,128)(2,1)S(1)}, u32[]{:S(2)}, u32[]{:S(2)}) collective-permute-start(bf16[32,4224]{1,0:T(8,128)(2,1)S(1)} %get-tuple-element.19), channel_id=1, source_target_pairs={{0,14},{1,15},{2,0},{3,1},{4,2},{5,3},{6,4},{7,5},{8,6},{9,7},{10,... | collective-permute-start | bytes 811016 | tf_op jit(solution)/shard_map/ppermute | solution.py:174
  83.5 43.6 %all-to-all-start.1 = ((bf16[64,3,768]{2,1,0:T(4,128)(2,1)}), bf16[64,3,768]{2,1,0:T(4,128)(2,1)}, u32[]{:S(2)}, u32[]{:S(2)}) async-start(bf16[64,3,768]{2,1,0:T(4,128)(2,1)} %reshape.461), calls=%async_computation.1 | async-start | bytes 786432 | tf_op jit(solution)/shard_map/all_to_all | solution.py:190
  95.6 95.9 %reduce-scatter.2.cloned.1.call-start = ((), (), s32[]{:S(2)}) async-start(), calls=%async_computation.3 | async-start | bytes 3538944 | tf_op jit(solution)/shard_map/reduce_scatter | solution.py:230
  99.3 17.5 %collective-permute-start.5 = (bf16[48,4096]{1,0:T(8,128)(2,1)}, bf16[48,4096]{1,0:T(8,128)(2,1)S(1)}, u32[]{:S(2)}, u32[]{:S(2)}) collective-permute-start(bf16[48,4096]{1,0:T(8,128)(2,1)} %get-tuple-element.10), channel_id=1, source_target_pairs={{0,32},{16,48},{32,0},{48,16},{1,33},{17,49},{33,1},{49,17},{2,34}... | collective-permute-start | bytes 1179656 | tf_op jit(solution)/shard_map/ppermute | solution.py:224
  102.4 20.3 %collective-permute-start.6 = (bf16[48,4096]{1,0:T(8,128)(2,1)S(1)}, bf16[48,4096]{1,0:T(8,128)(2,1)S(1)}, u32[]{:S(2)}, u32[]{:S(2)}) collective-permute-start(bf16[48,4096]{1,0:T(8,128)(2,1)S(1)} %get-tuple-element.11), channel_id=1, source_target_pairs={{0,48},{16,0},{32,16},{48,32},{1,49},{17,1},{33,17},{49,33},{2,50}... | collective-permute-start | bytes 1179656 | tf_op jit(solution)/shard_map/ppermute | solution.py:224
  104.4 20.3 %collective-permute-start.4 = (bf16[48,4096]{1,0:T(8,128)(2,1)}, bf16[48,4096]{1,0:T(8,128)(2,1)S(1)}, u32[]{:S(2)}, u32[]{:S(2)}) collective-permute-start(bf16[48,4096]{1,0:T(8,128)(2,1)} %get-tuple-element.9), channel_id=1, source_target_pairs={{0,16},{16,32},{32,48},{48,0},{1,17},{17,33},{33,49},{49,1},{2,18}... | collective-permute-start | bytes 1179656 | tf_op jit(solution)/shard_map/ppermute | solution.py:224
  109.6 21.6 %collective-permute-start.8 = (bf16[48,4096]{1,0:T(8,128)(2,1)S(1)}, bf16[48,4096]{1,0:T(8,128)(2,1)S(1)}, u32[]{:S(2)}, u32[]{:S(2)}) collective-permute-start(bf16[48,4096]{1,0:T(8,128)(2,1)S(1)} %get-tuple-element.8.refs_0_), channel_id=1, source_target_pairs={{0,64},{64,0},{1,65},{65,1},{2,66},{66,2},{3,67},{67,3},{4,68},{68... | collective-permute-start | bytes 1179656 | tf_op jit(solution)/shard_map/ppermute | solution.py:226
  116.8 14.4 %collective-permute-start.10 = (bf16[48,4096]{1,0:T(8,128)(2,1)S(1)}, bf16[48,4096]{1,0:T(8,128)(2,1)S(1)}, u32[]{:S(2)}, u32[]{:S(2)}) collective-permute-start(bf16[48,4096]{1,0:T(8,128)(2,1)S(1)} %collective-permute-done.5.refs_2_), channel_id=1, source_target_pairs={{0,64},{64,0},{1,65},{65,1},{2,66},{66,2},{3,67},{67,3},{4,68},{68... | collective-permute-start | bytes 1179656 | tf_op jit(solution)/shard_map/ppermute | solution.py:226
  122.8 8.4 %collective-permute-start.11 = (bf16[48,4096]{1,0:T(8,128)(2,1)S(1)}, bf16[48,4096]{1,0:T(8,128)(2,1)S(1)}, u32[]{:S(2)}, u32[]{:S(2)}) collective-permute-start(bf16[48,4096]{1,0:T(8,128)(2,1)S(1)} %collective-permute-done.6.refs_3_), channel_id=1, source_target_pairs={{0,64},{64,0},{1,65},{65,1},{2,66},{66,2},{3,67},{67,3},{4,68},{68... | collective-permute-start | bytes 1179656 | tf_op jit(solution)/shard_map/ppermute | solution.py:226
  124.7 6.5 %collective-permute-start.9 = (bf16[48,4096]{1,0:T(8,128)(2,1)S(1)}, bf16[48,4096]{1,0:T(8,128)(2,1)}, u32[]{:S(2)}, u32[]{:S(2)}) collective-permute-start(bf16[48,4096]{1,0:T(8,128)(2,1)S(1)} %collective-permute-done.4.refs_1_), channel_id=1, source_target_pairs={{0,64},{64,0},{1,65},{65,1},{2,66},{66,2},{3,67},{67,3},{4,68},{68... | collective-permute-start | bytes 1179656 | tf_op jit(solution)/shard_map/ppermute | solution.py:226
  129.2 3.3 %collective-permute-start.7 = (bf16[384,192]{1,0:T(8,128)(2,1)S(1)}, bf16[384,192]{1,0:T(8,128)(2,1)S(1)}, u32[]{:S(2)}, u32[]{:S(2)}) collective-permute-start(bf16[384,192]{1,0:T(8,128)(2,1)S(1)} %get-tuple-element.21), channel_id=1, source_target_pairs={{0,64},{64,0},{1,65},{65,1},{2,66},{66,2},{3,67},{67,3},{4,68},{68... | collective-permute-start | bytes 442376 | tf_op jit(solution)/shard_map/ppermute | solution.py:227
  137.5 20.5 %copy-start.1 = (f32[16,8]{0,1:T(8,128)S(1)}, f32[16,8]{0,1:T(8,128)}, u32[]{:S(2)}) copy-start(f32[16,8]{0,1:T(8,128)} %param.7) | copy-start | bytes 1540
  137.5 47.3 %copy-start = (bf16[16,8,768]{2,1,0:T(8,128)(2,1)S(1)}, bf16[16,8,768]{2,1,0:T(8,128)(2,1)}, u32[]{:S(2)}) copy-start(bf16[16,8,768]{2,1,0:T(8,128)(2,1)} %param.6) | copy-start | bytes 589828
  143.7 40.8 %all-to-all-start = ((bf16[64,3,768]{2,1,0:T(4,128)(2,1)}), bf16[64,3,768]{2,1,0:T(4,128)(2,1)S(1)}, u32[]{:S(2)}, u32[]{:S(2)}) async-start(bf16[64,3,768]{2,1,0:T(4,128)(2,1)} %reshape.458), calls=%async_computation | async-start | bytes 786432 | tf_op jit(solution)/shard_map/all_to_all | solution.py:233
Sparse Core Ops, SparseCore 0:
  137.6 53.9 reduce-scatter.1

commit v6 on v4

v6 whole, which is shorter than its diff:
```python
import jax
import jax.numpy as jnp
import numpy as np
from jax import lax
from jax.experimental import pallas as pl
from jax.experimental.pallas import tpu as pltpu
from jax.sharding import Mesh
from jax.sharding import PartitionSpec as P

MOST = 3
TOK = 16
CORES = 2
X, Y, ZH, ZL = 4, 8, 4, 4
Z = ZH * ZL
LANES = 128
BLOCK = 1024
BF16 = jnp.bfloat16
F32 = jnp.float32
MIB = 1024 * 1024


def pick_kernel(home, lane, own, out):
    tokens, held = own.shape
    width = held - LANES
    rows = out.shape[0]
    at = lax.broadcasted_iota(jnp.int32, (home.shape[0], tokens), 1)
    line = jnp.where(at == home[...], 1.0, 0.0).astype(BF16)
    values = jnp.dot(line, own[:, width:], preferred_element_type=F32)
    lanes = lax.broadcasted_iota(jnp.int32, values.shape, 1)
    value = jnp.sum(jnp.where(lanes == lane[...], values, 0.0), axis=1, keepdims=True)
    first = home[...] // TOK * TOK
    token = jnp.where(value > 0.0, value.astype(jnp.int32) - 1 + first, -1)
    pick = jnp.where(at == token, 1.0, 0.0).astype(BF16)
    whole, lower, upper = pick[:rows], pick[rows : 2 * rows], pick[2 * rows :]
    for start in range(0, width, BLOCK):
        block = own[:, start : start + BLOCK]
        out[:, start : start + BLOCK] = jnp.dot(
            whole, block, preferred_element_type=F32
        ).astype(out.dtype)
    for start in range(0, width // 2, BLOCK):
        block = own[:, start : start + BLOCK]
        total = jnp.dot(lower, block, preferred_element_type=F32)
        block = own[:, width // 2 + start : width // 2 + start + BLOCK]
        total = total + jnp.dot(upper, block, preferred_element_type=F32)
        out[:, width + start : width + start + BLOCK] = total.astype(out.dtype)


def pick_rows(home, lane, own, rows):
    tokens, held = own.shape
    width = held - LANES
    return pl.pallas_call(
        pick_kernel,
        out_shape=jax.ShapeDtypeStruct((rows, width + width // 2), BF16),
        in_specs=[pl.BlockSpec(memory_space=pltpu.VMEM)] * 3,
        out_specs=pl.BlockSpec(memory_space=pltpu.VMEM),
        compiler_params=pltpu.CompilerParams(vmem_limit_bytes=32 * MIB),
        cost_estimate=pl.CostEstimate(
            flops=4 * rows * tokens * width,
            bytes_accessed=2 * width * (2 * rows + tokens),
            transcendentals=0,
        ),
        name="pick_rows",
    )(home, lane, own)


def joined(whole, halves):
    return jnp.concatenate([whole[...], halves[...]], axis=0)


def weight_kernel(own_a, own_b, pair_a, pair_b, rows_a, rows_b, other_a, other_b, out):
    left = jnp.concatenate([own_a[...], own_b[...]], axis=1)
    total = jnp.dot(left, joined(rows_a, rows_b), preferred_element_type=F32)
    left = jnp.concatenate([pair_a[...], pair_b[...]], axis=1)
    total = total + jnp.dot(left, joined(other_a, other_b), preferred_element_type=F32)
    out[...] = total.astype(out.dtype)


def weight_term(left_own, left_pair, rows_own, rows_pair):
    half = left_own.shape[0]
    rows, packed = rows_own.shape
    width = packed // 3 * 2
    blocks = width // BLOCK
    left_a = pl.BlockSpec((half, rows), lambda i: (0, 0))
    left_b = pl.BlockSpec((half, rows), lambda i: (0, 1 + i // (blocks // 2)))
    rows_a = pl.BlockSpec((rows, BLOCK), lambda i: (0, i))
    rows_b = pl.BlockSpec((rows, BLOCK), lambda i: (0, blocks + i % (blocks // 2)))
    return pl.pallas_call(
        weight_kernel,
        grid=(blocks,),
        out_shape=jax.ShapeDtypeStruct((half, width), BF16),
        in_specs=[left_a, left_b, left_a, left_b, rows_a, rows_b, rows_a, rows_b],
        out_specs=pl.BlockSpec((half, BLOCK), lambda i: (0, i)),
        compiler_params=pltpu.CompilerParams(vmem_limit_bytes=49 * MIB),
        cost_estimate=pl.CostEstimate(
            flops=8 * half * rows * width,
            bytes_accessed=2 * (2 * rows * packed + half * width),
            transcendentals=0,
        ),
        name="weight_term",
    )(left_own, left_own, left_pair, left_pair, rows_own, rows_own, rows_pair, rows_pair)


def hidden_kernel(rows_a, rows_b, weight, order, out, total):
    step = pl.program_id(0)
    rows = rows_a.shape[0]

    @pl.when(step == 0)
    def _():
        total[...] = jnp.zeros_like(total)

    now = lax.dot_general(
        joined(rows_a, rows_b),
        weight[...],
        (((1,), (1,)), ((), ())),
        preferred_element_type=F32,
    )
    total[:rows] += now[:rows]
    late = step >= pl.num_programs(0) // 2

    @pl.when(jnp.logical_not(late))
    def _():
        total[rows : 2 * rows] += now[rows:]

    @pl.when(late)
    def _():
        total[2 * rows :] += now[rows:]

    @pl.when(step == pl.num_programs(0) - 1)
    def _():
        rounded = total[...].astype(BF16)
        out[...] = jnp.dot(order[...], rounded, preferred_element_type=F32).astype(out.dtype)


def hidden_term(rows_own, weight, order):
    slots, spread = order.shape
    hidden, width = weight.shape[1:]
    rows = rows_own.shape[0]
    blocks = width // BLOCK
    return pl.pallas_call(
        hidden_kernel,
        grid=(blocks,),
        out_shape=jax.ShapeDtypeStruct((slots, hidden), BF16),
        in_specs=[
            pl.BlockSpec((rows, BLOCK), lambda i: (0, i)),
            pl.BlockSpec((rows, BLOCK), lambda i: (0, blocks + i % (blocks // 2))),
            pl.BlockSpec((None, hidden, BLOCK), lambda i: (0, 0, i)),
            pl.BlockSpec((slots, spread), lambda i: (0, 0)),
        ],
        out_specs=pl.BlockSpec((slots, hidden), lambda i: (0, 0)),
        scratch_shapes=[pltpu.VMEM((spread, hidden), F32)],
        compiler_params=pltpu.CompilerParams(vmem_limit_bytes=49 * MIB),
        cost_estimate=pl.CostEstimate(
            flops=4 * rows * hidden * width,
            bytes_accessed=2 * (2 * rows * width + hidden * width + slots * hidden),
            transcendentals=0,
        ),
        name="hidden_term",
    )(rows_own, rows_own, weight, order)


def shards(out_grad, hidden_acts, gate_weights, expert_idx, down_weight):
    tok_rows, top_count = expert_idx.shape
    routed = tok_rows * top_count
    width = out_grad.shape[1]
    hidden = hidden_acts.shape[2]
    half = hidden // CORES
    experts = X * Z
    slot_count = experts * MOST
    core = lax.axis_index("core")
    high_at = lax.axis_index("zh")
    swap = [(0, 1), (1, 0)]

    flat_expert = expert_idx.reshape(routed)
    member = (flat_expert[:, None] == jnp.arange(experts, dtype=jnp.int32)[None, :]).astype(BF16)
    row_line = jnp.arange(routed, dtype=jnp.int32)
    earlier_mask = (row_line[:, None] > row_line[None, :]).astype(BF16)
    earlier = jnp.dot(earlier_mask, member, preferred_element_type=F32)
    position = jnp.sum(earlier * member.astype(F32), axis=1).astype(jnp.int32)
    slot_index = flat_expert * MOST + position
    placement = (jnp.arange(slot_count, dtype=jnp.int32)[:, None] == slot_index[None, :]).astype(BF16)

    plane_of = (jnp.arange(Z, dtype=jnp.int32)[:, None] == (flat_expert % Z)[None, :]).astype(BF16)
    lane_of = (flat_expert // Z) * MOST + position
    token_of = (row_line // top_count + 1).astype(F32)
    token_at = jnp.where(
        lane_of[:, None] == jnp.arange(LANES, dtype=jnp.int32)[None, :], token_of[:, None], 0.0
    ).astype(BF16)
    table = jnp.dot(plane_of, token_at, preferred_element_type=F32).astype(BF16)

    own = lax.all_gather(jnp.concatenate([out_grad, table], axis=1), "zh", axis=0, tiled=True)

    gate_half = lax.optimization_barrier(gate_weights.astype(BF16)).astype(F32)
    flat_acts = hidden_acts.reshape(routed, hidden).astype(F32)
    gated = (gate_half.reshape(routed, 1) * flat_acts).astype(BF16)
    send_acts = jnp.dot(placement, gated, preferred_element_type=F32).astype(BF16)
    acts_in = lax.all_to_all(
        send_acts.reshape(experts, MOST, hidden),
        ("x", "zh", "zl"),
        split_axis=0,
        concat_axis=0,
        tiled=True,
    ).reshape(slot_count, hidden)

    packed = X * ZL * 8
    device, row = np.divmod(np.arange(packed, dtype=np.int32), 8)
    entry = np.concatenate([row, 8 + row % 4, 8 + row % 4])
    used = np.concatenate([row >= 0, row < 4, row >= 4])
    device = np.tile(device, 3)
    high, rank = np.divmod(entry, MOST)
    slot = device // ZL * (Z * MOST) + (high * ZL + device % ZL) * MOST + rank
    slot = np.where(used, slot, -1).astype(np.int32)
    order = (jnp.arange(slot_count, dtype=jnp.int32)[:, None] == slot[None, :]).astype(BF16)

    line = np.arange(hidden, dtype=np.int32)
    piece = hidden // (Y * CORES)
    unit = (((line % half) // piece * CORES + line // half) * piece + line % piece).astype(np.int32)
    reorder = (unit[:, None] == line[None, :]).astype(BF16)
    acts_rows = lax.dot_general(
        order, acts_in, (((0,), (0,)), ((), ())), preferred_element_type=F32
    ).astype(BF16)
    left = lax.dot_general(
        reorder, acts_rows, (((1,), (1,)), ((), ())), preferred_element_type=F32
    ).astype(BF16)
    left_own = lax.dynamic_slice_in_dim(left, core * half, half, 0)
    left_away = lax.dynamic_slice_in_dim(left, (1 - core) * half, half, 0)
    left_pair = lax.ppermute(left_away, "core", swap)

    home = np.where(used, high * tok_rows + device % ZL, -tok_rows).astype(np.int32)[:, None]
    lane = (device // ZL * MOST + rank).astype(np.int32)[:, None]
    picked = pick_rows(home + high_at * ZL, lane, own, packed)
    rows = lax.all_to_all(picked, ("x", "zl"), split_axis=0, concat_axis=0, tiled=True)
    rows, left_own, left_pair = lax.optimization_barrier((rows, left_own, left_pair))
    rows_pair = lax.ppermute(rows, "core", swap)

    part = weight_term(left_own, left_pair, rows, rows_pair)
    summed = lax.psum_scatter(part, "y", scatter_dimension=0, tiled=True)

    grad_hidden = hidden_term(rows, down_weight, order)
    back = lax.all_to_all(
        grad_hidden.reshape(experts, MOST, hidden),
        ("x", "zh", "zl"),
        split_axis=0,
        concat_axis=0,
        tiled=True,
    ).reshape(slot_count, hidden)
    grad_tok = lax.dot_general(
        placement, back, (((0,), (0,)), ((), ())), preferred_element_type=F32
    )
    act_grad = (gate_half.reshape(routed, 1) * grad_tok).astype(BF16)
    score = jnp.sum(grad_tok * flat_acts, axis=1).astype(BF16).astype(F32)
    score = score.reshape(tok_rows, top_count)
    logit_grad = gate_weights * (score - jnp.sum(gate_weights * score, axis=1, keepdims=True))
    return act_grad.reshape(tok_rows, top_count, hidden), logit_grad, summed[None]


def solution(mesh):
    dims = Mesh(mesh.devices.reshape(Y, CORES, X, ZH, ZL), ("y", "core", "x", "zh", "zl"))
    experts = ("x", "zh", "zl")
    tokens = ("y", "core") + experts
    return jax.shard_map(
        shards,
        mesh=dims,
        in_specs=(
            P(tokens, None),
            P(tokens, None, None),
            P(tokens, None),
            P(tokens, None),
            P(experts, None, None),
        ),
        out_specs=(
            P(tokens, None, None),
            P(tokens, None),
            P(experts, ("y", "core"), None),
        ),
        check_vma=False,
    )
```

time: 198 us -> 188 us (0.949)
  starting transfers between devices: 52.9 us -> 44.1 us
  waiting for transfers between devices: 70.3 us -> 62.8 us
  blocking collectives: 37.1 us -> 44.1 us
    ppermute x4 -> x0, starting transfers between devices: 19.2 us -> none  [shifted(): return lax.ppermute(part, planes, [(i, (i + by) % Z) for i in range(Z)])]
    all_to_all x3, starting transfers between devices: 29.4 us -> 40.2 us  [the longest x1 22.6 us: shards(): lax.all_to_all(send_acts.reshape(experts, MOST, hidden), ('x', 'zh', 'zl'...]
    all_to_all x3, waiting for transfers between devices: 61.1 us -> 53.2 us  [the longest x1 26.8 us: shards(): lax.all_to_all(picked, ('x', 'zl'), split_axis=0, concat_axis=0, tiled=True)]
    all_gather x1, blocking collectives: 37.1 us -> 44.1 us  [shards(): lax.all_gather(jnp.concatenate([out_grad, table], axis=1), 'zh', axis=0,...]
    ppermute x1, waiting for transfers between devices: 0.01 us -> 3.38 us  [shards(): rows_pair = lax.ppermute(rows, 'core', swap)]
    ppermute x4 -> x0, waiting for transfers between devices: 3.28 us -> none  [shifted(): return lax.ppermute(part, planes, [(i, (i + by) % Z) for i in range(Z)])]
  transfers between devices with their start and end apart: 10 -> 6, of which waited for: 7 -> 5; matrix products, arithmetic and copies ran while one was open for 4% -> 3% of each run, Pallas kernels for 3% -> 4%
where the time goes in v6:
time: 188 us; the launch traced here: 187 us
  waiting for transfers between devices  62.8 us (33%)
  starting transfers between devices  44.1 us (23%)
  blocking collectives  44.1 us (23%)
  between operations  14.2 us (8%)
  Pallas kernels  11.8 us (6%)
  matrix products  4.94 us (3%)
  local copies, waits for them, and re-layouts  4.25 us (2%)
    all_gather x1, blocking collectives, shards(): lax.all_gather(jnp.concatenate([out_grad, table], axis=1), 'zh', axis=0,...  44.1 us
    all_to_all x1, waiting for transfers between devices, shards(): lax.all_to_all(picked, ('x', 'zl'), split_axis=0, concat_axis=0, tiled=True)  26.8 us
    all_to_all x1, waiting for transfers between devices, shards(): lax.all_to_all(grad_hidden.reshape(experts, MOST, hidden), ('x', 'zh', 'z...  26.4 us
    all_to_all x1, starting transfers between devices, shards(): lax.all_to_all(send_acts.reshape(experts, MOST, hidden), ('x', 'zh', 'zl'...  22.6 us
    all_to_all x1, starting transfers between devices, shards(): lax.all_to_all(grad_hidden.reshape(experts, MOST, hidden), ('x', 'zh', 'z...  9.63 us
    all_to_all x1, starting transfers between devices, shards(): lax.all_to_all(picked, ('x', 'zl'), split_axis=0, concat_axis=0, tiled=True)  7.99 us
    pallas_call x1, Pallas kernels, hidden_term(): pl.pallas_call(hidden_kernel, grid=(blocks,), out_shape=jax.ShapeDtypeStr...  5.47 us
    reduce_scatter x1, waiting for transfers between devices, shards(): summed = lax.psum_scatter(part, 'y', scatter_dimension=0, tiled=True)  4.66 us
  transfers between devices with their start and end apart: 6, of which 5 were waited for; matrix products, arithmetic and copies ran while one was open for 3% of the time, Pallas kernels for 4%

profile of v6, /device:TPU:6, one launch (start us, length us, event | category | flops | bytes accessed | tf_op | source)
XLA Modules:
  0.0 187.3 jit_solution(13905988972787214697)
XLA Ops:
  7.2 0.0 copy-start.3
  7.2 0.8 copy.25
  8.0 0.1 reshape.117
  8.1 0.2 fusion
  8.3 0.7 convert_element_type.74
  8.9 0.1 copy.24
  9.0 0.1 reshape.123
  9.1 1.2 convolution_convert_fusion.2
  10.4 0.0 copy-start.2
  10.4 0.9 reshape.118
  11.3 0.0 copy-start
  11.3 22.6 %all-to-all-start.1 = ((bf16[64,3,768]{2,1,0:T(4,128)(2,1)}), bf16[64,3,768]{2,1,0:T(4,128)(2,1)S(1)}, u32[]{:S(2)}, u32[]{:S(2)}) async-start(bf16[64,3,768]{2,1,0:T(4,128)(2,1)} %reshape.118), calls=%async_computation.1 | async-start | bytes 786432 | tf_op jit(solution)/shard_map/all_to_all | solution.py:196
  33.9 0.2 convolution_convert_fusion.3
  34.1 0.0 copy-done.3
  34.1 44.1 %all_gather.3.own = bf16[64,4224]{1,0:T(8,128)(2,1)S(1)} all-gather(bf16[16,4224]{1,0:T(8,128)(2,1)S(1)} %pad_maximum_fusion), channel_id=1, replica_groups=mesh['y'=8,'core'=2,'x'=4,'zh'=4,'zl'=4] {'zh'}, dimensions={0}, use_global_device_ids=true | all-gather | bytes 675840 | tf_op jit(solution)/shard_map/all_gather | solution.py:190
  78.2 0.0 copy-done.2
  78.3 0.0 copy-done
  78.3 2.4 %pick_rows.1 = bf16[128,6144]{1,0:T(8,128)(2,1)} custom-call(s32[384,1]{1,0:T(8,128)S(1)} %broadcast_add_fusion.home, s32[384,1]{1,0:T(8,128)S(1)} %copy-done, bf16[64,4224]{1,0:T(8,128)(2,1)S(1)} %all_gather.3.own), custom_call_target="tpu_custom_call" | custom-call | flops 134217728 | bytes 2621440 | tf_op jit(solution)/shard_map/pick_rows/pallas_call | solution.py:51
  80.6 0.0 all-to-all-done.1
  80.6 8.0 %all-to-all-start = ((bf16[16,8,6144]{2,1,0:T(8,128)(2,1)}), bf16[16,8,6144]{2,1,0:T(8,128)(2,1)S(1)}, u32[]{:S(2)}, u32[]{:S(2)}) async-start(bf16[16,8,6144]{2,1,0:T(8,128)(2,1)} %bitcast), calls=%async_computation | async-start | bytes 3145728 | tf_op jit(solution)/shard_map/all_to_all | solution.py:231
  88.6 0.0 reduce-scatter.2.cloned.1.call-start
  88.7 0.3 reshape.119
  88.9 0.0 copy-done.5
  88.9 2.3 %convolution_convert_fusion = bf16[384,768]{0,1:T(8,128)(2,1)S(1)} fusion(bf16[768,768]{1,0:T(8,128)(2,1)} %constant.72.clone, bf16[192,768]{1,0:T(8,128)(2,1)S(1)} %reshape.119, s32[384]{0:T(512)S(1)} %copy-done.5), kind=kOutput, calls=%fused_computation | convolution fusion | flops 566894592 | bytes 2065920 | tf_op jit(solution)/shard_map/dot_general | solution.py:221
  91.2 0.1 dynamic-slice_bitcast_fusion
  91.3 1.9 %collective-permute-start = (bf16[384,384]{1,0:T(8,128)(2,1)S(1)}, bf16[384,384]{1,0:T(8,128)(2,1)S(1)}, u32[]{:S(2)}, u32[]{:S(2)}) collective-permute-start(bf16[384,384]{1,0:T(8,128)(2,1)S(1)} %get-tuple-element.18), channel_id=1, source_target_pairs={{0,64},{64,0},{1,65},{65,1},{2,66},{66,2},{3,67},{67,3},{4,68},{68... | collective-permute-start | bytes 884744 | tf_op jit(solution)/shard_map/ppermute | solution.py:226
  93.2 1.5 collective-permute-done.pair_a.pair_b
  94.8 26.8 %all-to-all-done = bf16[16,8,6144]{2,1,0:T(8,128)(2,1)S(1)} async-done(((bf16[16,8,6144]{2,1,0:T(8,128)(2,1)}), bf16[16,8,6144]{2,1,0:T(8,128)(2,1)S(1)}, u32[]{:S(2)}, u32[]{:S(2)}) %all-to-all-start) | async-done | bytes 1572896 | tf_op jit(solution)/shard_map/all_to_all | solution.py:231
  121.6 1.9 %collective-permute-start.1 = (bf16[128,6144]{1,0:T(8,128)(2,1)S(1)}, bf16[128,6144]{1,0:T(8,128)(2,1)S(1)}, u32[]{:S(2)}, u32[]{:S(2)}) collective-permute-start(bf16[128,6144]{1,0:T(8,128)(2,1)S(1)} %bitcast.19), channel_id=1, source_target_pairs={{0,64},{64,0},{1,65},{65,1},{2,66},{66,2},{3,67},{67,3},{4,68},{68... | collective-permute-start | bytes 4718600 | tf_op jit(solution)/shard_map/ppermute | solution.py:233
  123.5 3.4 %collective-permute-done.1.other_a.other_b = bf16[128,6144]{1,0:T(8,128)(2,1)S(1)} collective-permute-done((bf16[128,6144]{1,0:T(8,128)(2,1)S(1)}, bf16[128,6144]{1,0:T(8,128)(2,1)S(1)}, u32[]{:S(2)}, u32[]{:S(2)}) %collective-permute-start.1) | collective-permute-done | bytes 1572896 | tf_op jit(solution)/shard_map/ppermute | solution.py:233
  126.9 4.0 %weight_term.1 = bf16[384,4096]{1,0:T(8,128)(2,1)} custom-call(bf16[384,384]{1,0:T(8,128)(2,1)S(1)} %get-tuple-element.7.own_a.own_b, bf16[384,384]{1,0:T(8,128)(2,1)S(1)} %get-tuple-element.7.own_a.own_b, bf16[384,384]{1,0:T(8,128)(2,1)S(1)} %collective-permute-done.pair_a.pair_b, bf16[384,384]{1,0:T(8,128)(2,1)S(1)} %collective-permute-done.pair_a.pair_b, ...), custom_call_target="tpu_custom_call" | custom-call | flops 1610612736 | bytes 6291456 | tf_op jit(solution)/shard_map/weight_term/pallas_call | solution.py:87
  130.9 0.0 reduce-scatter.2.cloned.1.call-update
  131.0 5.5 %hidden_term.1 = bf16[192,768]{1,0:T(8,128)(2,1)S(1)} custom-call(bf16[128,6144]{1,0:T(8,128)(2,1)S(1)} %bitcast.22, bf16[128,6144]{1,0:T(8,128)(2,1)S(1)} %bitcast.23, bf16[1,768,4096]{2,1,0:T(8,128)(2,1)} %weight.1, bf16[192,384]{1,0:T(8,128)(2,1)S(1)} %fusion.3.order), custom_call_target="tpu_custom_call" | custom-call | flops 1610612736 | bytes 8683520 | tf_op jit(solution)/shard_map/hidden_term/pallas_call | solution.py:139
  136.4 0.0 copy-start.4
  136.5 0.0 copy-start.1
  136.5 0.9 reshape.120
  137.4 9.6 %all-to-all-start.2 = ((bf16[64,3,768]{2,1,0:T(4,128)(2,1)}), bf16[64,3,768]{2,1,0:T(4,128)(2,1)S(1)}, u32[]{:S(2)}, u32[]{:S(2)}) async-start(bf16[64,3,768]{2,1,0:T(4,128)(2,1)} %reshape.120), calls=%async_computation.2 | async-start | bytes 786432 | tf_op jit(solution)/shard_map/all_to_all | solution.py:239
  147.0 0.0 copy-done.4
  147.0 0.1 copy.29
  147.1 26.4 %all-to-all-done.2 = bf16[64,3,768]{2,1,0:T(4,128)(2,1)S(1)} async-done(((bf16[64,3,768]{2,1,0:T(4,128)(2,1)}), bf16[64,3,768]{2,1,0:T(4,128)(2,1)S(1)}, u32[]{:S(2)}, u32[]{:S(2)}) %all-to-all-start.2) | async-done | bytes 294944 | tf_op jit(solution)/shard_map/all_to_all | solution.py:239
  173.5 0.2 reshape.121
  173.7 0.0 copy-done.1
  173.8 1.0 fusion.2
  174.8 0.1 reshape.125
  174.9 0.1 multiply_reduce_fusion
  175.0 0.1 subtract_multiply_fusion
  175.1 0.7 copy.30
  175.8 4.7 %reduce-scatter.2.cloned.1.call-done = bf16[48,4096]{1,0:T(8,128)(2,1)} async-done(((bf16[384,4096]{1,0:T(8,128)(2,1)}), bf16[48,4096]{1,0:T(8,128)(2,1)}) %reduce-scatter.2.cloned.1.call-update) | async-done | bytes 393232 | tf_op jit(solution)/shard_map/reduce_scatter | solution.py:236
  (5 shorter events, 0.1 us)
Async XLA Ops:
  7.2 26.9 %copy-start.3 = (bf16[16,4096]{1,0:T(8,128)(2,1)S(1)}, bf16[16,4096]{1,0:T(8,128)(2,1)}, u32[]{:S(2)}) copy-start(bf16[16,4096]{1,0:T(8,128)(2,1)} %param.9) | copy-start | bytes 393220
  10.4 67.9 %copy-start.2 = (s32[384,1]{1,0:T(8,128)S(1)}, s32[384,1]{1,0:T(8,128)}, u32[]{:S(2)}) copy-start(s32[384,1]{1,0:T(8,128)} %constant.73.clone) | copy-start | bytes 4612
  11.3 67.0 %copy-start = (s32[384,1]{1,0:T(8,128)S(1)}, s32[384,1]{1,0:T(8,128)}, u32[]{:S(2)}) copy-start(s32[384,1]{1,0:T(8,128)} %constant.74.clone.lane) | copy-start | bytes 4612
  11.3 69.4 %all-to-all-start.1 = ((bf16[64,3,768]{2,1,0:T(4,128)(2,1)}), bf16[64,3,768]{2,1,0:T(4,128)(2,1)S(1)}, u32[]{:S(2)}, u32[]{:S(2)}) async-start(bf16[64,3,768]{2,1,0:T(4,128)(2,1)} %reshape.118), calls=%async_computation.1 | async-start | bytes 786432 | tf_op jit(solution)/shard_map/all_to_all | solution.py:196
  80.6 8.3 %copy-start.5 = (s32[384]{0:T(512)S(1)}, s32[384]{0:T(512)}, u32[]{:S(2)}) copy-start(s32[384]{0:T(512)} %constant.80) | copy-start | bytes 4612
  80.6 41.0 %all-to-all-start = ((bf16[16,8,6144]{2,1,0:T(8,128)(2,1)}), bf16[16,8,6144]{2,1,0:T(8,128)(2,1)S(1)}, u32[]{:S(2)}, u32[]{:S(2)}) async-start(bf16[16,8,6144]{2,1,0:T(8,128)(2,1)} %bitcast), calls=%async_computation | async-start | bytes 3145728 | tf_op jit(solution)/shard_map/all_to_all | solution.py:231
  88.6 91.8 %reduce-scatter.2.cloned.1.call-start = ((), (), s32[]{:S(2)}) async-start(), calls=%async_computation.4 | async-start | bytes 3538944 | tf_op jit(solution)/shard_map/reduce_scatter | solution.py:236
  91.3 3.5 %collective-permute-start = (bf16[384,384]{1,0:T(8,128)(2,1)S(1)}, bf16[384,384]{1,0:T(8,128)(2,1)S(1)}, u32[]{:S(2)}, u32[]{:S(2)}) collective-permute-start(bf16[384,384]{1,0:T(8,128)(2,1)S(1)} %get-tuple-element.18), channel_id=1, source_target_pairs={{0,64},{64,0},{1,65},{65,1},{2,66},{66,2},{3,67},{67,3},{4,68},{68... | collective-permute-start | bytes 884744 | tf_op jit(solution)/shard_map/ppermute | solution.py:226
  121.6 5.3 %collective-permute-start.1 = (bf16[128,6144]{1,0:T(8,128)(2,1)S(1)}, bf16[128,6144]{1,0:T(8,128)(2,1)S(1)}, u32[]{:S(2)}, u32[]{:S(2)}) collective-permute-start(bf16[128,6144]{1,0:T(8,128)(2,1)S(1)} %bitcast.19), channel_id=1, source_target_pairs={{0,64},{64,0},{1,65},{65,1},{2,66},{66,2},{3,67},{67,3},{4,68},{68... | collective-permute-start | bytes 4718600 | tf_op jit(solution)/shard_map/ppermute | solution.py:233
  136.4 10.5 %copy-start.4 = (f32[16,8]{0,1:T(8,128)S(1)}, f32[16,8]{0,1:T(8,128)}, u32[]{:S(2)}) copy-start(f32[16,8]{0,1:T(8,128)} %param.11) | copy-start | bytes 1540
  136.5 37.3 %copy-start.1 = (bf16[16,8,768]{2,1,0:T(8,128)(2,1)S(1)}, bf16[16,8,768]{2,1,0:T(8,128)(2,1)}, u32[]{:S(2)}) copy-start(bf16[16,8,768]{2,1,0:T(8,128)(2,1)} %param.10) | copy-start | bytes 589828
  137.4 36.1 %all-to-all-start.2 = ((bf16[64,3,768]{2,1,0:T(4,128)(2,1)}), bf16[64,3,768]{2,1,0:T(4,128)(2,1)S(1)}, u32[]{:S(2)}, u32[]{:S(2)}) async-start(bf16[64,3,768]{2,1,0:T(4,128)(2,1)} %reshape.120), calls=%async_computation.2 | async-start | bytes 786432 | tf_op jit(solution)/shard_map/all_to_all | solution.py:239
Sparse Core Ops, SparseCore 0:
  131.1 49.3 reduce-scatter.1

commit v7 on v6

--- a/solution.py
+++ b/solution.py
@@ -19,7 +19,7 @@
 MIB = 1024 * 1024
 
 
-def pick_kernel(home, lane, own, out):
+def pick_kernel(home, lane, source, own, acts, out):
     tokens, held = own.shape
     width = held - LANES
     rows = out.shape[0]
@@ -43,15 +43,27 @@
         block = own[:, width // 2 + start : width // 2 + start + BLOCK]
         total = total + jnp.dot(upper, block, preferred_element_type=F32)
         out[:, width + start : width + start + BLOCK] = total.astype(out.dtype)
-
-
-def pick_rows(home, lane, own, rows):
+    at = lax.broadcasted_iota(jnp.int32, (home.shape[0], acts.shape[0]), 1)
+    pick = jnp.where(at == source[...], 1.0, 0.0).astype(BF16)
+    whole, lower, upper = pick[:rows], pick[rows : 2 * rows], pick[2 * rows :]
+    first = width + width // 2
+    hidden = acts.shape[1]
+    out[:, first : first + hidden] = jnp.dot(
+        whole, acts[...], preferred_element_type=F32
+    ).astype(out.dtype)
+    total = jnp.dot(lower, acts[:, : hidden // 2], preferred_element_type=F32)
+    total = total + jnp.dot(upper, acts[:, hidden // 2 :], preferred_element_type=F32)
+    out[:, first + hidden :] = total.astype(out.dtype)
+
+
+def pick_rows(home, lane, source, own, acts, rows):
     tokens, held = own.shape
     width = held - LANES
+    packed = (width + acts.shape[1]) // 2 * 3
     return pl.pallas_call(
         pick_kernel,
-        out_shape=jax.ShapeDtypeStruct((rows, width + width // 2), BF16),
-        in_specs=[pl.BlockSpec(memory_space=pltpu.VMEM)] * 3,
+        out_shape=jax.ShapeDtypeStruct((rows, packed), BF16),
+        in_specs=[pl.BlockSpec(memory_space=pltpu.VMEM)] * 5,
         out_specs=pl.BlockSpec(memory_space=pltpu.VMEM),
         compiler_params=pltpu.CompilerParams(vmem_limit_bytes=32 * MIB),
         cost_estimate=pl.CostEstimate(
@@ -60,36 +72,59 @@
             transcendentals=0,
         ),
         name="pick_rows",
-    )(home, lane, own)
+    )(home, lane, source, own, acts)
 
 
 def joined(whole, halves):
     return jnp.concatenate([whole[...], halves[...]], axis=0)
 
 
-def weight_kernel(own_a, own_b, pair_a, pair_b, rows_a, rows_b, other_a, other_b, out):
-    left = jnp.concatenate([own_a[...], own_b[...]], axis=1)
-    total = jnp.dot(left, joined(rows_a, rows_b), preferred_element_type=F32)
-    left = jnp.concatenate([pair_a[...], pair_b[...]], axis=1)
-    total = total + jnp.dot(left, joined(other_a, other_b), preferred_element_type=F32)
+def weight_kernel(core, *refs):
+    acts, rows, (out, left_own, left_pair) = refs[:4], refs[4:8], refs[8:]
+    step = pl.program_id(0)
+    slots, hidden = acts[0].shape
+    half = hidden // 2
+
+    @pl.when(step == 0)
+    def _():
+        line = lax.broadcasted_iota(jnp.int32, (slots, slots), 0)
+        at = lax.broadcasted_iota(jnp.int32, (slots, slots), 1)
+        lower = jnp.logical_and(line % 8 < 4, at == line + 4 * core[0])
+        upper = jnp.logical_and(line % 8 >= 4, at == line - 4 + 4 * core[0])
+        pick = jnp.concatenate([lower, upper], axis=0)
+        pick = jnp.where(pick, 1.0, 0.0).astype(BF16)
+        for whole, halves, left in ((acts[0], acts[1], left_own), (acts[2], acts[3], left_pair)):
+            mine = jnp.where(core[0] == 0, whole[:, :half], whole[:, half:])
+            spread = jnp.dot(pick, halves[...], preferred_element_type=F32)
+            both = jnp.concatenate([mine.astype(F32), spread], axis=0)
+            left[...] = jnp.transpose(both).astype(left.dtype)
+
+    late = step >= pl.num_programs(0) // 2
+    total = jnp.zeros(out.shape, F32)
+    for whole, halves, left in ((rows[0], rows[1], left_own), (rows[2], rows[3], left_pair)):
+        side = jnp.where(late, left[:, 2 * slots :], left[:, slots : 2 * slots])
+        side = jnp.concatenate([left[:, :slots], side], axis=1)
+        total = total + jnp.dot(side, joined(whole, halves), preferred_element_type=F32)
     out[...] = total.astype(out.dtype)
 
 
-def weight_term(left_own, left_pair, rows_own, rows_pair):
-    half = left_own.shape[0]
+def weight_term(core, rows_own, rows_pair, width, hidden):
     rows, packed = rows_own.shape
-    width = packed // 3 * 2
     blocks = width // BLOCK
-    left_a = pl.BlockSpec((half, rows), lambda i: (0, 0))
-    left_b = pl.BlockSpec((half, rows), lambda i: (0, 1 + i // (blocks // 2)))
+    half = hidden // 2
+    first = width // 2 * 3
+    acts_a = pl.BlockSpec((rows, hidden), lambda i: (0, first // hidden))
+    acts_b = pl.BlockSpec((rows, half), lambda i: (0, (first + hidden) // half))
     rows_a = pl.BlockSpec((rows, BLOCK), lambda i: (0, i))
     rows_b = pl.BlockSpec((rows, BLOCK), lambda i: (0, blocks + i % (blocks // 2)))
     return pl.pallas_call(
         weight_kernel,
         grid=(blocks,),
         out_shape=jax.ShapeDtypeStruct((half, width), BF16),
-        in_specs=[left_a, left_b, left_a, left_b, rows_a, rows_b, rows_a, rows_b],
+        in_specs=[pl.BlockSpec(memory_space=pltpu.SMEM)]
+        + [acts_a, acts_b, acts_a, acts_b, rows_a, rows_b, rows_a, rows_b],
         out_specs=pl.BlockSpec((half, BLOCK), lambda i: (0, i)),
+        scratch_shapes=[pltpu.VMEM((half, 3 * rows), BF16)] * 2,
         compiler_params=pltpu.CompilerParams(vmem_limit_bytes=49 * MIB),
         cost_estimate=pl.CostEstimate(
             flops=8 * half * rows * width,
@@ -97,7 +132,7 @@
             transcendentals=0,
         ),
         name="weight_term",
-    )(left_own, left_own, left_pair, left_pair, rows_own, rows_own, rows_pair, rows_pair)
+    )(core, *[rows_own] * 2, *[rows_pair] * 2, *[rows_own] * 2, *[rows_pair] * 2)
 
 
 def hidden_kernel(rows_a, rows_b, weight, order, out, total):
@@ -163,10 +198,8 @@
     routed = tok_rows * top_count
     width = out_grad.shape[1]
     hidden = hidden_acts.shape[2]
-    half = hidden // CORES
     experts = X * Z
     slot_count = experts * MOST
-    core = lax.axis_index("core")
     high_at = lax.axis_index("zh")
     swap = [(0, 1), (1, 0)]
 
@@ -189,17 +222,22 @@
 
     own = lax.all_gather(jnp.concatenate([out_grad, table], axis=1), "zh", axis=0, tiled=True)
 
+    line = np.arange(hidden, dtype=np.int32)
+    half = hidden // CORES
+    piece = hidden // (Y * CORES)
+    unit = (((line % half) // piece * CORES + line // half) * piece + line % piece).astype(np.int32)
+    reorder = (unit[:, None] == line[None, :]).astype(BF16)
     gate_half = lax.optimization_barrier(gate_weights.astype(BF16)).astype(F32)
     flat_acts = hidden_acts.reshape(routed, hidden).astype(F32)
     gated = (gate_half.reshape(routed, 1) * flat_acts).astype(BF16)
-    send_acts = jnp.dot(placement, gated, preferred_element_type=F32).astype(BF16)
-    acts_in = lax.all_to_all(
-        send_acts.reshape(experts, MOST, hidden),
-        ("x", "zh", "zl"),
-        split_axis=0,
-        concat_axis=0,
-        tiled=True,
-    ).reshape(slot_count, hidden)
+    gated = lax.dot_general(
+        gated, reorder, (((1,), (1,)), ((), ())), preferred_element_type=F32
+    ).astype(BF16)
+    group = flat_expert // Z * ZL + flat_expert % ZL
+    out_index = (flat_expert // ZL % ZH * (X * ZL) + group) * MOST + position
+    to_planes = (jnp.arange(slot_count, dtype=jnp.int32)[:, None] == out_index[None, :]).astype(BF16)
+    send_acts = jnp.dot(to_planes, gated, preferred_element_type=F32).astype(BF16)
+    acts = lax.all_to_all(send_acts, "zh", split_axis=0, concat_axis=0, tiled=True)
 
     packed = X * ZL * 8
     device, row = np.divmod(np.arange(packed, dtype=np.int32), 8)
@@ -211,28 +249,16 @@
     slot = np.where(used, slot, -1).astype(np.int32)
     order = (jnp.arange(slot_count, dtype=jnp.int32)[:, None] == slot[None, :]).astype(BF16)
 
-    line = np.arange(hidden, dtype=np.int32)
-    piece = hidden // (Y * CORES)
-    unit = (((line % half) // piece * CORES + line // half) * piece + line % piece).astype(np.int32)
-    reorder = (unit[:, None] == line[None, :]).astype(BF16)
-    acts_rows = lax.dot_general(
-        order, acts_in, (((0,), (0,)), ((), ())), preferred_element_type=F32
-    ).astype(BF16)
-    left = lax.dot_general(
-        reorder, acts_rows, (((1,), (1,)), ((), ())), preferred_element_type=F32
-    ).astype(BF16)
-    left_own = lax.dynamic_slice_in_dim(left, core * half, half, 0)
-    left_away = lax.dynamic_slice_in_dim(left, (1 - core) * half, half, 0)
-    left_pair = lax.ppermute(left_away, "core", swap)
-
     home = np.where(used, high * tok_rows + device % ZL, -tok_rows).astype(np.int32)[:, None]
     lane = (device // ZL * MOST + rank).astype(np.int32)[:, None]
-    picked = pick_rows(home + high_at * ZL, lane, own, packed)
+    source = np.where(used, (high * (X * ZL) + device) * MOST + rank, -1).astype(np.int32)[:, None]
+    picked = pick_rows(home + high_at * ZL, lane, source, own, acts, packed)
     rows = lax.all_to_all(picked, ("x", "zl"), split_axis=0, concat_axis=0, tiled=True)
-    rows, left_own, left_pair = lax.optimization_barrier((rows, left_own, left_pair))
-    rows_pair = lax.ppermute(rows, "core", swap)
-
-    part = weight_term(left_own, left_pair, rows, rows_pair)
+    rows, order = lax.optimization_barrier((rows, order))
+    rows_pair = lax.ppermute(rows, "core", [(0, 1), (1, 0)])
+
+    core = lax.axis_index("core").astype(jnp.int32).reshape(1)
+    part = weight_term(core, rows, rows_pair, out_grad.shape[1], hidden)
     summed = lax.psum_scatter(part, "y", scatter_dimension=0, tiled=True)
 
     grad_hidden = hidden_term(rows, down_weight, order)

time: 188 us -> 192 us (1.021)
  waiting for transfers between devices: 62.8 us -> 77.4 us
  starting transfers between devices: 44.1 us -> 37.1 us
  blocking collectives: 44.1 us -> 40.7 us
    all_to_all x1, waiting for transfers between devices: 26.8 us -> 42.4 us  [shards(): lax.all_to_all(picked, ('x', 'zl'), split_axis=0, concat_axis=0, tiled=True)]
    all_to_all x1, starting transfers between devices: 22.6 us -> 18.7 us  [shards(): lax.all_to_all(send_acts, 'zh', split_axis=0, concat_axis=0, tiled=True)]
    all_gather x1, blocking collectives: 44.1 us -> 40.7 us  [shards(): lax.all_gather(jnp.concatenate([out_grad, table], axis=1), 'zh', axis=0,...]
    ppermute x2 -> x1, waiting for transfers between devices: 4.92 us -> 3.92 us  [shards(): rows_pair = lax.ppermute(rows, 'core', [(0, 1), (1, 0)])]
  transfers between devices with their start and end apart: 6 -> 5, of which waited for: 5 -> 4; matrix products, arithmetic and copies ran while one was open for 3% -> 2% of each run, Pallas kernels for 4% -> 3%
where the time goes in v7:
time: 192 us
  waiting for transfers between devices  77.4 us (40%)
  blocking collectives  40.7 us (21%)
  starting transfers between devices  37.1 us (19%)
  between operations  14.2 us (7%)
  Pallas kernels  12.7 us (7%)
  matrix products  4.35 us (2%)
  local copies, waits for them, and re-layouts  4.29 us (2%)
    all_to_all x1, waiting for transfers between devices, shards(): lax.all_to_all(picked, ('x', 'zl'), split_axis=0, concat_axis=0, tiled=True)  42.4 us
    all_gather x1, blocking collectives, shards(): lax.all_gather(jnp.concatenate([out_grad, table], axis=1), 'zh', axis=0,...  40.7 us
    all_to_all x1, waiting for transfers between devices, shards(): lax.all_to_all(grad_hidden.reshape(experts, MOST, hidden), ('x', 'zh', 'z...  26.4 us
    all_to_all x1, starting transfers between devices, shards(): lax.all_to_all(send_acts, 'zh', split_axis=0, concat_axis=0, tiled=True)  18.7 us
    all_to_all x1, starting transfers between devices, shards(): lax.all_to_all(grad_hidden.reshape(experts, MOST, hidden), ('x', 'zh', 'z...  9.17 us
    all_to_all x1, starting transfers between devices, shards(): lax.all_to_all(picked, ('x', 'zl'), split_axis=0, concat_axis=0, tiled=True)  7.24 us
    pallas_call x1, Pallas kernels, weight_term(): pl.pallas_call(weight_kernel, grid=(blocks,), out_shape=jax.ShapeDtypeStr...  5.74 us
    pallas_call x1, Pallas kernels, hidden_term(): pl.pallas_call(hidden_kernel, grid=(blocks,), out_shape=jax.ShapeDtypeStr...  5.64 us
  transfers between devices with their start and end apart: 5, of which 4 were waited for; matrix products, arithmetic and copies ran while one was open for 2% of the time, Pallas kernels for 3%

profile of v7, /device:TPU:6, one launch (start us, length us, event | category | flops | bytes accessed | tf_op | source)
XLA Modules:
  0.0 191.8 jit_solution(154904783805912237)
XLA Ops:
  7.2 0.0 copy-start.4
  7.2 0.0 copy-start.5
  7.2 0.8 convert_element_type.74
  7.9 0.1 copy.23
  8.0 0.1 reshape.198
  8.1 0.8 copy.24
  8.9 0.1 reshape.193
  9.0 0.2 fusion
  9.2 0.0 copy-start.1
  9.2 0.0 copy-start.2
  9.2 2.9 %convolution_convert_fusion = bf16[192,768]{1,0:T(8,128)(2,1)} fusion(bf16[768,768]{1,0:T(8,128)(2,1)} %constant.93.clone, bf16[16,8,768]{2,1,0:T(8,128)(2,1)} %param.11, f32[128]{0:T(128)S(1)} %reshape.198, s32[128]{0:T(128)S(1)} %get-tuple-element.16), kind=kOutput, calls=%fused_computation | convolution fusion | flops 189308928 | bytes 1672192 | tf_op jit(solution)/shard_map/dot_general | solution.py:239
  12.1 18.7 %all-to-all-start = ((bf16[4,48,768]{2,1,0:T(8,128)(2,1)}), bf16[4,48,768]{2,1,0:T(8,128)(2,1)S(1)}, u32[]{:S(2)}, u32[]{:S(2)}) async-start(bf16[4,48,768]{2,1,0:T(8,128)(2,1)} %bitcast.1), calls=%async_computation | async-start | bytes 589824 | tf_op jit(solution)/shard_map/all_to_all | solution.py:240
  30.8 0.2 convolution_convert_fusion.2
  31.1 0.0 copy-done.5
  31.1 40.7 %all_gather.3.own = bf16[64,4224]{1,0:T(8,128)(2,1)S(1)} all-gather(bf16[16,4224]{1,0:T(8,128)(2,1)S(1)} %pad_maximum_fusion), channel_id=1, replica_groups=mesh['y'=8,'core'=2,'x'=4,'zh'=4,'zl'=4] {'zh'}, dimensions={0}, use_global_device_ids=true | all-gather | bytes 675840 | tf_op jit(solution)/shard_map/all_gather | solution.py:223
  71.8 0.0 copy-done.4
  71.8 0.0 all-to-all-done
  71.8 0.0 copy-done.1
  71.8 0.0 copy-done.2
  71.8 1.3 pick_rows.1
  73.2 0.0 copy-start
  73.2 1.3 copy-done
  74.4 0.0 copy-start.7
  74.4 7.2 %all-to-all-start.1 = ((bf16[16,8,7296]{2,1,0:T(8,128)(2,1)}), bf16[16,8,7296]{2,1,0:T(8,128)(2,1)S(1)}, u32[]{:S(2)}, u32[]{:S(2)}) async-start(bf16[16,8,7296]{2,1,0:T(8,128)(2,1)} %bitcast.25), calls=%async_computation.1 | async-start | bytes 3735552 | tf_op jit(solution)/shard_map/all_to_all | solution.py:256
  81.7 0.0 reduce-scatter.2.cloned.1.call-start
  81.7 0.0 copy-done.7
  81.8 42.4 %all-to-all-done.1 = bf16[16,8,7296]{2,1,0:T(8,128)(2,1)S(1)} async-done(((bf16[16,8,7296]{2,1,0:T(8,128)(2,1)}), bf16[16,8,7296]{2,1,0:T(8,128)(2,1)S(1)}, u32[]{:S(2)}, u32[]{:S(2)}) %all-to-all-start.1) | async-done | bytes 1867808 | tf_op jit(solution)/shard_map/all_to_all | solution.py:256
  124.2 1.9 collective-permute-start
  126.1 3.9 %collective-permute-done.refs_2_.refs_3_.refs_6_.refs_7_ = bf16[128,7296]{1,0:T(8,128)(2,1)} collective-permute-done((bf16[128,7296]{1,0:T(8,128)(2,1)S(1)}, bf16[128,7296]{1,0:T(8,128)(2,1)}, u32[]{:S(2)}, u32[]{:S(2)}) %collective-permute-start) | collective-permute-done | bytes 1867808 | tf_op jit(solution)/shard_map/ppermute | solution.py:258
  130.1 5.7 %weight_term.1 = bf16[384,4096]{1,0:T(8,128)(2,1)} custom-call(s32[1]{0:T(128)} %bitcast.7.core, bf16[128,7296]{1,0:T(8,128)(2,1)S(1)} %bitcast.19, bf16[128,7296]{1,0:T(8,128)(2,1)S(1)} %bitcast.20, bf16[128,7296]{1,0:T(8,128)(2,1)} %collective-permute-done.refs_2_.refs_3_.refs_6_.refs_7_, ...), custom_call_target="tpu_custom_call" | custom-call | flops 1610612736 | bytes 6881280 | tf_op jit(solution)/shard_map/weight_term/pallas_call | solution.py:120
  135.8 0.0 reduce-scatter.2.cloned.1.call-update
  135.8 0.0 copy-start.6
  135.8 5.6 %hidden_term.1 = bf16[192,768]{1,0:T(8,128)(2,1)S(1)} custom-call(bf16[128,7296]{1,0:T(8,128)(2,1)S(1)} %bitcast.23, bf16[128,7296]{1,0:T(8,128)(2,1)S(1)} %bitcast.24, bf16[1,768,4096]{2,1,0:T(8,128)(2,1)} %weight.1, bf16[192,384]{1,0:T(8,128)(2,1)S(1)} %fusion.3.order), custom_call_target="tpu_custom_call" | custom-call | flops 1610612736 | bytes 8683520 | tf_op jit(solution)/shard_map/hidden_term/pallas_call | solution.py:174
  141.5 0.0 copy-start.3
  141.5 0.9 reshape.194
  142.4 9.2 %all-to-all-start.2 = ((bf16[64,3,768]{2,1,0:T(4,128)(2,1)}), bf16[64,3,768]{2,1,0:T(4,128)(2,1)S(1)}, u32[]{:S(2)}, u32[]{:S(2)}) async-start(bf16[64,3,768]{2,1,0:T(4,128)(2,1)} %reshape.194), calls=%async_computation.2 | async-start | bytes 786432 | tf_op jit(solution)/shard_map/all_to_all | solution.py:265
  151.6 0.0 copy-done.6
  151.6 0.1 copy.27
  151.7 26.4 %all-to-all-done.2 = bf16[64,3,768]{2,1,0:T(4,128)(2,1)S(1)} async-done(((bf16[64,3,768]{2,1,0:T(4,128)(2,1)}), bf16[64,3,768]{2,1,0:T(4,128)(2,1)S(1)}, u32[]{:S(2)}, u32[]{:S(2)}) %all-to-all-start.2) | async-done | bytes 294944 | tf_op jit(solution)/shard_map/all_to_all | solution.py:265
  178.1 0.2 reshape.195
  178.3 0.0 copy-done.3
  178.3 1.0 fusion.2
  179.4 0.1 reshape.200
  179.5 0.1 multiply_reduce_fusion
  179.6 0.1 subtract_multiply_fusion
  179.7 0.7 copy.28
  180.3 4.6 %reduce-scatter.2.cloned.1.call-done = bf16[48,4096]{1,0:T(8,128)(2,1)} async-done(((bf16[384,4096]{1,0:T(8,128)(2,1)}), bf16[48,4096]{1,0:T(8,128)(2,1)}) %reduce-scatter.2.cloned.1.call-update) | async-done | bytes 393232 | tf_op jit(solution)/shard_map/reduce_scatter | solution.py:262
  (5 shorter events, 0.1 us)
Async XLA Ops:
  7.2 64.6 %copy-start.4 = (s32[384,1]{1,0:T(8,128)S(1)}, s32[384,1]{1,0:T(8,128)}, u32[]{:S(2)}) copy-start(s32[384,1]{1,0:T(8,128)} %constant.95.clone) | copy-start | bytes 4612
  7.2 23.9 %copy-start.5 = (bf16[16,4096]{1,0:T(8,128)(2,1)S(1)}, bf16[16,4096]{1,0:T(8,128)(2,1)}, u32[]{:S(2)}) copy-start(bf16[16,4096]{1,0:T(8,128)(2,1)} %param.10) | copy-start | bytes 393220
  9.2 62.6 %copy-start.1 = (s32[384,1]{1,0:T(8,128)S(1)}, s32[384,1]{1,0:T(8,128)}, u32[]{:S(2)}) copy-start(s32[384,1]{1,0:T(8,128)} %constant.97.clone.source) | copy-start | bytes 4612
  9.2 62.6 %copy-start.2 = (s32[384,1]{1,0:T(8,128)S(1)}, s32[384,1]{1,0:T(8,128)}, u32[]{:S(2)}) copy-start(s32[384,1]{1,0:T(8,128)} %constant.96.clone.lane) | copy-start | bytes 4612
  12.1 59.7 %all-to-all-start = ((bf16[4,48,768]{2,1,0:T(8,128)(2,1)}), bf16[4,48,768]{2,1,0:T(8,128)(2,1)S(1)}, u32[]{:S(2)}, u32[]{:S(2)}) async-start(bf16[4,48,768]{2,1,0:T(8,128)(2,1)} %bitcast.1), calls=%async_computation | async-start | bytes 589824 | tf_op jit(solution)/shard_map/all_to_all | solution.py:240
  73.2 1.3 copy-start
  74.4 7.3 %copy-start.7 = (s32[384]{0:T(512)S(1)}, s32[384]{0:T(512)}, u32[]{:S(2)}) copy-start(s32[384]{0:T(512)} %constant.103) | copy-start | bytes 4612
  74.4 49.8 %all-to-all-start.1 = ((bf16[16,8,7296]{2,1,0:T(8,128)(2,1)}), bf16[16,8,7296]{2,1,0:T(8,128)(2,1)S(1)}, u32[]{:S(2)}, u32[]{:S(2)}) async-start(bf16[16,8,7296]{2,1,0:T(8,128)(2,1)} %bitcast.25), calls=%async_computation.1 | async-start | bytes 3735552 | tf_op jit(solution)/shard_map/all_to_all | solution.py:256
  81.7 103.3 %reduce-scatter.2.cloned.1.call-start = ((), (), s32[]{:S(2)}) async-start(), calls=%async_computation.4 | async-start | bytes 3538944 | tf_op jit(solution)/shard_map/reduce_scatter | solution.py:262
  124.2 5.8 %collective-permute-start = (bf16[128,7296]{1,0:T(8,128)(2,1)S(1)}, bf16[128,7296]{1,0:T(8,128)(2,1)}, u32[]{:S(2)}, u32[]{:S(2)}) collective-permute-start(bf16[128,7296]{1,0:T(8,128)(2,1)S(1)} %bitcast.18), channel_id=1, source_target_pairs={{0,64},{64,0},{1,65},{65,1},{2,66},{66,2},{3,67},{67,3},{4,68},{68... | collective-permute-start | bytes 5603336 | tf_op jit(solution)/shard_map/ppermute | solution.py:258
  135.8 15.7 %copy-start.6 = (f32[16,8]{0,1:T(8,128)S(1)}, f32[16,8]{0,1:T(8,128)}, u32[]{:S(2)}) copy-start(f32[16,8]{0,1:T(8,128)} %param.12) | copy-start | bytes 1540
  141.5 36.8 %copy-start.3 = (bf16[16,8,768]{2,1,0:T(8,128)(2,1)S(1)}, bf16[16,8,768]{2,1,0:T(8,128)(2,1)}, u32[]{:S(2)}) copy-start(bf16[16,8,768]{2,1,0:T(8,128)(2,1)} %param.11) | copy-start | bytes 589828
  142.4 35.7 %all-to-all-start.2 = ((bf16[64,3,768]{2,1,0:T(4,128)(2,1)}), bf16[64,3,768]{2,1,0:T(4,128)(2,1)S(1)}, u32[]{:S(2)}, u32[]{:S(2)}) async-start(bf16[64,3,768]{2,1,0:T(4,128)(2,1)} %reshape.194), calls=%async_computation.2 | async-start | bytes 786432 | tf_op jit(solution)/shard_map/all_to_all | solution.py:265
Sparse Core Ops, SparseCore 0:
  136.0 48.9 reduce-scatter.1

commit v8 on v6

--- a/solution.py
+++ b/solution.py
@@ -14,6 +14,7 @@
 Z = ZH * ZL
 LANES = 128
 BLOCK = 1024
+SHIFT = 2
 BF16 = jnp.bfloat16
 F32 = jnp.float32
 MIB = 1024 * 1024
@@ -167,7 +168,8 @@
     experts = X * Z
     slot_count = experts * MOST
     core = lax.axis_index("core")
-    high_at = lax.axis_index("zh")
+    z_at = lax.axis_index(("zh", "zl"))
+    shift = core * SHIFT
     swap = [(0, 1), (1, 0)]
 
     flat_expert = expert_idx.reshape(routed)
@@ -207,8 +209,9 @@
     used = np.concatenate([row >= 0, row < 4, row >= 4])
     device = np.tile(device, 3)
     high, rank = np.divmod(entry, MOST)
-    slot = device // ZL * (Z * MOST) + (high * ZL + device % ZL) * MOST + rank
-    slot = np.where(used, slot, -1).astype(np.int32)
+    across, along = np.divmod(device, ZL)
+    slot = across * (Z * MOST) + (high * ZL + (along + shift) % ZL) * MOST + rank
+    slot = jnp.where(used, slot, -1)
     order = (jnp.arange(slot_count, dtype=jnp.int32)[:, None] == slot[None, :]).astype(BF16)
 
     line = np.arange(hidden, dtype=np.int32)
@@ -225,10 +228,24 @@
     left_away = lax.dynamic_slice_in_dim(left, (1 - core) * half, half, 0)
     left_pair = lax.ppermute(left_away, "core", swap)
 
-    home = np.where(used, high * tok_rows + device % ZL, -tok_rows).astype(np.int32)[:, None]
-    lane = (device // ZL * MOST + rank).astype(np.int32)[:, None]
-    picked = pick_rows(home + high_at * ZL, lane, own, packed)
-    rows = lax.all_to_all(picked, ("x", "zl"), split_axis=0, concat_axis=0, tiled=True)
+    start = (z_at + Z - shift) // ZL * ZL + shift
+    plane = (start + along[:, None]) % Z
+    home = jnp.where(used[:, None], (high * tok_rows)[:, None] + plane, -tok_rows)
+    lane = (across * MOST + rank).astype(np.int32)[:, None]
+    picked = pick_rows(home.astype(jnp.int32), lane, own, packed)
+    lines = [
+        [(c * X + x) * Z + (k * ZL + c * SHIFT + m) % Z for x in range(X) for m in range(ZL)]
+        for c in range(CORES)
+        for k in range(ZH)
+    ]
+    rows = lax.all_to_all(
+        picked,
+        ("core", "x", "zh", "zl"),
+        split_axis=0,
+        concat_axis=0,
+        axis_index_groups=lines,
+        tiled=True,
+    )
     rows, left_own, left_pair = lax.optimization_barrier((rows, left_own, left_pair))
     rows_pair = lax.ppermute(rows, "core", swap)
 

time: 188 us -> 180 us (0.957)
  waiting for transfers between devices: 62.8 us -> 52.9 us
  starting transfers between devices: 44.1 us -> 46.2 us
    all_to_all x1, waiting for transfers between devices: 26.8 us -> 17.2 us  [shards(): lax.all_to_all(picked, ('core', 'x', 'zh', 'zl'), split_axis=0, concat_ax...]
where the time goes in v8:
time: 180 us
  waiting for transfers between devices  52.9 us (29%)
  starting transfers between devices  46.2 us (26%)
  blocking collectives  44.1 us (24%)
  between operations  14.3 us (8%)
  Pallas kernels  11.8 us (7%)
  matrix products  4.94 us (3%)
  local copies, waits for them, and re-layouts  4.29 us (2%)
    all_gather x1, blocking collectives, shards(): lax.all_gather(jnp.concatenate([out_grad, table], axis=1), 'zh', axis=0,...  44.1 us
    all_to_all x1, waiting for transfers between devices, shards(): lax.all_to_all(grad_hidden.reshape(experts, MOST, hidden), ('x', 'zh', 'z...  26.4 us
    all_to_all x1, starting transfers between devices, shards(): lax.all_to_all(send_acts.reshape(experts, MOST, hidden), ('x', 'zh', 'zl'...  22.6 us
    all_to_all x1, waiting for transfers between devices, shards(): lax.all_to_all(picked, ('core', 'x', 'zh', 'zl'), split_axis=0, concat_ax...  17.2 us
    all_to_all x1, starting transfers between devices, shards(): lax.all_to_all(grad_hidden.reshape(experts, MOST, hidden), ('x', 'zh', 'z...  10.6 us
    all_to_all x1, starting transfers between devices, shards(): lax.all_to_all(picked, ('core', 'x', 'zh', 'zl'), split_axis=0, concat_ax...  8 us
    pallas_call x1, Pallas kernels, hidden_term(): pl.pallas_call(hidden_kernel, grid=(blocks,), out_shape=jax.ShapeDtypeStr...  5.47 us
    reduce_scatter x1, waiting for transfers between devices, shards(): summed = lax.psum_scatter(part, 'y', scatter_dimension=0, tiled=True)  4.67 us
  transfers between devices with their start and end apart: 6, of which 5 were waited for; matrix products, arithmetic and copies ran while one was open for 3% of the time, Pallas kernels for 4%

profile of v8, /device:TPU:6, one launch (start us, length us, event | category | flops | bytes accessed | tf_op | source)
XLA Modules:
  0.0 179.6 jit_solution(980666021116344346)
XLA Ops:
  7.2 0.8 copy.25
  8.0 0.1 reshape.118
  8.1 0.2 fusion
  8.3 0.7 convert_element_type.74
  8.9 0.1 copy.24
  9.0 0.1 reshape.124
  9.1 1.2 convolution_convert_fusion.2
  10.4 0.0 copy-start.2
  10.4 0.0 copy-start.3
  10.4 0.0 copy-start.5
  10.4 0.9 reshape.119
  11.3 22.6 %all-to-all-start.1 = ((bf16[64,3,768]{2,1,0:T(4,128)(2,1)}), bf16[64,3,768]{2,1,0:T(4,128)(2,1)S(1)}, u32[]{:S(2)}, u32[]{:S(2)}) async-start(bf16[64,3,768]{2,1,0:T(4,128)(2,1)} %reshape.119), calls=%async_computation.1 | async-start | bytes 786432 | tf_op jit(solution)/shard_map/all_to_all | solution.py:198
  33.9 0.2 convolution_convert_fusion.3
  34.1 44.1 %all_gather.3.own = bf16[64,4224]{1,0:T(8,128)(2,1)S(1)} all-gather(bf16[16,4224]{1,0:T(8,128)(2,1)S(1)} %pad_maximum_fusion), channel_id=1, replica_groups=mesh['y'=8,'core'=2,'x'=4,'zh'=4,'zl'=4] {'zh'}, dimensions={0}, use_global_device_ids=true | all-gather | bytes 675840 | tf_op jit(solution)/shard_map/all_gather | solution.py:192
  78.3 0.0 copy-done.2
  78.3 0.0 copy-done.5
  78.3 0.1 fusion.5.home
  78.4 2.4 %pick_rows.1 = bf16[128,6144]{1,0:T(8,128)(2,1)} custom-call(s32[384,1]{1,0:T(8,128)S(1)} %fusion.5.home, s32[384,1]{1,0:T(8,128)S(1)} %copy-done, bf16[64,4224]{1,0:T(8,128)(2,1)S(1)} %all_gather.3.own), custom_call_target="tpu_custom_call" | custom-call | flops 134217728 | bytes 2621440 | tf_op jit(solution)/shard_map/pick_rows/pallas_call | solution.py:52
  80.8 0.0 all-to-all-done.1
  80.8 0.0 copy-start.10
  80.8 8.0 %all-to-all-start = ((bf16[16,8,6144]{2,1,0:T(8,128)(2,1)}), bf16[16,8,6144]{2,1,0:T(8,128)(2,1)S(1)}, u32[]{:S(2)}, u32[]{:S(2)}) async-start(bf16[16,8,6144]{2,1,0:T(8,128)(2,1)} %bitcast), calls=%async_computation | async-start | bytes 3145728 | tf_op jit(solution)/shard_map/all_to_all | solution.py:241
  88.8 0.0 reduce-scatter.2.cloned.1.call-start
  88.9 0.0 copy-done.7
  88.9 0.0 copy-done.8
  88.9 0.3 reshape.120
  89.2 2.3 %convolution_convert_fusion = bf16[384,768]{0,1:T(8,128)(2,1)S(1)} fusion(bf16[768,768]{1,0:T(8,128)(2,1)} %constant.125.clone, bf16[192,768]{1,0:T(8,128)(2,1)S(1)} %reshape.120, s32[384]{0:T(512)S(1)} %fusion.25), kind=kOutput, calls=%fused_computation | convolution fusion | flops 566894592 | bytes 2065920 | tf_op jit(solution)/shard_map/dot_general | solution.py:224
  91.5 0.1 dynamic-slice_bitcast_fusion
  91.5 1.9 %collective-permute-start = (bf16[384,384]{1,0:T(8,128)(2,1)S(1)}, bf16[384,384]{1,0:T(8,128)(2,1)S(1)}, u32[]{:S(2)}, u32[]{:S(2)}) collective-permute-start(bf16[384,384]{1,0:T(8,128)(2,1)S(1)} %get-tuple-element.15), channel_id=1, source_target_pairs={{0,64},{64,0},{1,65},{65,1},{2,66},{66,2},{3,67},{67,3},{4,68},{68... | collective-permute-start | bytes 884744 | tf_op jit(solution)/shard_map/ppermute | solution.py:229
  93.5 1.5 collective-permute-done.pair_a.pair_b
  95.0 17.2 %all-to-all-done = bf16[16,8,6144]{2,1,0:T(8,128)(2,1)S(1)} async-done(((bf16[16,8,6144]{2,1,0:T(8,128)(2,1)}), bf16[16,8,6144]{2,1,0:T(8,128)(2,1)S(1)}, u32[]{:S(2)}, u32[]{:S(2)}) %all-to-all-start) | async-done | bytes 1572896 | tf_op jit(solution)/shard_map/all_to_all | solution.py:241
  112.3 3.0 %collective-permute-start.1 = (bf16[128,6144]{1,0:T(8,128)(2,1)S(1)}, bf16[128,6144]{1,0:T(8,128)(2,1)S(1)}, u32[]{:S(2)}, u32[]{:S(2)}) collective-permute-start(bf16[128,6144]{1,0:T(8,128)(2,1)S(1)} %bitcast.19), channel_id=1, source_target_pairs={{0,64},{64,0},{1,65},{65,1},{2,66},{66,2},{3,67},{67,3},{4,68},{68... | collective-permute-start | bytes 4718600 | tf_op jit(solution)/shard_map/ppermute | solution.py:250
  115.3 3.0 %collective-permute-done.1.other_a.other_b = bf16[128,6144]{1,0:T(8,128)(2,1)S(1)} collective-permute-done((bf16[128,6144]{1,0:T(8,128)(2,1)S(1)}, bf16[128,6144]{1,0:T(8,128)(2,1)S(1)}, u32[]{:S(2)}, u32[]{:S(2)}) %collective-permute-start.1) | collective-permute-done | bytes 1572896 | tf_op jit(solution)/shard_map/ppermute | solution.py:250
  118.3 4.0 %weight_term.1 = bf16[384,4096]{1,0:T(8,128)(2,1)} custom-call(bf16[384,384]{1,0:T(8,128)(2,1)S(1)} %get-tuple-element.7.own_a.own_b, bf16[384,384]{1,0:T(8,128)(2,1)S(1)} %get-tuple-element.7.own_a.own_b, bf16[384,384]{1,0:T(8,128)(2,1)S(1)} %collective-permute-done.pair_a.pair_b, bf16[384,384]{1,0:T(8,128)(2,1)S(1)} %collective-permute-done.pair_a.pair_b, ...), custom_call_target="tpu_custom_call" | custom-call | flops 1610612736 | bytes 6291456 | tf_op jit(solution)/shard_map/weight_term/pallas_call | solution.py:88
  122.3 0.0 reduce-scatter.2.cloned.1.call-update
  122.4 5.5 %hidden_term.1 = bf16[192,768]{1,0:T(8,128)(2,1)S(1)} custom-call(bf16[128,6144]{1,0:T(8,128)(2,1)S(1)} %bitcast.22, bf16[128,6144]{1,0:T(8,128)(2,1)S(1)} %bitcast.23, bf16[1,768,4096]{2,1,0:T(8,128)(2,1)} %weight.1, bf16[192,384]{1,0:T(8,128)(2,1)S(1)} %fusion.3.order), custom_call_target="tpu_custom_call" | custom-call | flops 1610612736 | bytes 8683520 | tf_op jit(solution)/shard_map/hidden_term/pallas_call | solution.py:140
  127.8 0.0 copy-start.6
  127.9 0.0 copy-start.1
  127.9 0.9 reshape.121
  128.8 10.6 %all-to-all-start.2 = ((bf16[64,3,768]{2,1,0:T(4,128)(2,1)}), bf16[64,3,768]{2,1,0:T(4,128)(2,1)S(1)}, u32[]{:S(2)}, u32[]{:S(2)}) async-start(bf16[64,3,768]{2,1,0:T(4,128)(2,1)} %reshape.121), calls=%async_computation.2 | async-start | bytes 786432 | tf_op jit(solution)/shard_map/all_to_all | solution.py:256
  139.4 0.1 copy.28
  139.4 26.4 %all-to-all-done.2 = bf16[64,3,768]{2,1,0:T(4,128)(2,1)S(1)} async-done(((bf16[64,3,768]{2,1,0:T(4,128)(2,1)}), bf16[64,3,768]{2,1,0:T(4,128)(2,1)S(1)}, u32[]{:S(2)}, u32[]{:S(2)}) %all-to-all-start.2) | async-done | bytes 294944 | tf_op jit(solution)/shard_map/all_to_all | solution.py:256
  165.9 0.2 reshape.122
  166.1 1.0 fusion.2
  167.2 0.1 reshape.126
  167.3 0.1 multiply_reduce_fusion
  167.4 0.1 subtract_multiply_fusion
  167.4 0.7 copy.29
  168.1 4.7 %reduce-scatter.2.cloned.1.call-done = bf16[48,4096]{1,0:T(8,128)(2,1)} async-done(((bf16[384,4096]{1,0:T(8,128)(2,1)}), bf16[48,4096]{1,0:T(8,128)(2,1)}) %reduce-scatter.2.cloned.1.call-update) | async-done | bytes 393232 | tf_op jit(solution)/shard_map/reduce_scatter | solution.py:253
  (16 shorter events, 0.1 us)
Async XLA Ops:
  7.2 26.9 %copy-start.4 = (bf16[16,4096]{1,0:T(8,128)(2,1)S(1)}, bf16[16,4096]{1,0:T(8,128)(2,1)}, u32[]{:S(2)}) copy-start(bf16[16,4096]{1,0:T(8,128)(2,1)} %param.15) | copy-start | bytes 393220
  10.4 67.9 %copy-start.2 = (s32[384,1]{1,0:T(8,128)S(1)}, s32[384,1]{1,0:T(8,128)}, u32[]{:S(2)}) copy-start(s32[384,1]{1,0:T(8,128)} %constant.126.clone) | copy-start | bytes 4612
  10.4 67.9 %copy-start.3 = (s32[384,1]{1,0:T(8,128)S(1)}, s32[384,1]{1,0:T(8,128)}, u32[]{:S(2)}) copy-start(s32[384,1]{1,0:T(8,128)} %constant.127.clone) | copy-start | bytes 4612
  10.4 67.9 %copy-start.5 = (pred[384,1]{1,0:T(32,128)(4,1)S(1)}, pred[384,1]{1,0:T(32,128)(4,1)}, u32[]{:S(2)}) copy-start(pred[384,1]{1,0:T(32,128)(4,1)} %constant.128.clone) | copy-start | bytes 1156
  11.3 67.1 %copy-start = (s32[384,1]{1,0:T(8,128)S(1)}, s32[384,1]{1,0:T(8,128)}, u32[]{:S(2)}) copy-start(s32[384,1]{1,0:T(8,128)} %constant.129.clone.lane) | copy-start | bytes 4612
  11.3 69.5 %all-to-all-start.1 = ((bf16[64,3,768]{2,1,0:T(4,128)(2,1)}), bf16[64,3,768]{2,1,0:T(4,128)(2,1)S(1)}, u32[]{:S(2)}, u32[]{:S(2)}) async-start(bf16[64,3,768]{2,1,0:T(4,128)(2,1)} %reshape.119), calls=%async_computation.1 | async-start | bytes 786432 | tf_op jit(solution)/shard_map/all_to_all | solution.py:198
  80.8 8.1 %copy-start.7 = (s32[384]{0:T(512)S(1)}, s32[384]{0:T(512)}, u32[]{:S(2)}) copy-start(s32[384]{0:T(512)} %constant.120.clone) | copy-start | bytes 4612
  80.8 8.1 %copy-start.8 = (s32[384]{0:T(512)S(1)}, s32[384]{0:T(512)}, u32[]{:S(2)}) copy-start(s32[384]{0:T(512)} %constant.121.clone) | copy-start | bytes 4612
  80.8 8.1 %copy-start.9 = (s32[384]{0:T(512)S(1)}, s32[384]{0:T(512)}, u32[]{:S(2)}) copy-start(s32[384]{0:T(512)} %constant.135) | copy-start | bytes 4612
  80.8 8.1 %copy-start.10 = (pred[384]{0:T(512)(128)(4,1)S(1)}, pred[384]{0:T(512)(128)(4,1)}, u32[]{:S(2)}) copy-start(pred[384]{0:T(512)(128)(4,1)} %constant.124.clone) | copy-start | bytes 1156
  80.8 31.5 %all-to-all-start = ((bf16[16,8,6144]{2,1,0:T(8,128)(2,1)}), bf16[16,8,6144]{2,1,0:T(8,128)(2,1)S(1)}, u32[]{:S(2)}, u32[]{:S(2)}) async-start(bf16[16,8,6144]{2,1,0:T(8,128)(2,1)} %bitcast), calls=%async_computation | async-start | bytes 3145728 | tf_op jit(solution)/shard_map/all_to_all | solution.py:241
  88.8 84.0 %reduce-scatter.2.cloned.1.call-start = ((), (), s32[]{:S(2)}) async-start(), calls=%async_computation.4 | async-start | bytes 3538944 | tf_op jit(solution)/shard_map/reduce_scatter | solution.py:253
  91.5 3.5 %collective-permute-start = (bf16[384,384]{1,0:T(8,128)(2,1)S(1)}, bf16[384,384]{1,0:T(8,128)(2,1)S(1)}, u32[]{:S(2)}, u32[]{:S(2)}) collective-permute-start(bf16[384,384]{1,0:T(8,128)(2,1)S(1)} %get-tuple-element.15), channel_id=1, source_target_pairs={{0,64},{64,0},{1,65},{65,1},{2,66},{66,2},{3,67},{67,3},{4,68},{68... | collective-permute-start | bytes 884744 | tf_op jit(solution)/shard_map/ppermute | solution.py:229
  112.3 6.1 %collective-permute-start.1 = (bf16[128,6144]{1,0:T(8,128)(2,1)S(1)}, bf16[128,6144]{1,0:T(8,128)(2,1)S(1)}, u32[]{:S(2)}, u32[]{:S(2)}) collective-permute-start(bf16[128,6144]{1,0:T(8,128)(2,1)S(1)} %bitcast.19), channel_id=1, source_target_pairs={{0,64},{64,0},{1,65},{65,1},{2,66},{66,2},{3,67},{67,3},{4,68},{68... | collective-permute-start | bytes 4718600 | tf_op jit(solution)/shard_map/ppermute | solution.py:250
  127.8 11.5 %copy-start.6 = (f32[16,8]{0,1:T(8,128)S(1)}, f32[16,8]{0,1:T(8,128)}, u32[]{:S(2)}) copy-start(f32[16,8]{0,1:T(8,128)} %param.17) | copy-start | bytes 1540
  127.9 38.3 %copy-start.1 = (bf16[16,8,768]{2,1,0:T(8,128)(2,1)S(1)}, bf16[16,8,768]{2,1,0:T(8,128)(2,1)}, u32[]{:S(2)}) copy-start(bf16[16,8,768]{2,1,0:T(8,128)(2,1)} %param.16) | copy-start | bytes 589828
  128.8 37.1 %all-to-all-start.2 = ((bf16[64,3,768]{2,1,0:T(4,128)(2,1)}), bf16[64,3,768]{2,1,0:T(4,128)(2,1)S(1)}, u32[]{:S(2)}, u32[]{:S(2)}) async-start(bf16[64,3,768]{2,1,0:T(4,128)(2,1)} %reshape.121), calls=%async_computation.2 | async-start | bytes 786432 | tf_op jit(solution)/shard_map/all_to_all | solution.py:256
Sparse Core Ops, SparseCore 0:
  122.5 50.2 reduce-scatter.1

commit v9 on v8

--- a/solution.py
+++ b/solution.py
@@ -195,6 +195,7 @@
     flat_acts = hidden_acts.reshape(routed, hidden).astype(F32)
     gated = (gate_half.reshape(routed, 1) * flat_acts).astype(BF16)
     send_acts = jnp.dot(placement, gated, preferred_element_type=F32).astype(BF16)
+    send_acts, own = lax.optimization_barrier((send_acts, own))
     acts_in = lax.all_to_all(
         send_acts.reshape(experts, MOST, hidden),
         ("x", "zh", "zl"),

time: 180 us -> 189 us (1.050)
  waiting for transfers between devices: 52.9 us -> 78 us
  starting transfers between devices: 46.2 us -> 36.7 us
  blocking collectives: 44.1 us -> 37.1 us
    all_to_all x1, waiting for transfers between devices: 0.01 us -> 23.5 us  [shards(): lax.all_to_all(send_acts.reshape(experts, MOST, hidden), ('x', 'zh', 'zl'...]
    all_to_all x1, starting transfers between devices: 22.6 us -> 15.2 us  [shards(): lax.all_to_all(send_acts.reshape(experts, MOST, hidden), ('x', 'zh', 'zl'...]
    all_gather x1, blocking collectives: 44.1 us -> 37.1 us  [shards(): lax.all_gather(jnp.concatenate([out_grad, table], axis=1), 'zh', axis=0,...]
    all_to_all x1, starting transfers between devices: 8 us -> 5.67 us  [shards(): lax.all_to_all(picked, ('core', 'x', 'zh', 'zl'), split_axis=0, concat_ax...]
    all_to_all x1, waiting for transfers between devices: 17.2 us -> 19.2 us  [shards(): lax.all_to_all(picked, ('core', 'x', 'zh', 'zl'), split_axis=0, concat_ax...]
    all_to_all x1, starting transfers between devices: 10.6 us -> 8.63 us  [shards(): lax.all_to_all(grad_hidden.reshape(experts, MOST, hidden), ('x', 'zh', 'z...]
  transfers between devices with their start and end apart: 6 -> 6, of which waited for: 5 -> 6; matrix products, arithmetic and copies ran while one was open for 3% -> 3% of each run, Pallas kernels for 4% -> 4%
where the time goes in v9:
time: 189 us; the launch traced here: 188 us
  waiting for transfers between devices  78 us (41%)
  blocking collectives  37.1 us (20%)
  starting transfers between devices  36.7 us (19%)
  between operations  14.3 us (8%)
  Pallas kernels  11.8 us (6%)
  local copies, waits for them, and re-layouts  4.27 us (2%)
  matrix products  4.02 us (2%)
  other arithmetic  2.02 us (1%)
    all_gather x1, blocking collectives, shards(): lax.all_gather(jnp.concatenate([out_grad, table], axis=1), 'zh', axis=0,...  37.1 us
    all_to_all x1, waiting for transfers between devices, shards(): lax.all_to_all(grad_hidden.reshape(experts, MOST, hidden), ('x', 'zh', 'z...  26.6 us
    all_to_all x1, waiting for transfers between devices, shards(): lax.all_to_all(send_acts.reshape(experts, MOST, hidden), ('x', 'zh', 'zl'...  23.5 us
    all_to_all x1, waiting for transfers between devices, shards(): lax.all_to_all(picked, ('core', 'x', 'zh', 'zl'), split_axis=0, concat_ax...  19.2 us
    all_to_all x1, starting transfers between devices, shards(): lax.all_to_all(send_acts.reshape(experts, MOST, hidden), ('x', 'zh', 'zl'...  15.2 us
    all_to_all x1, starting transfers between devices, shards(): lax.all_to_all(grad_hidden.reshape(experts, MOST, hidden), ('x', 'zh', 'z...  8.63 us
    all_to_all x1, starting transfers between devices, shards(): lax.all_to_all(picked, ('core', 'x', 'zh', 'zl'), split_axis=0, concat_ax...  5.67 us
    pallas_call x1, Pallas kernels, hidden_term(): pl.pallas_call(hidden_kernel, grid=(blocks,), out_shape=jax.ShapeDtypeStr...  5.46 us
  transfers between devices with their start and end apart: 6, of which 6 were waited for; matrix products, arithmetic and copies ran while one was open for 3% of the time, Pallas kernels for 4%

profile of v9, /device:TPU:6, one launch (start us, length us, event | category | flops | bytes accessed | tf_op | source)
XLA Modules:
  0.0 188.2 jit_solution(8024503932513889642)
XLA Ops:
  7.2 0.0 copy-start.1
  7.2 0.8 copy.25
  8.0 0.1 reshape.118
  8.1 0.2 fusion
  8.3 0.2 convolution_convert_fusion.3
  8.5 0.9 pad_maximum_fusion
  9.4 37.1 %all_gather.3.own = bf16[64,4224]{1,0:T(8,128)(2,1)S(1)} all-gather(bf16[16,4224]{1,0:T(8,128)(2,1)S(1)} %pad_maximum_fusion), channel_id=1, replica_groups=mesh['y'=8,'core'=2,'x'=4,'zh'=4,'zl'=4] {'zh'}, dimensions={0}, use_global_device_ids=true | all-gather | bytes 675840 | tf_op jit(solution)/shard_map/all_gather | solution.py:192
  46.5 0.7 convert_element_type.74
  47.2 0.1 copy.24
  47.3 0.1 reshape.124
  47.4 0.0 copy-done.1
  47.4 0.3 convolution_convert_fusion.2
  47.7 0.0 copy-start
  47.7 0.9 reshape.119
  48.6 15.2 %all-to-all-start.1 = ((bf16[64,3,768]{2,1,0:T(4,128)(2,1)}), bf16[64,3,768]{2,1,0:T(4,128)(2,1)S(1)}, u32[]{:S(2)}, u32[]{:S(2)}) async-start(bf16[64,3,768]{2,1,0:T(4,128)(2,1)} %reshape.119), calls=%async_computation.1 | async-start | bytes 786432 | tf_op jit(solution)/shard_map/all_to_all | solution.py:199
  63.8 0.0 copy-done.2
  63.8 0.0 copy-done.3
  63.9 0.0 copy-done.4
  63.9 0.1 fusion.5.home
  64.0 0.0 copy-done
  64.0 2.4 %pick_rows.1 = bf16[128,6144]{1,0:T(8,128)(2,1)} custom-call(s32[384,1]{1,0:T(8,128)S(1)} %fusion.5.home, s32[384,1]{1,0:T(8,128)S(1)} %copy-done, bf16[64,4224]{1,0:T(8,128)(2,1)S(1)} %all_gather.3.own), custom_call_target="tpu_custom_call" | custom-call | flops 134217728 | bytes 2621440 | tf_op jit(solution)/shard_map/pick_rows/pallas_call | solution.py:52
  66.4 23.5 %all-to-all-done.1 = bf16[64,3,768]{2,1,0:T(4,128)(2,1)S(1)} async-done(((bf16[64,3,768]{2,1,0:T(4,128)(2,1)}), bf16[64,3,768]{2,1,0:T(4,128)(2,1)S(1)}, u32[]{:S(2)}, u32[]{:S(2)}) %all-to-all-start.1) | async-done | bytes 294944 | tf_op jit(solution)/shard_map/all_to_all | solution.py:199
  89.9 5.7 %all-to-all-start = ((bf16[16,8,6144]{2,1,0:T(8,128)(2,1)}), bf16[16,8,6144]{2,1,0:T(8,128)(2,1)S(1)}, u32[]{:S(2)}, u32[]{:S(2)}) async-start(bf16[16,8,6144]{2,1,0:T(8,128)(2,1)} %bitcast.1), calls=%async_computation | async-start | bytes 3145728 | tf_op jit(solution)/shard_map/all_to_all | solution.py:242
  95.6 0.0 reduce-scatter.2.cloned.1.call-start
  95.6 0.0 copy-done.6
  95.7 0.3 reshape.120
  96.0 2.3 %convolution_convert_fusion = bf16[384,768]{0,1:T(8,128)(2,1)S(1)} fusion(bf16[768,768]{1,0:T(8,128)(2,1)} %constant.125.clone, bf16[192,768]{1,0:T(8,128)(2,1)S(1)} %reshape.120, s32[384]{0:T(512)S(1)} %fusion.25), kind=kOutput, calls=%fused_computation | convolution fusion | flops 566894592 | bytes 2065920 | tf_op jit(solution)/shard_map/dot_general | solution.py:225
  98.2 0.1 dynamic-slice_bitcast_fusion
  98.3 3.5 %collective-permute-start = (bf16[384,384]{1,0:T(8,128)(2,1)S(1)}, bf16[384,384]{1,0:T(8,128)(2,1)S(1)}, u32[]{:S(2)}, u32[]{:S(2)}) collective-permute-start(bf16[384,384]{1,0:T(8,128)(2,1)S(1)} %get-tuple-element.19), channel_id=1, source_target_pairs={{0,64},{64,0},{1,65},{65,1},{2,66},{66,2},{3,67},{67,3},{4,68},{68... | collective-permute-start | bytes 884744 | tf_op jit(solution)/shard_map/ppermute | solution.py:230
  101.9 1.2 collective-permute-done.pair_a.pair_b
  103.1 19.2 %all-to-all-done = bf16[16,8,6144]{2,1,0:T(8,128)(2,1)S(1)} async-done(((bf16[16,8,6144]{2,1,0:T(8,128)(2,1)}), bf16[16,8,6144]{2,1,0:T(8,128)(2,1)S(1)}, u32[]{:S(2)}, u32[]{:S(2)}) %all-to-all-start) | async-done | bytes 1572896 | tf_op jit(solution)/shard_map/all_to_all | solution.py:242
  122.3 3.6 %collective-permute-start.1 = (bf16[128,6144]{1,0:T(8,128)(2,1)S(1)}, bf16[128,6144]{1,0:T(8,128)(2,1)S(1)}, u32[]{:S(2)}, u32[]{:S(2)}) collective-permute-start(bf16[128,6144]{1,0:T(8,128)(2,1)S(1)} %bitcast.19), channel_id=1, source_target_pairs={{0,64},{64,0},{1,65},{65,1},{2,66},{66,2},{3,67},{67,3},{4,68},{68... | collective-permute-start | bytes 4718600 | tf_op jit(solution)/shard_map/ppermute | solution.py:251
  125.8 3.0 %collective-permute-done.1.other_a.other_b = bf16[128,6144]{1,0:T(8,128)(2,1)S(1)} collective-permute-done((bf16[128,6144]{1,0:T(8,128)(2,1)S(1)}, bf16[128,6144]{1,0:T(8,128)(2,1)S(1)}, u32[]{:S(2)}, u32[]{:S(2)}) %collective-permute-start.1) | collective-permute-done | bytes 1572896 | tf_op jit(solution)/shard_map/ppermute | solution.py:251
  128.9 4.0 %weight_term.1 = bf16[384,4096]{1,0:T(8,128)(2,1)} custom-call(bf16[384,384]{1,0:T(8,128)(2,1)S(1)} %get-tuple-element.11.own_a.own_b, bf16[384,384]{1,0:T(8,128)(2,1)S(1)} %get-tuple-element.11.own_a.own_b, bf16[384,384]{1,0:T(8,128)(2,1)S(1)} %collective-permute-done.pair_a.pair_b, bf16[384,384]{1,0:T(8,128)(2,1)S(1)} %collective-permute-done.pair_a.pair_b, ...), custom_call_target="tpu_custom_call" | custom-call | flops 1610612736 | bytes 6291456 | tf_op jit(solution)/shard_map/weight_term/pallas_call | solution.py:88
  132.9 0.0 reduce-scatter.2.cloned.1.call-update
  132.9 5.5 %hidden_term.1 = bf16[192,768]{1,0:T(8,128)(2,1)S(1)} custom-call(bf16[128,6144]{1,0:T(8,128)(2,1)S(1)} %bitcast.22, bf16[128,6144]{1,0:T(8,128)(2,1)S(1)} %bitcast.23, bf16[1,768,4096]{2,1,0:T(8,128)(2,1)} %weight.1, bf16[192,384]{1,0:T(8,128)(2,1)S(1)} %fusion.3.order), custom_call_target="tpu_custom_call" | custom-call | flops 1610612736 | bytes 8683520 | tf_op jit(solution)/shard_map/hidden_term/pallas_call | solution.py:140
  138.4 0.0 copy-start.5
  138.4 0.9 reshape.121
  139.3 8.6 %all-to-all-start.2 = ((bf16[64,3,768]{2,1,0:T(4,128)(2,1)}), bf16[64,3,768]{2,1,0:T(4,128)(2,1)S(1)}, u32[]{:S(2)}, u32[]{:S(2)}) async-start(bf16[64,3,768]{2,1,0:T(4,128)(2,1)} %reshape.121), calls=%async_computation.2 | async-start | bytes 786432 | tf_op jit(solution)/shard_map/all_to_all | solution.py:257
  148.0 0.1 copy.28
  148.0 26.6 %all-to-all-done.2 = bf16[64,3,768]{2,1,0:T(4,128)(2,1)S(1)} async-done(((bf16[64,3,768]{2,1,0:T(4,128)(2,1)}), bf16[64,3,768]{2,1,0:T(4,128)(2,1)S(1)}, u32[]{:S(2)}, u32[]{:S(2)}) %all-to-all-start.2) | async-done | bytes 294944 | tf_op jit(solution)/shard_map/all_to_all | solution.py:257
  174.7 0.2 reshape.122
  174.9 1.0 fusion.2
  176.0 0.1 reshape.126
  176.0 0.1 multiply_reduce_fusion
  176.2 0.1 subtract_multiply_fusion
  176.2 0.7 copy.29
  176.9 4.4 %reduce-scatter.2.cloned.1.call-done = bf16[48,4096]{1,0:T(8,128)(2,1)} async-done(((bf16[384,4096]{1,0:T(8,128)(2,1)}), bf16[48,4096]{1,0:T(8,128)(2,1)}) %reduce-scatter.2.cloned.1.call-update) | async-done | bytes 393232 | tf_op jit(solution)/shard_map/reduce_scatter | solution.py:254
  (14 shorter events, 0.1 us)
Async XLA Ops:
  7.2 40.2 %copy-start.1 = (bf16[16,8,768]{2,1,0:T(8,128)(2,1)S(1)}, bf16[16,8,768]{2,1,0:T(8,128)(2,1)}, u32[]{:S(2)}) copy-start(bf16[16,8,768]{2,1,0:T(8,128)(2,1)} %param.16) | copy-start | bytes 589828
  46.5 17.4 %copy-start.2 = (s32[384,1]{1,0:T(8,128)S(1)}, s32[384,1]{1,0:T(8,128)}, u32[]{:S(2)}) copy-start(s32[384,1]{1,0:T(8,128)} %constant.126.clone) | copy-start | bytes 4612
  46.5 17.4 %copy-start.3 = (s32[384,1]{1,0:T(8,128)S(1)}, s32[384,1]{1,0:T(8,128)}, u32[]{:S(2)}) copy-start(s32[384,1]{1,0:T(8,128)} %constant.127.clone) | copy-start | bytes 4612
  46.5 17.4 %copy-start.4 = (pred[384,1]{1,0:T(32,128)(4,1)S(1)}, pred[384,1]{1,0:T(32,128)(4,1)}, u32[]{:S(2)}) copy-start(pred[384,1]{1,0:T(32,128)(4,1)} %constant.128.clone) | copy-start | bytes 1156
  47.7 16.3 %copy-start = (s32[384,1]{1,0:T(8,128)S(1)}, s32[384,1]{1,0:T(8,128)}, u32[]{:S(2)}) copy-start(s32[384,1]{1,0:T(8,128)} %constant.129.clone.lane) | copy-start | bytes 4612
  48.6 41.3 %all-to-all-start.1 = ((bf16[64,3,768]{2,1,0:T(4,128)(2,1)}), bf16[64,3,768]{2,1,0:T(4,128)(2,1)S(1)}, u32[]{:S(2)}, u32[]{:S(2)}) async-start(bf16[64,3,768]{2,1,0:T(4,128)(2,1)} %reshape.119), calls=%async_computation.1 | async-start | bytes 786432 | tf_op jit(solution)/shard_map/all_to_all | solution.py:199
  89.9 5.7 %copy-start.6 = (s32[384]{0:T(512)S(1)}, s32[384]{0:T(512)}, u32[]{:S(2)}) copy-start(s32[384]{0:T(512)} %constant.120.clone) | copy-start | bytes 4612
  89.9 5.7 %copy-start.7 = (s32[384]{0:T(512)S(1)}, s32[384]{0:T(512)}, u32[]{:S(2)}) copy-start(s32[384]{0:T(512)} %constant.121.clone) | copy-start | bytes 4612
  89.9 5.7 %copy-start.8 = (s32[384]{0:T(512)S(1)}, s32[384]{0:T(512)}, u32[]{:S(2)}) copy-start(s32[384]{0:T(512)} %constant.135) | copy-start | bytes 4612
  89.9 5.8 %copy-start.9 = (pred[384]{0:T(512)(128)(4,1)S(1)}, pred[384]{0:T(512)(128)(4,1)}, u32[]{:S(2)}) copy-start(pred[384]{0:T(512)(128)(4,1)} %constant.124.clone) | copy-start | bytes 1156
  89.9 32.3 %all-to-all-start = ((bf16[16,8,6144]{2,1,0:T(8,128)(2,1)}), bf16[16,8,6144]{2,1,0:T(8,128)(2,1)S(1)}, u32[]{:S(2)}, u32[]{:S(2)}) async-start(bf16[16,8,6144]{2,1,0:T(8,128)(2,1)} %bitcast.1), calls=%async_computation | async-start | bytes 3145728 | tf_op jit(solution)/shard_map/all_to_all | solution.py:242
  95.6 85.7 %reduce-scatter.2.cloned.1.call-start = ((), (), s32[]{:S(2)}) async-start(), calls=%async_computation.4 | async-start | bytes 3538944 | tf_op jit(solution)/shard_map/reduce_scatter | solution.py:254
  98.3 4.7 %collective-permute-start = (bf16[384,384]{1,0:T(8,128)(2,1)S(1)}, bf16[384,384]{1,0:T(8,128)(2,1)S(1)}, u32[]{:S(2)}, u32[]{:S(2)}) collective-permute-start(bf16[384,384]{1,0:T(8,128)(2,1)S(1)} %get-tuple-element.19), channel_id=1, source_target_pairs={{0,64},{64,0},{1,65},{65,1},{2,66},{66,2},{3,67},{67,3},{4,68},{68... | collective-permute-start | bytes 884744 | tf_op jit(solution)/shard_map/ppermute | solution.py:230
  122.3 6.6 %collective-permute-start.1 = (bf16[128,6144]{1,0:T(8,128)(2,1)S(1)}, bf16[128,6144]{1,0:T(8,128)(2,1)S(1)}, u32[]{:S(2)}, u32[]{:S(2)}) collective-permute-start(bf16[128,6144]{1,0:T(8,128)(2,1)S(1)} %bitcast.19), channel_id=1, source_target_pairs={{0,64},{64,0},{1,65},{65,1},{2,66},{66,2},{3,67},{67,3},{4,68},{68... | collective-permute-start | bytes 4718600 | tf_op jit(solution)/shard_map/ppermute | solution.py:251
  138.4 9.5 %copy-start.5 = (f32[16,8]{0,1:T(8,128)S(1)}, f32[16,8]{0,1:T(8,128)}, u32[]{:S(2)}) copy-start(f32[16,8]{0,1:T(8,128)} %param.17) | copy-start | bytes 1540
  139.3 35.4 %all-to-all-start.2 = ((bf16[64,3,768]{2,1,0:T(4,128)(2,1)}), bf16[64,3,768]{2,1,0:T(4,128)(2,1)S(1)}, u32[]{:S(2)}, u32[]{:S(2)}) async-start(bf16[64,3,768]{2,1,0:T(4,128)(2,1)} %reshape.121), calls=%async_computation.2 | async-start | bytes 786432 | tf_op jit(solution)/shard_map/all_to_all | solution.py:257
Sparse Core Ops, SparseCore 0:
  133.0 48.2 reduce-scatter.1

commit v10 on v8

--- a/solution.py
+++ b/solution.py
@@ -18,6 +18,37 @@
 BF16 = jnp.bfloat16
 F32 = jnp.float32
 MIB = 1024 * 1024
+
+
+def spread_kernel(slot, gate, acts, out):
+    lines, packed = out.shape
+    half = packed // MOST
+    line = lax.broadcasted_iota(jnp.int32, (lines, acts.shape[0]), 0)
+    for rank in range(MOST):
+        weight = jnp.where(slot[...] == line // 2 * MOST + rank, gate[...], 0.0)
+        lower = jnp.where(line % 2 == 0, weight, 0.0).astype(BF16)
+        upper = jnp.where(line % 2 == 1, weight, 0.0).astype(BF16)
+        total = jnp.dot(lower, acts[:, :half], preferred_element_type=F32)
+        total = total + jnp.dot(upper, acts[:, half:], preferred_element_type=F32)
+        out[:, rank * half : (rank + 1) * half] = total.astype(out.dtype)
+
+
+def spread_acts(slot, gate, acts, lines):
+    routed, hidden = acts.shape
+    packed = hidden // 2 * MOST
+    return pl.pallas_call(
+        spread_kernel,
+        out_shape=jax.ShapeDtypeStruct((lines, packed), BF16),
+        in_specs=[pl.BlockSpec(memory_space=pltpu.VMEM)] * 3,
+        out_specs=pl.BlockSpec(memory_space=pltpu.VMEM),
+        compiler_params=pltpu.CompilerParams(vmem_limit_bytes=16 * MIB),
+        cost_estimate=pl.CostEstimate(
+            flops=4 * lines * routed * packed,
+            bytes_accessed=2 * (routed * hidden + lines * packed),
+            transcendentals=0,
+        ),
+        name="spread_acts",
+    )(slot, gate, acts)
 
 
 def pick_kernel(home, lane, own, out):
@@ -164,7 +195,6 @@
     routed = tok_rows * top_count
     width = out_grad.shape[1]
     hidden = hidden_acts.shape[2]
-    half = hidden // CORES
     experts = X * Z
     slot_count = experts * MOST
     core = lax.axis_index("core")
@@ -193,15 +223,22 @@
 
     gate_half = lax.optimization_barrier(gate_weights.astype(BF16)).astype(F32)
     flat_acts = hidden_acts.reshape(routed, hidden).astype(F32)
-    gated = (gate_half.reshape(routed, 1) * flat_acts).astype(BF16)
-    send_acts = jnp.dot(placement, gated, preferred_element_type=F32).astype(BF16)
+    half = hidden // CORES
+    send_acts = spread_acts(
+        slot_index.reshape(1, routed),
+        gate_half.reshape(1, routed),
+        hidden_acts.reshape(routed, hidden),
+        2 * experts,
+    )
     acts_in = lax.all_to_all(
-        send_acts.reshape(experts, MOST, hidden),
+        send_acts.reshape(experts, 2, MOST * half),
         ("x", "zh", "zl"),
         split_axis=0,
         concat_axis=0,
         tiled=True,
-    ).reshape(slot_count, hidden)
+    )
+    acts_in = jnp.transpose(acts_in.reshape(experts, 2, MOST, half), (0, 2, 1, 3))
+    acts_in = acts_in.reshape(slot_count, hidden)
 
     packed = X * ZL * 8
     device, row = np.divmod(np.arange(packed, dtype=np.int32), 8)

time: 180 us -> 177 us (0.983)
  blocking collectives: 44.1 us -> 39.6 us
    all_gather x1, blocking collectives: 44.1 us -> 39.6 us  [shards(): lax.all_gather(jnp.concatenate([out_grad, table], axis=1), 'zh', axis=0,...]
  transfers between devices with their start and end apart: 6 -> 6, of which waited for: 5 -> 5; matrix products, arithmetic and copies ran while one was open for 3% -> 4% of each run, Pallas kernels for 4% -> 4%
where the time goes in v10:
time: 177 us; the launch traced here: 176 us
  waiting for transfers between devices  53.1 us (30%)
  starting transfers between devices  45.9 us (26%)
  blocking collectives  39.6 us (22%)
  between operations  14.3 us (8%)
  Pallas kernels  12.1 us (7%)
  local copies, waits for them, and re-layouts  5.62 us (3%)
  matrix products  3.72 us (2%)
    all_gather x1, blocking collectives, shards(): lax.all_gather(jnp.concatenate([out_grad, table], axis=1), 'zh', axis=0,...  39.6 us
    all_to_all x1, waiting for transfers between devices, shards(): lax.all_to_all(grad_hidden.reshape(experts, MOST, hidden), ('x', 'zh', 'z...  26.6 us
    all_to_all x1, starting transfers between devices, shards(): lax.all_to_all(send_acts.reshape(experts, 2, MOST * half), ('x', 'zh', 'z...  22.6 us
    all_to_all x1, waiting for transfers between devices, shards(): lax.all_to_all(picked, ('core', 'x', 'zh', 'zl'), split_axis=0, concat_ax...  17.5 us
    all_to_all x1, starting transfers between devices, shards(): lax.all_to_all(grad_hidden.reshape(experts, MOST, hidden), ('x', 'zh', 'z...  10.2 us
    all_to_all x1, starting transfers between devices, shards(): lax.all_to_all(picked, ('core', 'x', 'zh', 'zl'), split_axis=0, concat_ax...  8.04 us
    pallas_call x1, Pallas kernels, hidden_term(): pl.pallas_call(hidden_kernel, grid=(blocks,), out_shape=jax.ShapeDtypeStr...  5.45 us
    reduce_scatter x1, waiting for transfers between devices, shards(): summed = lax.psum_scatter(part, 'y', scatter_dimension=0, tiled=True)  4.48 us
  transfers between devices with their start and end apart: 6, of which 5 were waited for; matrix products, arithmetic and copies ran while one was open for 4% of the time, Pallas kernels for 4%

profile of v10, /device:TPU:6, one launch (start us, length us, event | category | flops | bytes accessed | tf_op | source)
XLA Modules:
  0.0 176.1 jit_solution(4945426422868997925)
XLA Ops:
  7.2 0.8 copy.37
  7.9 0.7 broadcast_multiply_fusion
  8.6 0.1 reshape.140
  8.7 0.2 fusion
  8.9 0.1 copy.38
  8.9 0.1 mul.74
  9.0 0.7 convert_element_type.74
  9.7 0.1 copy.36
  9.8 0.1 reshape.141.gate
  9.9 0.0 copy-start
  9.9 0.9 copy-done
  10.9 0.3 spread_acts.1
  11.2 0.0 copy-start.3
  11.2 0.0 copy-start.4
  11.2 0.0 copy-start.6
  11.2 0.8 reshape.143
  12.0 22.6 %all-to-all-start.1 = ((bf16[64,2,1152]{2,1,0:T(2,128)(2,1)}), bf16[64,2,1152]{2,1,0:T(2,128)(2,1)S(1)}, u32[]{:S(2)}, u32[]{:S(2)}) async-start(bf16[64,2,1152]{2,1,0:T(2,128)(2,1)} %reshape.143), calls=%async_computation.1 | async-start | bytes 589824 | tf_op jit(solution)/shard_map/all_to_all | solution.py:233
  34.7 0.2 convolution_convert_fusion.2
  34.9 39.6 %all_gather.3.own = bf16[64,4224]{1,0:T(8,128)(2,1)S(1)} all-gather(bf16[16,4224]{1,0:T(8,128)(2,1)S(1)} %pad_maximum_fusion), channel_id=1, replica_groups=mesh['y'=8,'core'=2,'x'=4,'zh'=4,'zl'=4] {'zh'}, dimensions={0}, use_global_device_ids=true | all-gather | bytes 675840 | tf_op jit(solution)/shard_map/all_gather | solution.py:222
  74.5 0.1 fusion.3.home
  74.6 2.4 %pick_rows.1 = bf16[128,6144]{1,0:T(8,128)(2,1)} custom-call(s32[384,1]{1,0:T(8,128)S(1)} %fusion.3.home, s32[384,1]{1,0:T(8,128)S(1)} %copy-done.2, bf16[64,4224]{1,0:T(8,128)(2,1)S(1)} %all_gather.3.own), custom_call_target="tpu_custom_call" | custom-call | flops 134217728 | bytes 2621440 | tf_op jit(solution)/shard_map/pick_rows/pallas_call | solution.py:83
  77.0 0.0 copy-start.11
  77.0 8.0 %all-to-all-start = ((bf16[16,8,6144]{2,1,0:T(8,128)(2,1)}), bf16[16,8,6144]{2,1,0:T(8,128)(2,1)S(1)}, u32[]{:S(2)}, u32[]{:S(2)}) async-start(bf16[16,8,6144]{2,1,0:T(8,128)(2,1)} %bitcast), calls=%async_computation | async-start | bytes 3145728 | tf_op jit(solution)/shard_map/all_to_all | solution.py:278
  85.1 0.0 reduce-scatter.2.cloned.1.call-start
  85.2 0.1 reshape.144
  85.3 0.4 copy.41
  85.7 2.3 %convolution_convert_fusion = bf16[384,768]{0,1:T(8,128)(2,1)S(1)} fusion(bf16[768,768]{1,0:T(8,128)(2,1)} %constant.125.clone, bf16[192,768]{1,0:T(8,128)(2,1)S(1)} %bitcast.30, s32[384]{0:T(512)S(1)} %fusion.19), kind=kOutput, calls=%fused_computation | convolution fusion | flops 566894592 | bytes 2065920 | tf_op jit(solution)/shard_map/dot_general | solution.py:261
  88.0 0.1 dynamic-slice_bitcast_fusion
  88.1 1.9 %collective-permute-start = (bf16[384,384]{1,0:T(8,128)(2,1)S(1)}, bf16[384,384]{1,0:T(8,128)(2,1)S(1)}, u32[]{:S(2)}, u32[]{:S(2)}) collective-permute-start(bf16[384,384]{1,0:T(8,128)(2,1)S(1)} %get-tuple-element.18), channel_id=1, source_target_pairs={{0,64},{64,0},{1,65},{65,1},{2,66},{66,2},{3,67},{67,3},{4,68},{68... | collective-permute-start | bytes 884744 | tf_op jit(solution)/shard_map/ppermute | solution.py:266
  90.0 1.5 collective-permute-done.pair_a.pair_b
  91.6 17.5 %all-to-all-done = bf16[16,8,6144]{2,1,0:T(8,128)(2,1)S(1)} async-done(((bf16[16,8,6144]{2,1,0:T(8,128)(2,1)}), bf16[16,8,6144]{2,1,0:T(8,128)(2,1)S(1)}, u32[]{:S(2)}, u32[]{:S(2)}) %all-to-all-start) | async-done | bytes 1572896 | tf_op jit(solution)/shard_map/all_to_all | solution.py:278
  109.0 3.1 %collective-permute-start.1 = (bf16[128,6144]{1,0:T(8,128)(2,1)S(1)}, bf16[128,6144]{1,0:T(8,128)(2,1)S(1)}, u32[]{:S(2)}, u32[]{:S(2)}) collective-permute-start(bf16[128,6144]{1,0:T(8,128)(2,1)S(1)} %bitcast.22), channel_id=1, source_target_pairs={{0,64},{64,0},{1,65},{65,1},{2,66},{66,2},{3,67},{67,3},{4,68},{68... | collective-permute-start | bytes 4718600 | tf_op jit(solution)/shard_map/ppermute | solution.py:287
  112.1 3.0 %collective-permute-done.1.other_a.other_b = bf16[128,6144]{1,0:T(8,128)(2,1)S(1)} collective-permute-done((bf16[128,6144]{1,0:T(8,128)(2,1)S(1)}, bf16[128,6144]{1,0:T(8,128)(2,1)S(1)}, u32[]{:S(2)}, u32[]{:S(2)}) %collective-permute-start.1) | collective-permute-done | bytes 1572896 | tf_op jit(solution)/shard_map/ppermute | solution.py:287
  115.2 4.0 %weight_term.1 = bf16[384,4096]{1,0:T(8,128)(2,1)} custom-call(bf16[384,384]{1,0:T(8,128)(2,1)S(1)} %get-tuple-element.7.own_a.own_b, bf16[384,384]{1,0:T(8,128)(2,1)S(1)} %get-tuple-element.7.own_a.own_b, bf16[384,384]{1,0:T(8,128)(2,1)S(1)} %collective-permute-done.pair_a.pair_b, bf16[384,384]{1,0:T(8,128)(2,1)S(1)} %collective-permute-done.pair_a.pair_b, ...), custom_call_target="tpu_custom_call" | custom-call | flops 1610612736 | bytes 6291456 | tf_op jit(solution)/shard_map/weight_term/pallas_call | solution.py:119
  119.1 0.0 reduce-scatter.2.cloned.1.call-update
  119.2 5.5 %hidden_term.1 = bf16[192,768]{1,0:T(8,128)(2,1)S(1)} custom-call(bf16[128,6144]{1,0:T(8,128)(2,1)S(1)} %bitcast.25, bf16[128,6144]{1,0:T(8,128)(2,1)S(1)} %bitcast.26, bf16[1,768,4096]{2,1,0:T(8,128)(2,1)} %weight.1, bf16[192,384]{1,0:T(8,128)(2,1)S(1)} %fusion.1.order), custom_call_target="tpu_custom_call" | custom-call | flops 1610612736 | bytes 8683520 | tf_op jit(solution)/shard_map/hidden_term/pallas_call | solution.py:171
  124.7 0.9 reshape.146
  125.6 10.2 %all-to-all-start.2 = ((bf16[64,3,768]{2,1,0:T(4,128)(2,1)}), bf16[64,3,768]{2,1,0:T(4,128)(2,1)S(1)}, u32[]{:S(2)}, u32[]{:S(2)}) async-start(bf16[64,3,768]{2,1,0:T(4,128)(2,1)} %reshape.146), calls=%async_computation.2 | async-start | bytes 786432 | tf_op jit(solution)/shard_map/all_to_all | solution.py:293
  135.8 0.1 mul.64
  135.9 0.1 copy.44
  136.0 26.6 %all-to-all-done.2 = bf16[64,3,768]{2,1,0:T(4,128)(2,1)S(1)} async-done(((bf16[64,3,768]{2,1,0:T(4,128)(2,1)}), bf16[64,3,768]{2,1,0:T(4,128)(2,1)S(1)}, u32[]{:S(2)}, u32[]{:S(2)}) %all-to-all-start.2) | async-done | bytes 294944 | tf_op jit(solution)/shard_map/all_to_all | solution.py:293
  162.6 0.2 reshape.147
  162.8 1.0 multiply_reduce_fusion
  163.9 0.1 reshape.149
  163.9 0.1 multiply_reduce_fusion.1
  164.1 0.1 subtract_multiply_fusion
  164.1 0.7 copy.45
  164.8 4.5 %reduce-scatter.2.cloned.1.call-done = bf16[48,4096]{1,0:T(8,128)(2,1)} async-done(((bf16[384,4096]{1,0:T(8,128)(2,1)}), bf16[48,4096]{1,0:T(8,128)(2,1)}) %reduce-scatter.2.cloned.1.call-update) | async-done | bytes 393232 | tf_op jit(solution)/shard_map/reduce_scatter | solution.py:290
  (26 shorter events, 0.2 us)
Async XLA Ops:
  9.9 0.9 copy-start
  10.9 24.0 %copy-start.5 = (bf16[16,4096]{1,0:T(8,128)(2,1)S(1)}, bf16[16,4096]{1,0:T(8,128)(2,1)}, u32[]{:S(2)}) copy-start(bf16[16,4096]{1,0:T(8,128)(2,1)} %param.15) | copy-start | bytes 393220
  11.2 63.3 %copy-start.3 = (s32[384,1]{1,0:T(8,128)S(1)}, s32[384,1]{1,0:T(8,128)}, u32[]{:S(2)}) copy-start(s32[384,1]{1,0:T(8,128)} %constant.126.clone) | copy-start | bytes 4612
  11.2 63.3 %copy-start.4 = (s32[384,1]{1,0:T(8,128)S(1)}, s32[384,1]{1,0:T(8,128)}, u32[]{:S(2)}) copy-start(s32[384,1]{1,0:T(8,128)} %constant.127.clone) | copy-start | bytes 4612
  11.2 63.3 %copy-start.6 = (pred[384,1]{1,0:T(32,128)(4,1)S(1)}, pred[384,1]{1,0:T(32,128)(4,1)}, u32[]{:S(2)}) copy-start(pred[384,1]{1,0:T(32,128)(4,1)} %constant.128.clone) | copy-start | bytes 1156
  12.0 62.6 %copy-start.2 = (s32[384,1]{1,0:T(8,128)S(1)}, s32[384,1]{1,0:T(8,128)}, u32[]{:S(2)}) copy-start(s32[384,1]{1,0:T(8,128)} %constant.129.clone.lane) | copy-start | bytes 4612
  12.0 65.0 %all-to-all-start.1 = ((bf16[64,2,1152]{2,1,0:T(2,128)(2,1)}), bf16[64,2,1152]{2,1,0:T(2,128)(2,1)S(1)}, u32[]{:S(2)}, u32[]{:S(2)}) async-start(bf16[64,2,1152]{2,1,0:T(2,128)(2,1)} %reshape.143), calls=%async_computation.1 | async-start | bytes 589824 | tf_op jit(solution)/shard_map/all_to_all | solution.py:233
  77.0 8.1 %copy-start.8 = (s32[384]{0:T(512)S(1)}, s32[384]{0:T(512)}, u32[]{:S(2)}) copy-start(s32[384]{0:T(512)} %constant.120.clone) | copy-start | bytes 4612
  77.0 8.1 %copy-start.9 = (s32[384]{0:T(512)S(1)}, s32[384]{0:T(512)}, u32[]{:S(2)}) copy-start(s32[384]{0:T(512)} %constant.121.clone) | copy-start | bytes 4612
  77.0 8.1 %copy-start.10 = (s32[384]{0:T(512)S(1)}, s32[384]{0:T(512)}, u32[]{:S(2)}) copy-start(s32[384]{0:T(512)} %constant.135) | copy-start | bytes 4612
  77.0 8.1 %copy-start.11 = (pred[384]{0:T(512)(128)(4,1)S(1)}, pred[384]{0:T(512)(128)(4,1)}, u32[]{:S(2)}) copy-start(pred[384]{0:T(512)(128)(4,1)} %constant.124.clone) | copy-start | bytes 1156
  77.0 32.0 %all-to-all-start = ((bf16[16,8,6144]{2,1,0:T(8,128)(2,1)}), bf16[16,8,6144]{2,1,0:T(8,128)(2,1)S(1)}, u32[]{:S(2)}, u32[]{:S(2)}) async-start(bf16[16,8,6144]{2,1,0:T(8,128)(2,1)} %bitcast), calls=%async_computation | async-start | bytes 3145728 | tf_op jit(solution)/shard_map/all_to_all | solution.py:278
  85.1 84.2 %reduce-scatter.2.cloned.1.call-start = ((), (), s32[]{:S(2)}) async-start(), calls=%async_computation.4 | async-start | bytes 3538944 | tf_op jit(solution)/shard_map/reduce_scatter | solution.py:290
  88.1 3.5 %collective-permute-start = (bf16[384,384]{1,0:T(8,128)(2,1)S(1)}, bf16[384,384]{1,0:T(8,128)(2,1)S(1)}, u32[]{:S(2)}, u32[]{:S(2)}) collective-permute-start(bf16[384,384]{1,0:T(8,128)(2,1)S(1)} %get-tuple-element.18), channel_id=1, source_target_pairs={{0,64},{64,0},{1,65},{65,1},{2,66},{66,2},{3,67},{67,3},{4,68},{68... | collective-permute-start | bytes 884744 | tf_op jit(solution)/shard_map/ppermute | solution.py:266
  109.0 6.1 %collective-permute-start.1 = (bf16[128,6144]{1,0:T(8,128)(2,1)S(1)}, bf16[128,6144]{1,0:T(8,128)(2,1)S(1)}, u32[]{:S(2)}, u32[]{:S(2)}) collective-permute-start(bf16[128,6144]{1,0:T(8,128)(2,1)S(1)} %bitcast.22), channel_id=1, source_target_pairs={{0,64},{64,0},{1,65},{65,1},{2,66},{66,2},{3,67},{67,3},{4,68},{68... | collective-permute-start | bytes 4718600 | tf_op jit(solution)/shard_map/ppermute | solution.py:287
  124.7 11.2 %copy-start.7 = (f32[16,8]{0,1:T(8,128)S(1)}, f32[16,8]{0,1:T(8,128)}, u32[]{:S(2)}) copy-start(f32[16,8]{0,1:T(8,128)} %param.17) | copy-start | bytes 1540
  124.7 38.1 %copy-start.1 = (bf16[16,8,768]{2,1,0:T(8,128)(2,1)S(1)}, bf16[16,8,768]{2,1,0:T(8,128)(2,1)}, u32[]{:S(2)}) copy-start(bf16[16,8,768]{2,1,0:T(8,128)(2,1)} %param.16) | copy-start | bytes 589828
  125.6 37.0 %all-to-all-start.2 = ((bf16[64,3,768]{2,1,0:T(4,128)(2,1)}), bf16[64,3,768]{2,1,0:T(4,128)(2,1)S(1)}, u32[]{:S(2)}, u32[]{:S(2)}) async-start(bf16[64,3,768]{2,1,0:T(4,128)(2,1)} %reshape.146), calls=%async_computation.2 | async-start | bytes 786432 | tf_op jit(solution)/shard_map/all_to_all | solution.py:293
Sparse Core Ops, SparseCore 0:
  119.3 49.9 reduce-scatter.1
